TPU v7x, 32 devices: a whole 2x2x4 slice. The times are simulated.
32 devices in a mesh: brick: 4 (over y, x), bulk: 8 (over z, core).
Axes of the slice: x: 2, y: 2, z: 4, core: 2. Of those that a mesh axis runs over, the one named last changes fastest.
Arguments:
- amp_traces: float32 [64, 512, 256], P(None, ('bulk', 'brick')), may hold values from -6 to 6
- patch_owner: int32 [65536, 1], P(('brick', 'bulk')), may hold values from 0 to 7; in each aligned block of 2048 rows (0 to 2047, 2048 to 4095, ...) at most 1024 rows name the same one
- patch_fault: int32 [65536], P(('brick', 'bulk')), may hold values from 0 to 15
- patch_trace: int32 [65536], P(('brick', 'bulk')), may hold values from 0 to 1023
- patch_offset: int32 [65536], P(('brick', 'bulk')), may hold values from 0 to 128
Outputs:
- fault_attr: float32 [64, 512, 256], P('brick', 'bulk')
- fault_profile: float32 [512, 128], P(('brick', 'bulk'))
Inputs may be any that keep to these rules, and one draw needn't show every extreme that they name: `patch_owner`: among the 2048 patches of one device, at most 1024 name the same owner, and in every draw some device has exactly 1024 patches with one owner.
All inputs are finite; a program needn't handle non-finite values.
Results may differ from a plain program's by a relative error of at most 0.0003.
Values sent between devices are 32-bit elements; how exact they have to be, the bound alone decides.
No kernel may reach another device: no remote copies, remote signals or barrier semaphores. Data moves between devices by JAX's collectives and lax.ppermute only.
A program may use at most 64 MiB of HBM per device.

v0:
```python
import jax
import jax.numpy as jnp
from jax import lax
from jax.sharding import PartitionSpec as P

PATCH = 128
F_DEV = 16


def padded_2(block, sides, width):
    for axis, dim in sides:
        count = lax.axis_size(axis)
        forward = [(i, i + 1) for i in range(count - 1)]
        backward = [(target, source) for source, target in forward]
        low = lax.ppermute(
            lax.slice_in_dim(block, block.shape[dim] - width, None, axis=dim), axis, forward
        )
        high = lax.ppermute(lax.slice_in_dim(block, 0, width, axis=dim), axis, backward)
        block = jnp.concatenate([low, block, high], axis=dim)
    return block


def box_sum(values, radius, dimension):
    length = values.shape[dimension] - 2 * radius
    summed = lax.slice_in_dim(values, 0, length, axis=dimension)
    for offset in range(1, 2 * radius + 1):
        summed = summed + lax.slice_in_dim(values, offset, offset + length, axis=dimension)
    return summed


def time_sum(values, radius):
    widths = [(0, 0)] * (values.ndim - 1) + [(radius, radius)]
    return box_sum(jnp.pad(values, widths), radius, values.ndim - 1)


def gradient_energy(padded):
    slope_inline = 0.5 * (padded[2:, 1:-1, :] - padded[:-2, 1:-1, :])
    slope_cross = 0.5 * (padded[1:-1, 2:, :] - padded[1:-1, :-2, :])
    centre = jnp.pad(padded[1:-1, 1:-1, :], ((0, 0), (0, 0), (1, 1)))
    slope_time = 0.5 * (centre[:, :, 2:] - centre[:, :, :-2])
    return jnp.stack(
        [slope_inline * slope_inline, slope_cross * slope_cross, slope_time * slope_time]
    )


def smooth_tensor(energy):
    return time_sum(box_sum(box_sum(energy, 2, 1), 2, 2), 2)


def finish(tensor, near_amp):
    lateral = (tensor[0] + tensor[1]) / (tensor[0] + tensor[1] + tensor[2] + 1e-05)
    stack = box_sum(box_sum(near_amp, 1, 0), 1, 1)
    power = box_sum(box_sum(near_amp * near_amp, 1, 0), 1, 1)
    semblance = time_sum(stack * stack, 4) / (9.0 * time_sum(power, 4) + 1e-05)
    return (1.0 - semblance) * lateral


def window_rows(chosen, offsets, width):
    samples = chosen.shape[1]
    steps = (samples - width).bit_length()
    current = chosen
    for level in range(steps):
        amount = 1 << level
        moved = jnp.concatenate(
            [current[:, amount:], jnp.zeros((current.shape[0], amount), current.dtype)], axis=1
        )
        taken = (offsets >> level & 1)[:, None] == 1
        current = jnp.where(taken, moved, current)
    return current[:, :width]


def local(amp_traces, patch_owner, patch_fault, patch_trace, patch_offset):
    bricked = lax.all_to_all(amp_traces, "brick", split_axis=0, concat_axis=1, tiled=True)
    near_amp = padded_2(bricked, (("brick", 0), ("bulk", 1)), 1)
    energy = gradient_energy(near_amp)
    rimmed = padded_2(energy, (("brick", 1), ("bulk", 2)), 2)
    attribute = finish(smooth_tensor(rimmed), near_amp)
    flattened = attribute.reshape(-1, attribute.shape[2])
    chosen = flattened[patch_trace]
    patch_rows = window_rows(chosen, patch_offset, PATCH)
    owners = patch_owner[:, 0]
    owner_count = lax.axis_size("bulk")
    count_patches = patch_rows.shape[0]
    one_hot = (owners[:, None] == jnp.arange(owner_count, dtype=jnp.int32)[None, :]).astype(
        jnp.int32
    )
    placed = jnp.cumsum(one_hot, axis=0)
    slot_rank = jnp.sum(placed * one_hot, axis=1) - 1
    capacity = 4 * count_patches // owner_count
    buffer = (
        jnp.zeros((owner_count, capacity, PATCH), jnp.float32).at[owners, slot_rank].set(patch_rows)
    )
    labels = (
        jnp.zeros((owner_count, capacity), jnp.float32)
        .at[owners, slot_rank]
        .set(patch_fault.astype(jnp.float32) + 1.0)
    )
    got_rows, got_labels = (
        lax.all_to_all(buffer, "bulk", split_axis=0, concat_axis=0, tiled=True),
        lax.all_to_all(labels, "bulk", split_axis=0, concat_axis=0, tiled=True),
    )
    wanted = jnp.arange(F_DEV, dtype=jnp.float32) + 1.0
    selector = (got_labels.reshape(1, -1) == wanted[:, None]).astype(jnp.float32)
    summed = jnp.dot(
        selector,
        got_rows.reshape(-1, PATCH),
        precision=lax.Precision.HIGHEST,
        preferred_element_type=jnp.float32,
    )
    counts = jnp.sum(selector, axis=1)
    profile = summed / jnp.maximum(counts, 1.0)[:, None]
    return (attribute, profile)


def solution(mesh):
    in_specs = (
        P(None, ("bulk", "brick"), None),
        P(("brick", "bulk"), None),
        P(("brick", "bulk")),
        P(("brick", "bulk")),
        P(("brick", "bulk")),
    )
    out_specs = (P("brick", "bulk", None), P(("brick", "bulk"), None))
    return jax.shard_map(local, mesh=mesh, in_specs=in_specs, out_specs=out_specs, check_vma=False)
```

profile of v0, /device:TPU:0, one launch (start us, length us, event | category | flops | bytes accessed | tf_op | source)
XLA Modules:
  0.0 212.4 jit_solution(9334432131796939233)
XLA Ops:
  0.7 5.3 %all-to-all-start = ((f32[64,16,256]{2,1,0:T(8,128)}), f32[64,16,256]{2,1,0:T(8,128)S(1)}, u32[]{:S(2)}, u32[]{:S(2)}) async-start(f32[64,16,256]{2,1,0:T(8,128)} %param.5), calls=%async_computation | async-start | bytes 2097152 | tf_op jit(solution)/shard_map/all_to_all | solution.py:73
  6.0 2.3 %reduce-window.6 = s32[8,16,128]{2,1,0:T(8,128)S(1)} reduce-window(s32[8,16,128]{2,1,0:T(8,128)S(1)} %fusion.51, s32[]{:T(128)} %constant.22.clone.1), window={size=1x1x128 pad=0_0x0_0x127_0}, to_apply=%region_0.1 | reduce-window | flops 2080768 | bytes 131076 | tf_op jit(solution)/shard_map/reduce-window
  9.2 8.6 %scatter_custom_fusion = f32[8192]{0:T(1024)} fusion(s32[2048]{0:T(1024)S(1)} %broadcast_select_fusion, f32[2048]{0:T(1024)S(1)} %convert_add_fusion, f32[]{:T(128)} %constant.18.clone.1), kind=kCustom, calls=%fused_computation.136 | custom fusion | bytes 32772
  17.8 1.8 all-to-all-done
  19.6 4.9 %all-to-all-start.1 = ((f32[8,1,1024]{2,1,0:T(1,128)}), f32[8,1,1024]{2,1,0:T(1,128)S(1)}, u32[]{:S(2)}, u32[]{:S(2)}) async-start(f32[8,1,1024]{2,1,0:T(1,128)} %bitcast.16), calls=%async_computation.1 | async-start | bytes 65536 | tf_op jit(solution)/shard_map/all_to_all | solution.py:100
  24.6 3.3 %collective-permute-start = (f32[1,64,256]{2,1,0:T(8,128)S(1)}, f32[1,64,256]{2,1,0:T(8,128)S(1)}, u32[]{:S(2)}, u32[]{:S(2)}) collective-permute-start(f32[1,64,256]{2,1,0:T(8,128)S(1)} %bitcast.65), channel_id=1, source_target_pairs={{0,8},{8,16},{16,24},{1,9},{9,17},{17,25},{2,10},{10,18},{18,26},{... | collective-permute-start | bytes 196616 | tf_op jit(solution)/shard_map/ppermute | solution.py:15
  28.0 1.3 collective-permute-start.1
  30.0 4.2 %collective-permute-done.1 = f32[1,64,256]{2,1,0:T(8,128)S(1)} collective-permute-done((f32[1,64,256]{2,1,0:T(8,128)S(1)}, f32[1,64,256]{2,1,0:T(8,128)S(1)}, u32[]{:S(2)}, u32[]{:S(2)}) %collective-permute-start.1) | collective-permute-done | bytes 65568 | tf_op jit(solution)/shard_map/ppermute | solution.py:18
  35.5 1.3 collective-permute-start.3
  36.8 4.0 %collective-permute-done.3 = f32[18,1,256]{2,1,0:T(1,128)S(1)} collective-permute-done((f32[18,1,256]{2,1,0:T(1,128)S(1)}, f32[18,1,256]{2,1,0:T(1,128)S(1)}, u32[]{:S(2)}, u32[]{:S(2)}) %collective-permute-start.3) | collective-permute-done | bytes 18464 | tf_op jit(solution)/shard_map/ppermute | solution.py:18
  41.8 4.3 %collective-permute-start.4 = (f32[3,2,64,256]{3,2,1,0:T(8,128)S(1)}, f32[3,2,64,256]{3,2,1,0:T(8,128)S(1)}, u32[]{:S(2)}, u32[]{:S(2)}) collective-permute-start(f32[3,2,64,256]{3,2,1,0:T(8,128)S(1)} %get-tuple-element.4), channel_id=1, source_target_pairs={{0,8},{8,16},{16,24},{1,9},{9,17},{17,25},{2,10},{10,18},{18,26},{... | collective-permute-start | bytes 1179656 | tf_op jit(solution)/shard_map/ppermute | solution.py:15
  46.1 1.3 collective-permute-start.5
  48.1 5.9 %collective-permute-done.4 = f32[3,2,64,256]{3,2,1,0:T(8,128)S(1)} collective-permute-done((f32[3,2,64,256]{3,2,1,0:T(8,128)S(1)}, f32[3,2,64,256]{3,2,1,0:T(8,128)S(1)}, u32[]{:S(2)}, u32[]{:S(2)}) %collective-permute-start.4) | collective-permute-done | bytes 393248 | tf_op jit(solution)/shard_map/ppermute | solution.py:15
  54.0 8.6 %collective-permute-done.5 = f32[3,2,64,256]{3,2,1,0:T(8,128)S(1)} collective-permute-done((f32[3,2,64,256]{3,2,1,0:T(8,128)S(1)}, f32[3,2,64,256]{3,2,1,0:T(8,128)S(1)}, u32[]{:S(2)}, u32[]{:S(2)}) %collective-permute-start.5) | collective-permute-done | bytes 393248 | tf_op jit(solution)/shard_map/ppermute | solution.py:18
  62.7 3.6 %collective-permute-start.6 = (f32[3,20,2,256]{3,2,1,0:T(2,128)S(1)}, f32[3,20,2,256]{3,2,1,0:T(2,128)S(1)}, u32[]{:S(2)}, u32[]{:S(2)}) collective-permute-start(f32[3,20,2,256]{3,2,1,0:T(2,128)S(1)} %get-tuple-element.2), channel_id=1, source_target_pairs={{0,1},{1,2},{2,3},{3,4},{4,5},{5,6},{6,7},{8,9},{9,10},{10,11},{11... | collective-permute-start | bytes 368648 | tf_op jit(solution)/shard_map/ppermute | solution.py:15
  66.3 1.5 collective-permute-start.7
  68.0 2.9 %collective-permute-done.7 = f32[3,20,2,256]{3,2,1,0:T(2,128)S(1)} collective-permute-done((f32[3,20,2,256]{3,2,1,0:T(2,128)S(1)}, f32[3,20,2,256]{3,2,1,0:T(2,128)S(1)}, u32[]{:S(2)}, u32[]{:S(2)}) %collective-permute-start.7) | collective-permute-done | bytes 122912 | tf_op jit(solution)/shard_map/ppermute | solution.py:18
  73.5 5.0 %fusion.3 = f32[3,16,64,256]{3,2,1,0:T(8,128)} fusion(f32[3,16,64,256]{3,2,1,0:T(8,128)S(1)} %slice_add_fusion.4), kind=kLoop, calls=%fused_computation.15 | loop fusion | flops 3145728 | bytes 6291456 | tf_op jit(solution)/shard_map/add | solution.py:27
  78.5 5.9 %fusion.33 = f32[16,64,256]{2,1,0:T(8,128)S(1)} fusion(f32[3,16,64,256]{3,2,1,0:T(8,128)} %fusion.3, f32[16,64,256]{2,1,0:T(8,128)S(1)} %slice_add_fusion.13, f32[16,64,256]{2,1,0:T(8,128)S(1)} %fusion.43), kind=kLoop, calls=%fused_computation.82 | loop fusion | flops 6553600 | bytes 6291456 | tf_op jit(solution)/shard_map/mul | solution.py:55
  84.4 6.6 %gather_fusion = f32[2048,256]{1,0:T(8,128)S(1)} fusion(f32[1024,256]{1,0:T(8,128)S(1)} %bitcast.53, s32[2048]{0:T(1024)S(1)} %fusion.54), kind=kCustom, calls=%fused_computation | custom fusion | bytes 4202496 | tf_op jit(solution)/shard_map/gather | solution.py:79
  98.8 8.9 %scatter_custom_fusion.1 = f32[8192,128]{1,0:T(8,128)} fusion(s32[2048]{0:T(1024)S(1)} %broadcast_select_fusion, f32[]{:T(128)} %constant.18.clone.1, f32[2048,256]{1,0:T(8,128)S(1)} %pad_select_fusion, f32[2048,128]{1,0:T(8,128)S(1)} %slice.334, pred[2048]{0:T(1024)(128)(4,1)S(1)} %get-tuple-element.17), kind=kCustom, calls=%fused_computation.36 | custom fusion | flops 262144 | bytes 6294528
  107.7 5.8 %all-to-all-start.2 = ((f32[8,1024,128]{2,1,0:T(8,128)}), f32[8,1024,128]{2,1,0:T(8,128)}, u32[]{:S(2)}, u32[]{:S(2)}) async-start(f32[8,1024,128]{2,1,0:T(8,128)} %bitcast.58), calls=%async_computation.2 | async-start | bytes 8388608 | tf_op jit(solution)/shard_map/all_to_all | solution.py:99
  113.8 94.3 %all-to-all-done.2 = f32[8,1024,128]{2,1,0:T(8,128)} async-done(((f32[8,1024,128]{2,1,0:T(8,128)}), f32[8,1024,128]{2,1,0:T(8,128)}, u32[]{:S(2)}, u32[]{:S(2)}) %all-to-all-start.2) | async-done | bytes 4194336 | tf_op jit(solution)/shard_map/all_to_all | solution.py:99
  208.2 4.3 %convolution_divide_fusion = f32[16,128]{1,0:T(8,128)} fusion(f32[8192,128]{1,0:T(8,128)} %bitcast.20, f32[8192]{0:T(1024)S(1)} %bitcast.61, f32[16]{0:T(128)S(1)} %iota_add_fusion, f32[16]{0:T(128)S(1)} %broadcast_maximum_fusion), kind=kOutput, calls=%fused_computation.52 | convolution fusion | flops 201459712 | bytes 4235392 | tf_op jit(solution)/shard_map/dot_general | solution.py:104
  (63 shorter events, 15.4 us)
Async XLA Ops:
  0.6 8.3 %copy-start.6 = (s32[2]{0:T(128)S(1)}, s32[2]{0:T(128)}, u32[]{:S(2)}) copy-start(s32[2]{0:T(128)} %constant.78) | copy-start | bytes 28
  0.6 8.4 %copy-start.5 = (s32[2]{0:T(128)S(1)}, s32[2]{0:T(128)}, u32[]{:S(2)}) copy-start(s32[2]{0:T(128)} %constant.81) | copy-start | bytes 28
  0.7 5.3 %copy-start.1 = (s32[2048,1]{0,1:T(1,128)S(1)}, s32[2048,1]{0,1:T(1,128)}, u32[]{:S(2)}) copy-start(s32[2048,1]{0,1:T(1,128)} %param.6) | copy-start | bytes 24580
  0.7 8.5 %copy-start.3 = (s32[2048]{0:T(1024)S(1)}, s32[2048]{0:T(1024)}, u32[]{:S(2)}) copy-start(s32[2048]{0:T(1024)} %param.7) | copy-start | bytes 24580
  0.7 28.6 %copy-start.2 = (s32[2048]{0:T(1024)S(1)}, s32[2048]{0:T(1024)}, u32[]{:S(2)}) copy-start(s32[2048]{0:T(1024)} %param.9) | copy-start | bytes 24580
  0.7 18.9 %all-to-all-start = ((f32[64,16,256]{2,1,0:T(8,128)}), f32[64,16,256]{2,1,0:T(8,128)S(1)}, u32[]{:S(2)}, u32[]{:S(2)}) async-start(f32[64,16,256]{2,1,0:T(8,128)} %param.5), calls=%async_computation | async-start | bytes 2097152 | tf_op jit(solution)/shard_map/all_to_all | solution.py:73
  8.3 28.5 %copy-start.4 = (s32[2048]{0:T(1024)S(1)}, s32[2048]{0:T(1024)}, u32[]{:S(2)}) copy-start(s32[2048]{0:T(1024)} %param.8) | copy-start | bytes 24580
  19.6 88.1 %all-to-all-start.1 = ((f32[8,1,1024]{2,1,0:T(1,128)}), f32[8,1,1024]{2,1,0:T(1,128)S(1)}, u32[]{:S(2)}, u32[]{:S(2)}) async-start(f32[8,1,1024]{2,1,0:T(1,128)} %bitcast.16), calls=%async_computation.1 | async-start | bytes 65536 | tf_op jit(solution)/shard_map/all_to_all | solution.py:100
  24.6 5.3 %collective-permute-start = (f32[1,64,256]{2,1,0:T(8,128)S(1)}, f32[1,64,256]{2,1,0:T(8,128)S(1)}, u32[]{:S(2)}, u32[]{:S(2)}) collective-permute-start(f32[1,64,256]{2,1,0:T(8,128)S(1)} %bitcast.65), channel_id=1, source_target_pairs={{0,8},{8,16},{16,24},{1,9},{9,17},{17,25},{2,10},{10,18},{18,26},{... | collective-permute-start | bytes 196616 | tf_op jit(solution)/shard_map/ppermute | solution.py:15
  28.0 6.2 %collective-permute-start.1 = (f32[1,64,256]{2,1,0:T(8,128)S(1)}, f32[1,64,256]{2,1,0:T(8,128)S(1)}, u32[]{:S(2)}, u32[]{:S(2)}) collective-permute-start(f32[1,64,256]{2,1,0:T(8,128)S(1)} %bitcast.64), channel_id=1, source_target_pairs={{8,0},{16,8},{24,16},{9,1},{17,9},{25,17},{10,2},{18,10},{26,18},{... | collective-permute-start | bytes 196616 | tf_op jit(solution)/shard_map/ppermute | solution.py:18
  34.2 2.6 %collective-permute-start.2 = (f32[18,1,256]{2,1,0:T(1,128)S(1)}, f32[18,1,256]{2,1,0:T(1,128)S(1)}, u32[]{:S(2)}, u32[]{:S(2)}) collective-permute-start(f32[18,1,256]{2,1,0:T(1,128)S(1)} %get-tuple-element.11), channel_id=1, source_target_pairs={{0,1},{1,2},{2,3},{3,4},{4,5},{5,6},{6,7},{8,9},{9,10},{10,11},{11... | collective-permute-start | bytes 55304 | tf_op jit(solution)/shard_map/ppermute | solution.py:15
  35.5 5.3 %collective-permute-start.3 = (f32[18,1,256]{2,1,0:T(1,128)S(1)}, f32[18,1,256]{2,1,0:T(1,128)S(1)}, u32[]{:S(2)}, u32[]{:S(2)}) collective-permute-start(f32[18,1,256]{2,1,0:T(1,128)S(1)} %get-tuple-element.10), channel_id=1, source_target_pairs={{1,0},{2,1},{3,2},{4,3},{5,4},{6,5},{7,6},{9,8},{10,9},{11,10},{12... | collective-permute-start | bytes 55304 | tf_op jit(solution)/shard_map/ppermute | solution.py:18
  41.8 12.2 %collective-permute-start.4 = (f32[3,2,64,256]{3,2,1,0:T(8,128)S(1)}, f32[3,2,64,256]{3,2,1,0:T(8,128)S(1)}, u32[]{:S(2)}, u32[]{:S(2)}) collective-permute-start(f32[3,2,64,256]{3,2,1,0:T(8,128)S(1)} %get-tuple-element.4), channel_id=1, source_target_pairs={{0,8},{8,16},{16,24},{1,9},{9,17},{17,25},{2,10},{10,18},{18,26},{... | collective-permute-start | bytes 1179656 | tf_op jit(solution)/shard_map/ppermute | solution.py:15
  46.1 16.5 %collective-permute-start.5 = (f32[3,2,64,256]{3,2,1,0:T(8,128)S(1)}, f32[3,2,64,256]{3,2,1,0:T(8,128)S(1)}, u32[]{:S(2)}, u32[]{:S(2)}) collective-permute-start(f32[3,2,64,256]{3,2,1,0:T(8,128)S(1)} %get-tuple-element.5), channel_id=1, source_target_pairs={{8,0},{16,8},{24,16},{9,1},{17,9},{25,17},{10,2},{18,10},{26,18},{... | collective-permute-start | bytes 1179656 | tf_op jit(solution)/shard_map/ppermute | solution.py:18
  62.7 5.3 %collective-permute-start.6 = (f32[3,20,2,256]{3,2,1,0:T(2,128)S(1)}, f32[3,20,2,256]{3,2,1,0:T(2,128)S(1)}, u32[]{:S(2)}, u32[]{:S(2)}) collective-permute-start(f32[3,20,2,256]{3,2,1,0:T(2,128)S(1)} %get-tuple-element.2), channel_id=1, source_target_pairs={{0,1},{1,2},{2,3},{3,4},{4,5},{5,6},{6,7},{8,9},{9,10},{10,11},{11... | collective-permute-start | bytes 368648 | tf_op jit(solution)/shard_map/ppermute | solution.py:15
  66.3 4.6 %collective-permute-start.7 = (f32[3,20,2,256]{3,2,1,0:T(2,128)S(1)}, f32[3,20,2,256]{3,2,1,0:T(2,128)S(1)}, u32[]{:S(2)}, u32[]{:S(2)}) collective-permute-start(f32[3,20,2,256]{3,2,1,0:T(2,128)S(1)} %get-tuple-element.3), channel_id=1, source_target_pairs={{1,0},{2,1},{3,2},{4,3},{5,4},{6,5},{7,6},{9,8},{10,9},{11,10},{12... | collective-permute-start | bytes 368648 | tf_op jit(solution)/shard_map/ppermute | solution.py:18
  84.4 6.7 %copy-start = (f32[16,64,256]{2,1,0:T(8,128)}, f32[16,64,256]{2,1,0:T(8,128)S(1)}, u32[]{:S(2)}) copy-start(f32[16,64,256]{2,1,0:T(8,128)S(1)} %fusion.33) | copy-start | bytes 3145732
  107.7 100.4 %all-to-all-start.2 = ((f32[8,1024,128]{2,1,0:T(8,128)}), f32[8,1024,128]{2,1,0:T(8,128)}, u32[]{:S(2)}, u32[]{:S(2)}) async-start(f32[8,1024,128]{2,1,0:T(8,128)} %bitcast.58), calls=%async_computation.2 | async-start | bytes 8388608 | tf_op jit(solution)/shard_map/all_to_all | solution.py:99
where the time goes:
time: 213 us; the launch traced here: 212 us
  waiting for transfers between devices  122 us (57%)
  starting transfers between devices  34 us (16%)
  other arithmetic  30.8 us (14%)
  local copies, waits for them, and re-layouts  20 us (9%)
  matrix products  4.29 us (2%)
    all_to_all x1, waiting for transfers between devices, local(): lax.all_to_all(buffer, 'bulk', split_axis=0, concat_axis=0, tiled=True)  94.3 us
    ppermute x4, waiting for transfers between devices, padded_2(): lax.ppermute(lax.slice_in_dim(block, 0, width, axis=dim), axis, backward)  19.7 us
    ppermute x4, starting transfers between devices, padded_2(): lax.ppermute(lax.slice_in_dim(block, block.shape[dim] - width, None, axis...  12.6 us
    unnamed x5, other arithmetic  9.22 us
    unnamed x15, local copies, waits for them, and re-layouts  8.67 us
    add x5, other arithmetic, box_sum(): summed + lax.slice_in_dim(values, offset, offset + length, axis=dimension)  7.06 us
    gather x1, local copies, waits for them, and re-layouts, local(): chosen = flattened[patch_trace]  6.64 us
    ppermute x4, waiting for transfers between devices, padded_2(): lax.ppermute(lax.slice_in_dim(block, block.shape[dim] - width, None, axis...  6.6 us
  transfers between devices with their start and end apart: 11, of which 8 were waited for; matrix products, arithmetic and copies ran while one was open for 24% of the time, Pallas kernels for 0%

commit v1 on v0

v1 whole, which is shorter than its diff:
```python
import jax
import jax.numpy as jnp
from jax import lax
from jax.experimental import pallas as pl
from jax.experimental.pallas import tpu as pltpu
from jax.sharding import PartitionSpec as P

PATCH = 128
F_DEV = 16
RIM = 3
LEAD = 8
LANES = 128


def split_bf16(values):
    high = values.astype(jnp.bfloat16)
    low = (values - high.astype(jnp.float32)).astype(jnp.bfloat16)
    return high, low


def dot(left, right):
    return jnp.dot(left, right, preferred_element_type=jnp.float32)


def brick_kernel(
    pieces_count, cx, cy, nt, patches, place,
    where_ref, low_ref, high_ref, band5_ref, band9_ref, faults_ref, *refs,
):
    pieces = refs[:pieces_count]
    picks_hbm, offsets_hbm, attr_hbm, partial_ref = refs[pieces_count:pieces_count + 4]
    amp, exy, ett, box, rows_bf, attr, picks, offsets, windows, sems = refs[pieces_count + 4:]
    halves = nt // LANES
    strip = cy // pieces_count
    brick, slab, bricks, slabs = where_ref[0], where_ref[1], where_ref[2], where_ref[3]
    wide = cy + 8

    fetches = []
    for d in range(pieces_count):
        column = pl.multiple_of(LEAD + strip * (brick ^ d), 8)
        for h in range(halves):
            fetches.append(pltpu.make_async_copy(
                pieces[d].at[:, :, pl.ds(h * LANES, LANES)],
                amp.at[:, h, pl.ds(column, strip), :],
                sems.at[d * halves + h],
            ))
    base = pieces_count * halves
    fetch_picks = pltpu.make_async_copy(picks_hbm, picks, sems.at[base])
    fetch_offsets = pltpu.make_async_copy(offsets_hbm, offsets, sems.at[base + 1])
    for copy in fetches:
        copy.start()
    fetch_picks.start()
    fetch_offsets.start()
    for h in range(halves):
        lanes = pl.ds(h * LANES, LANES)
        amp[:, h, LEAD - RIM:LEAD, :] = low_ref[:, :, lanes]
        amp[:, h, LEAD + cy:LEAD + cy + RIM, :] = high_ref[:, :, lanes]
    for copy in fetches:
        copy.wait()

    lane = lax.broadcasted_iota(jnp.int32, (wide, LANES), 1)
    first, last = lane == 0, lane == LANES - 1
    column = lax.broadcasted_iota(jnp.int32, (wide, LANES), 0)
    inside = jnp.logical_and(
        jnp.logical_or(slab > 0, column >= 2),
        jnp.logical_or(slab < slabs - 1, column < cy + 2),
    ).astype(jnp.float32)
    origin = LEAD - RIM

    def energy_row(e, carry):
        position = brick * cx + e - 2
        valid = jnp.logical_and(position >= 0, position < bricks * cx).astype(jnp.float32)
        mask = inside * valid
        centre = [amp[e + 1, h, origin + 1:origin + 1 + wide, :] for h in range(halves)]
        back = [pltpu.roll(c, 1, 1) for c in centre]
        ahead = [pltpu.roll(c, LANES - 1, 1) for c in centre]
        for h in range(halves):
            slope_x = (amp[e + 2, h, origin + 1:origin + 1 + wide, :]
                       - amp[e, h, origin + 1:origin + 1 + wide, :])
            slope_y = (amp[e + 1, h, origin + 2:origin + 2 + wide, :]
                       - amp[e + 1, h, origin:origin + wide, :])
            before = jnp.where(first, back[h - 1] if h > 0 else 0.0, back[h])
            after = jnp.where(last, ahead[h + 1] if h < halves - 1 else 0.0, ahead[h])
            slope_t = after - before
            exy[e, h] = (slope_x * slope_x + slope_y * slope_y) * mask
            ett[e, h] = slope_t * slope_t * mask
        return carry

    lax.fori_loop(0, cx + 4, energy_row, 0)

    def summed(field, slot, radius, rows, band):
        parts = []
        for h in range(halves):
            box[slot, h] = rows[h]
        for h in range(halves):
            total = box[slot, h, 0:cy, :]
            for j in range(1, 2 * radius + 1):
                total = total + box[slot, h, j:j + cy, :]
            parts.append(total)
        return parts

    def through_time(parts, band):
        whole = jnp.concatenate(parts, axis=1)
        high, low = split_bf16(whole)
        return dot(high, band) + dot(low, band)

    def attribute_row(r, carry):
        def inline5(field, h):
            total = field[r, h]
            for j in range(1, 5):
                total = total + field[r + j, h]
            return total

        tensor_xy = through_time(
            summed(exy, 0, 2, [inline5(exy, h) for h in range(halves)], None), band5_ref[...])
        tensor_t = through_time(
            summed(ett, 1, 2, [inline5(ett, h) for h in range(halves)], None), band5_ref[...])
        near = slice(LEAD - 1, LEAD - 1 + wide)
        stack_rows, power_rows = [], []
        for h in range(halves):
            rows = [amp[r + RIM + j, h, near, :] for j in (-1, 0, 1)]
            stack_rows.append(rows[0] + rows[1] + rows[2])
            power_rows.append(rows[0] * rows[0] + rows[1] * rows[1] + rows[2] * rows[2])
        stack = summed(None, 2, 1, stack_rows, None)
        power = summed(None, 3, 1, power_rows, None)
        spread = [9.0 * p - s * s for p, s in zip(power, stack)]
        scatter = through_time(spread, band9_ref[...]) + 1e-5
        whole = 9.0 * through_time(power, band9_ref[...]) + 1e-5
        both = whole * (tensor_xy + tensor_t + 4e-5)
        inverse = pl.reciprocal(both, approx=True)
        inverse = inverse * (2.0 - both * inverse)
        values = scatter * tensor_xy * inverse
        attr[r] = values
        high, low = split_bf16(values)
        at = pl.ds(pl.multiple_of(r * cy, 16), cy)
        rows_bf[at, 0:nt] = high
        rows_bf[at, nt:2 * nt] = low
        return carry

    lax.fori_loop(0, cx, attribute_row, 0)
    store = pltpu.make_async_copy(attr, attr_hbm, sems.at[base + 2])
    store.start()

    fetch_picks.wait()
    fetch_offsets.wait()
    block = 512
    lane_block = lax.broadcasted_iota(jnp.int32, (block, LANES), 1)

    def window_block(j, carry):
        at = pl.ds(pl.multiple_of(j * block, block), block)
        chosen = dot(picks[at, :], rows_bf[...])
        rows = chosen[:, 0:nt] + chosen[:, nt:2 * nt]
        shift = offsets[at, :]
        mixed = jnp.where(lane_block < shift, rows[:, LANES:nt], rows[:, 0:LANES])
        window = jnp.take_along_axis(mixed, (lane_block + shift) & (LANES - 1), axis=1)
        high, low = split_bf16(window)
        windows[at, 0:PATCH] = high
        windows[at, PATCH:2 * PATCH] = low
        return carry

    lax.fori_loop(0, patches // block, window_block, 0)
    sums = dot(faults_ref[...], windows[...])
    partial_ref[...] = sums[:, 0:PATCH] + sums[:, PATCH:2 * PATCH]
    store.wait()


def band(nt, radius):
    at = jnp.arange(nt, dtype=jnp.int32)
    return (jnp.abs(at[:, None] - at[None, :]) <= radius).astype(jnp.bfloat16)


def exchange_bricks(amp, cx):
    bricks = lax.axis_size("brick")
    mine = lax.axis_index("brick")
    padded = jnp.pad(amp, ((RIM, RIM), (0, 0), (0, 0)))
    pieces = []
    for d in range(bricks):
        piece = lax.dynamic_slice_in_dim(padded, (mine ^ d) * cx, cx + 2 * RIM, axis=0)
        if d > 0:
            piece = lax.ppermute(piece, "brick", [(s, s ^ d) for s in range(bricks)])
        pieces.append(piece)
    return pieces


def halo_columns(pieces, strip):
    bricks = lax.axis_size("brick")
    slabs = lax.axis_size("bulk")
    mine = lax.axis_index("brick")
    left = sum(jnp.where((mine ^ d) == 0, p[:, :RIM], 0.0) for d, p in enumerate(pieces))
    right = sum(
        jnp.where((mine ^ d) == bricks - 1, p[:, strip - RIM:], 0.0) for d, p in enumerate(pieces))
    low = lax.ppermute(right, "bulk", [(s, s + 1) for s in range(slabs - 1)])
    high = lax.ppermute(left, "bulk", [(s + 1, s) for s in range(slabs - 1)])
    return low, high


def reduce_scatter(parts, axis):
    count = lax.axis_size(axis)
    mine = lax.axis_index(axis)
    bit = 1
    while bit < count:
        pair = parts.reshape(parts.shape[0] // 2, 2, *parts.shape[1:])
        side = mine // bit % 2
        kept = lax.dynamic_index_in_dim(pair, side, 1, keepdims=False)
        sent = lax.dynamic_index_in_dim(pair, 1 - side, 1, keepdims=False)
        parts = kept + lax.ppermute(sent, axis, [(s, s ^ bit) for s in range(count)])
        bit *= 2
    return parts[0]


def local(amp_traces, patch_owner, patch_fault, patch_trace, patch_offset):
    bricks, slabs = lax.axis_size("brick"), lax.axis_size("bulk")
    nx, strip, nt = amp_traces.shape
    cx, cy = nx // bricks, strip * bricks
    patches = patch_fault.shape[0]
    faults = slabs * F_DEV

    pieces = exchange_bricks(amp_traces, cx)
    low, high = halo_columns(pieces, strip)

    picks = (patch_trace[:, None] == jnp.arange(cx * cy, dtype=jnp.int32)[None, :]).astype(jnp.bfloat16)
    offsets = jnp.broadcast_to(patch_offset[:, None], (patches, LANES))
    fault = patch_owner[:, 0] * F_DEV + patch_fault
    members = fault[None, :] == jnp.arange(faults, dtype=jnp.int32)[:, None]
    counts = jnp.sum(members.astype(jnp.float32), axis=1)
    members = members.astype(jnp.bfloat16)
    where = jnp.stack([
        lax.axis_index("brick"), lax.axis_index("bulk"), jnp.int32(bricks), jnp.int32(slabs)])

    halves = nt // LANES
    wide = cy + 8
    vmem = pl.BlockSpec(memory_space=pltpu.VMEM)
    anywhere = pl.BlockSpec(memory_space=pl.ANY)

    def kernel(*refs):
        brick_kernel(bricks, cx, cy, nt, patches, None, *refs)

    attribute, partial = pl.pallas_call(
        kernel,
        out_shape=(
            jax.ShapeDtypeStruct((cx, cy, nt), jnp.float32),
            jax.ShapeDtypeStruct((faults, PATCH), jnp.float32),
        ),
        in_specs=[pl.BlockSpec(memory_space=pltpu.SMEM)] + [vmem] * 5 + [anywhere] * (bricks + 2),
        out_specs=(anywhere, vmem),
        scratch_shapes=[
            pltpu.VMEM((cx + 2 * RIM, halves, cy + 2 * LEAD, LANES), jnp.float32),
            pltpu.VMEM((cx + 4, halves, wide, LANES), jnp.float32),
            pltpu.VMEM((cx + 4, halves, wide, LANES), jnp.float32),
            pltpu.VMEM((4, halves, wide, LANES), jnp.float32),
            pltpu.VMEM((cx * cy, 2 * nt), jnp.bfloat16),
            pltpu.VMEM((cx, cy, nt), jnp.float32),
            pltpu.VMEM((patches, cx * cy), jnp.bfloat16),
            pltpu.VMEM((patches, LANES), jnp.int32),
            pltpu.VMEM((patches, 2 * PATCH), jnp.bfloat16),
            pltpu.SemaphoreType.DMA((bricks * halves + 3,)),
        ],
        compiler_params=pltpu.CompilerParams(vmem_limit_bytes=48 * 1024 * 1024),
        cost_estimate=pl.CostEstimate(flops=2_500_000_000, bytes_accessed=10_000_000, transcendentals=0),
        name="brick_attribute",
    )(where, low, high, band(nt, 2), band(nt, 4), members, *pieces, picks, offsets)

    tally = jnp.pad(counts.reshape(slabs, 1, F_DEV), ((0, 0), (0, 0), (0, PATCH - F_DEV)))
    parts = jnp.concatenate([partial.reshape(slabs, F_DEV, PATCH), tally], axis=1)
    total = reduce_scatter(parts, "bulk")
    profile = total[:F_DEV] / jnp.maximum(total[F_DEV, :F_DEV], 1.0)[:, None]
    return attribute, profile


def solution(mesh):
    in_specs = (
        P(None, ("bulk", "brick"), None),
        P(("brick", "bulk"), None),
        P(("brick", "bulk")),
        P(("brick", "bulk")),
        P(("brick", "bulk")),
    )
    out_specs = (P("brick", "bulk", None), P(("brick", "bulk"), None))
    return jax.shard_map(local, mesh=mesh, in_specs=in_specs, out_specs=out_specs, check_vma=False)
```

time: 213 us -> 54.6 us (0.26)
  waiting for transfers between devices: 122 us -> 18.2 us
  other arithmetic: 30.8 us -> 3.73 us
  starting transfers between devices: 34 us -> 16.5 us
  local copies, waits for them, and re-layouts: 20 us -> 2.67 us
  Pallas kernels: 0 us -> 12.5 us
  matrix products: 4.29 us -> 0 us
    all_to_all x3 -> x0, waiting for transfers between devices: 96.1 us -> none  [the longest x1 94.3 us: local(): lax.all_to_all(buffer, 'bulk', split_axis=0, concat_axis=0, tiled=True)]
    all_to_all x3 -> x0, starting transfers between devices: 16 us -> none  [the longest x1 5.81 us: local(): lax.all_to_all(buffer, 'bulk', split_axis=0, concat_axis=0, tiled=True)]
    pallas_call x0 -> x1, Pallas kernels: none -> 12.5 us  [local(): pl.pallas_call(kernel, out_shape=(jax.ShapeDtypeStruct((cx, cy, nt), jnp....]
    unnamed x5 -> x0, other arithmetic: 9.22 us -> none
    unnamed x15 -> x11, local copies, waits for them, and re-layouts: 8.67 us -> 0.02 us
    ppermute x8, waiting for transfers between devices: 26.3 us -> 18.2 us  [the longest x3 13.2 us: exchange_bricks(): piece = lax.ppermute(piece, 'brick', [(s, s ^ d) for s in range(bricks)])]
    add x7 -> x5, other arithmetic: 7.07 us -> 0.2 us  [the longest x1 0.16 us: halo_columns(): sum((jnp.where(mine ^ d == 0, p[:, :RIM], 0.0) for d, p in enumerate(piec...]
    gather x1 -> x0, local copies, waits for them, and re-layouts: 6.64 us -> none  [local(): chosen = flattened[patch_trace]]
  transfers between devices with their start and end apart: 11 -> 8, of which waited for: 8 -> 7; matrix products, arithmetic and copies ran while one was open for 24% -> 5% of each run, Pallas kernels for 0% -> 0%
where the time goes in v1:
time: 54.6 us; the launch traced here: 54.4 us
  waiting for transfers between devices  18.2 us (33%)
  starting transfers between devices  16.5 us (30%)
  Pallas kernels  12.5 us (23%)
  other arithmetic  3.73 us (7%)
  local copies, waits for them, and re-layouts  2.67 us (5%)
  between operations  0.84 us (2%)
    ppermute x3, waiting for transfers between devices, exchange_bricks(): piece = lax.ppermute(piece, 'brick', [(s, s ^ d) for s in range(bricks)])  13.2 us
    pallas_call x1, Pallas kernels, local(): pl.pallas_call(kernel, out_shape=(jax.ShapeDtypeStruct((cx, cy, nt), jnp....  12.5 us
    ppermute x3, starting transfers between devices, reduce_scatter(): lax.ppermute(sent, axis, [(s, s ^ bit) for s in range(count)])  7.68 us
    ppermute x3, starting transfers between devices, exchange_bricks(): piece = lax.ppermute(piece, 'brick', [(s, s ^ d) for s in range(bricks)])  4.46 us
    ppermute x3, waiting for transfers between devices, reduce_scatter(): lax.ppermute(sent, axis, [(s, s ^ bit) for s in range(count)])  4.23 us
    ppermute x1, starting transfers between devices, halo_columns(): low = lax.ppermute(right, 'bulk', [(s, s + 1) for s in range(slabs - 1)])  3.04 us
    convert_element_type x1, other arithmetic, local(): (patch_trace[:, None] == jnp.arange(cx * cy, dtype=jnp.int32)[None, :]).a...  2.4 us
    dynamic_slice x1, local copies, waits for them, and re-layouts, exchange_bricks(): lax.dynamic_slice_in_dim(padded, (mine ^ d) * cx, cx + 2 * RIM, axis=0)  2.17 us
  transfers between devices with their start and end apart: 8, of which 7 were waited for; matrix products, arithmetic and copies ran while one was open for 5% of the time, Pallas kernels for 0%

profile of v1, /device:TPU:0, one launch (start us, length us, event | category | flops | bytes accessed | tf_op | source)
XLA Modules:
  0.0 54.4 jit_solution(10668946691080141859)
XLA Ops:
  0.7 2.2 %pad_dynamic-slice_fusion.5 = (f32[22,16,256]{2,1,0:T(8,128)S(1)}, f32[22,16,256]{2,1,0:T(8,128)}, f32[22,16,256]{2,1,0:T(8,128)S(1)}, f32[22,16,256]{2,1,0:T(8,128)S(1)}) fusion(s32[]{:T(128)S(6)} %select_n.107, f32[64,16,256]{2,1,0:T(8,128)} %param.5, s32[]{:T(128)S(6)} %select_n.110, s32[]{:T(128)S(6)} %select_n.113, s32[]{:T(128)S(6)} %select_n.116), kind=kLoop, calls=%fused_computation.7 | loop fusion | bytes 2490384 | tf_op jit(solution)/shard_map/dynamic_slice | solution.py:177
  2.9 2.9 %collective-permute-start = (f32[22,16,256]{2,1,0:T(8,128)}, f32[22,16,256]{2,1,0:T(8,128)S(1)}, u32[]{:S(2)}, u32[]{:S(2)}) collective-permute-start(f32[22,16,256]{2,1,0:T(8,128)} %get-tuple-element.9), channel_id=1, source_target_pairs={{0,8},{8,0},{16,24},{24,16},{1,9},{9,1},{17,25},{25,17},{2,10},{10... | collective-permute-start | bytes 1081352 | tf_op jit(solution)/shard_map/ppermute | solution.py:179
  5.8 1.5 %collective-permute-start.1 = (f32[22,16,256]{2,1,0:T(8,128)S(1)}, f32[22,16,256]{2,1,0:T(8,128)S(1)}, u32[]{:S(2)}, u32[]{:S(2)}) collective-permute-start(f32[22,16,256]{2,1,0:T(8,128)S(1)} %get-tuple-element.10), channel_id=1, source_target_pairs={{0,16},{8,24},{16,0},{24,8},{1,17},{9,25},{17,1},{25,9},{2,18},{10... | collective-permute-start | bytes 1081352 | tf_op jit(solution)/shard_map/ppermute | solution.py:179
  7.4 0.2 convert_reduce_fusion
  7.6 0.1 reshape.33
  7.7 2.4 %fusion.refs_10_ = bf16[2048,1024]{1,0:T(8,128)(2,1)} fusion(s32[2048]{0:T(1024)S(1)} %copy-done.1), kind=kLoop, calls=%fused_computation.1 | loop fusion | flops 4194304 | bytes 4202496 | tf_op jit(solution)/shard_map/convert_element_type | solution.py:220
  10.1 0.1 fusion.1.refs_5_
  10.2 5.0 %collective-permute-done.refs_7_ = f32[22,16,256]{2,1,0:T(8,128)S(1)} collective-permute-done((f32[22,16,256]{2,1,0:T(8,128)}, f32[22,16,256]{2,1,0:T(8,128)S(1)}, u32[]{:S(2)}, u32[]{:S(2)}) %collective-permute-start) | collective-permute-done | bytes 360480 | tf_op jit(solution)/shard_map/ppermute | solution.py:179
  15.2 7.2 %collective-permute-done.1.refs_8_ = f32[22,16,256]{2,1,0:T(8,128)S(1)} collective-permute-done((f32[22,16,256]{2,1,0:T(8,128)S(1)}, f32[22,16,256]{2,1,0:T(8,128)S(1)}, u32[]{:S(2)}, u32[]{:S(2)}) %collective-permute-start.1) | collective-permute-done | bytes 360480 | tf_op jit(solution)/shard_map/ppermute | solution.py:179
  22.4 1.0 %collective-permute-done.2.refs_9_ = f32[22,16,256]{2,1,0:T(8,128)S(1)} collective-permute-done((f32[22,16,256]{2,1,0:T(8,128)S(1)}, f32[22,16,256]{2,1,0:T(8,128)S(1)}, u32[]{:S(2)}, u32[]{:S(2)}) %collective-permute-start.2) | collective-permute-done | bytes 360480 | tf_op jit(solution)/shard_map/ppermute | solution.py:179
  23.4 0.2 fusion.13
  23.6 1.3 %collective-permute-start.4 = (f32[22,3,256]{2,1,0:T(4,128)S(1)}, f32[22,3,256]{2,1,0:T(4,128)S(1)}, u32[]{:S(2)}, u32[]{:S(2)}) collective-permute-start(f32[22,3,256]{2,1,0:T(4,128)S(1)} %get-tuple-element.6), channel_id=1, source_target_pairs={{1,0},{2,1},{3,2},{4,3},{5,4},{6,5},{7,6},{9,8},{10,9},{11,10},{12... | collective-permute-start | bytes 202760 | tf_op jit(solution)/shard_map/ppermute | solution.py:192
  24.9 3.0 %collective-permute-start.3 = (f32[22,3,256]{2,1,0:T(4,128)S(1)}, f32[22,3,256]{2,1,0:T(4,128)S(1)}, u32[]{:S(2)}, u32[]{:S(2)}) collective-permute-start(f32[22,3,256]{2,1,0:T(4,128)S(1)} %get-tuple-element.7), channel_id=1, source_target_pairs={{0,1},{1,2},{2,3},{3,4},{4,5},{5,6},{6,7},{8,9},{9,10},{10,11},{11... | collective-permute-start | bytes 202760 | tf_op jit(solution)/shard_map/ppermute | solution.py:191
  27.9 0.1 pad_add_fusion.refs_0_
  28.0 0.8 %collective-permute-done.3.refs_1_ = f32[22,3,256]{2,1,0:T(4,128)S(1)} collective-permute-done((f32[22,3,256]{2,1,0:T(4,128)S(1)}, f32[22,3,256]{2,1,0:T(4,128)S(1)}, u32[]{:S(2)}, u32[]{:S(2)}) %collective-permute-start.3) | collective-permute-done | bytes 67616 | tf_op jit(solution)/shard_map/ppermute | solution.py:191
  28.8 0.3 broadcast_in_dim.14.refs_11_
  29.1 12.5 %brick_attribute.1 = (f32[16,64,256]{2,1,0:T(8,128)}, f32[128,128]{1,0:T(8,128)S(1)}) custom-call(s32[4]{0:T(128)S(1)} %pad_add_fusion.refs_0_, f32[22,3,256]{2,1,0:T(4,128)S(1)} %collective-permute-done.3.refs_1_, f32[22,3,256]{2,1,0:T(4,128)S(1)} %collective-permute-done.4.refs_2_, bf16[256,256]{1,0:T(8,128)(2,1)S(1)} %get-tuple-element.16.refs_3_, ...), custom_call_target="tpu_custom_call" | custom-call | flops 2500000000 | bytes 10000000 | tf_op jit(solution)/shard_map/brick_attribute/pallas_call | solution.py:237
  41.7 1.9 %collective-permute-start.5 = (f32[4,17,128]{2,0,1:T(4,128)S(1)}, f32[4,17,128]{2,0,1:T(4,128)S(1)}, u32[]{:S(2)}, u32[]{:S(2)}) collective-permute-start(f32[4,17,128]{2,0,1:T(4,128)S(1)} %bitcast.24), channel_id=1, source_target_pairs={{0,1},{1,0},{2,3},{3,2},{4,5},{5,4},{6,7},{7,6},{8,9},{9,8},{10,11... | collective-permute-start | bytes 104456 | tf_op jit(solution)/shard_map/ppermute | solution.py:205
  43.6 0.9 %collective-permute-done.5 = f32[4,17,128]{2,0,1:T(4,128)S(1)} collective-permute-done((f32[4,17,128]{2,0,1:T(4,128)S(1)}, f32[4,17,128]{2,0,1:T(4,128)S(1)}, u32[]{:S(2)}, u32[]{:S(2)}) %collective-permute-start.5) | collective-permute-done | bytes 34848 | tf_op jit(solution)/shard_map/ppermute | solution.py:205
  44.5 2.7 %collective-permute-start.6 = (f32[2,17,128]{2,0,1:T(2,128)S(1)}, f32[2,17,128]{2,0,1:T(2,128)S(1)}, u32[]{:S(2)}, u32[]{:S(2)}) collective-permute-start(f32[2,17,128]{2,0,1:T(2,128)S(1)} %bitcast.27), channel_id=1, source_target_pairs={{0,2},{1,3},{2,0},{3,1},{4,6},{5,7},{6,4},{7,5},{8,10},{9,11},{10,... | collective-permute-start | bytes 52232 | tf_op jit(solution)/shard_map/ppermute | solution.py:205
  47.2 1.7 %collective-permute-done.6 = f32[2,17,128]{2,0,1:T(2,128)S(1)} collective-permute-done((f32[2,17,128]{2,0,1:T(2,128)S(1)}, f32[2,17,128]{2,0,1:T(2,128)S(1)}, u32[]{:S(2)}, u32[]{:S(2)}) %collective-permute-start.6) | collective-permute-done | bytes 17440 | tf_op jit(solution)/shard_map/ppermute | solution.py:205
  49.0 3.1 %collective-permute-start.7 = (f32[1,17,128]{2,0,1:T(1,128)S(1)}, f32[1,17,128]{2,0,1:T(1,128)S(1)}, u32[]{:S(2)}, u32[]{:S(2)}) collective-permute-start(f32[1,17,128]{2,0,1:T(1,128)S(1)} %constant_dynamic-slice_fusion), channel_id=1, source_target_pairs={{0,4},{1,5},{2,6},{3,7},{4,0},{5,1},{6,2},{7,3},{8,12},{9,13},{10,... | collective-permute-start | bytes 26120 | tf_op jit(solution)/shard_map/ppermute | solution.py:205
  52.1 1.6 %collective-permute-done.7 = f32[1,17,128]{2,0,1:T(1,128)S(1)} collective-permute-done((f32[1,17,128]{2,0,1:T(1,128)S(1)}, f32[1,17,128]{2,0,1:T(1,128)S(1)}, u32[]{:S(2)}, u32[]{:S(2)}) %collective-permute-start.7) | collective-permute-done | bytes 8736 | tf_op jit(solution)/shard_map/ppermute | solution.py:205
  53.8 0.7 %broadcast_divide_fusion = f32[16,128]{1,0:T(8,128)} fusion(f32[16,128]{1,0:T(8,128)S(1)} %bitcast.26, f32[16]{0:T(128)S(1)} %fusion.16), kind=kLoop, calls=%fused_computation.40 | loop fusion | flops 2048 | bytes 16448 | tf_op jit(solution)/shard_map/div | solution.py:265
  (26 shorter events, 0.2 us)
Async XLA Ops:
  0.7 6.7 %copy-start.4 = (s32[2048,1]{0,1:T(1,128)S(1)}, s32[2048,1]{0,1:T(1,128)}, u32[]{:S(2)}) copy-start(s32[2048,1]{0,1:T(1,128)} %param.6) | copy-start | bytes 24580
  0.7 6.7 %copy-start.3 = (s32[2048]{0:T(1024)S(1)}, s32[2048]{0:T(1024)}, u32[]{:S(2)}) copy-start(s32[2048]{0:T(1024)} %param.7) | copy-start | bytes 24580
  0.7 7.0 %copy-start.1 = (s32[2048]{0:T(1024)S(1)}, s32[2048]{0:T(1024)}, u32[]{:S(2)}) copy-start(s32[2048]{0:T(1024)} %param.8) | copy-start | bytes 24580
  2.9 12.4 %collective-permute-start = (f32[22,16,256]{2,1,0:T(8,128)}, f32[22,16,256]{2,1,0:T(8,128)S(1)}, u32[]{:S(2)}, u32[]{:S(2)}) collective-permute-start(f32[22,16,256]{2,1,0:T(8,128)} %get-tuple-element.9), channel_id=1, source_target_pairs={{0,8},{8,0},{16,24},{24,16},{1,9},{9,1},{17,25},{25,17},{2,10},{10... | collective-permute-start | bytes 1081352 | tf_op jit(solution)/shard_map/ppermute | solution.py:179
  5.8 16.6 %collective-permute-start.1 = (f32[22,16,256]{2,1,0:T(8,128)S(1)}, f32[22,16,256]{2,1,0:T(8,128)S(1)}, u32[]{:S(2)}, u32[]{:S(2)}) collective-permute-start(f32[22,16,256]{2,1,0:T(8,128)S(1)} %get-tuple-element.10), channel_id=1, source_target_pairs={{0,16},{8,24},{16,0},{24,8},{1,17},{9,25},{17,1},{25,9},{2,18},{10... | collective-permute-start | bytes 1081352 | tf_op jit(solution)/shard_map/ppermute | solution.py:179
  7.3 16.1 %collective-permute-start.2 = (f32[22,16,256]{2,1,0:T(8,128)S(1)}, f32[22,16,256]{2,1,0:T(8,128)S(1)}, u32[]{:S(2)}, u32[]{:S(2)}) collective-permute-start(f32[22,16,256]{2,1,0:T(8,128)S(1)} %get-tuple-element.11), channel_id=1, source_target_pairs={{0,24},{8,16},{16,8},{24,0},{1,25},{9,17},{17,9},{25,1},{2,26},{10... | collective-permute-start | bytes 1081352 | tf_op jit(solution)/shard_map/ppermute | solution.py:179
  7.7 15.7 %copy-start = (f32[64,16,256]{2,1,0:T(8,128)S(1)}, f32[64,16,256]{2,1,0:T(8,128)}, u32[]{:S(2)}) copy-start(f32[64,16,256]{2,1,0:T(8,128)} %param.5) | copy-start | bytes 3145732
  10.1 18.7 %copy-start.2 = (s32[2048]{0:T(1024)S(1)}, s32[2048]{0:T(1024)}, u32[]{:S(2)}) copy-start(s32[2048]{0:T(1024)} %param.9) | copy-start | bytes 24580
  23.6 4.4 %collective-permute-start.4 = (f32[22,3,256]{2,1,0:T(4,128)S(1)}, f32[22,3,256]{2,1,0:T(4,128)S(1)}, u32[]{:S(2)}, u32[]{:S(2)}) collective-permute-start(f32[22,3,256]{2,1,0:T(4,128)S(1)} %get-tuple-element.6), channel_id=1, source_target_pairs={{1,0},{2,1},{3,2},{4,3},{5,4},{6,5},{7,6},{9,8},{10,9},{11,10},{12... | collective-permute-start | bytes 202760 | tf_op jit(solution)/shard_map/ppermute | solution.py:192
  24.9 4.0 %collective-permute-start.3 = (f32[22,3,256]{2,1,0:T(4,128)S(1)}, f32[22,3,256]{2,1,0:T(4,128)S(1)}, u32[]{:S(2)}, u32[]{:S(2)}) collective-permute-start(f32[22,3,256]{2,1,0:T(4,128)S(1)} %get-tuple-element.7), channel_id=1, source_target_pairs={{0,1},{1,2},{2,3},{3,4},{4,5},{5,6},{6,7},{8,9},{9,10},{10,11},{11... | collective-permute-start | bytes 202760 | tf_op jit(solution)/shard_map/ppermute | solution.py:191
  41.7 2.8 %collective-permute-start.5 = (f32[4,17,128]{2,0,1:T(4,128)S(1)}, f32[4,17,128]{2,0,1:T(4,128)S(1)}, u32[]{:S(2)}, u32[]{:S(2)}) collective-permute-start(f32[4,17,128]{2,0,1:T(4,128)S(1)} %bitcast.24), channel_id=1, source_target_pairs={{0,1},{1,0},{2,3},{3,2},{4,5},{5,4},{6,7},{7,6},{8,9},{9,8},{10,11... | collective-permute-start | bytes 104456 | tf_op jit(solution)/shard_map/ppermute | solution.py:205
  44.5 4.4 %collective-permute-start.6 = (f32[2,17,128]{2,0,1:T(2,128)S(1)}, f32[2,17,128]{2,0,1:T(2,128)S(1)}, u32[]{:S(2)}, u32[]{:S(2)}) collective-permute-start(f32[2,17,128]{2,0,1:T(2,128)S(1)} %bitcast.27), channel_id=1, source_target_pairs={{0,2},{1,3},{2,0},{3,1},{4,6},{5,7},{6,4},{7,5},{8,10},{9,11},{10,... | collective-permute-start | bytes 52232 | tf_op jit(solution)/shard_map/ppermute | solution.py:205
  49.0 4.7 %collective-permute-start.7 = (f32[1,17,128]{2,0,1:T(1,128)S(1)}, f32[1,17,128]{2,0,1:T(1,128)S(1)}, u32[]{:S(2)}, u32[]{:S(2)}) collective-permute-start(f32[1,17,128]{2,0,1:T(1,128)S(1)} %constant_dynamic-slice_fusion), channel_id=1, source_target_pairs={{0,4},{1,5},{2,6},{3,7},{4,0},{5,1},{6,2},{7,3},{8,12},{9,13},{10,... | collective-permute-start | bytes 26120 | tf_op jit(solution)/shard_map/ppermute | solution.py:205

commit v2 on v1

--- a/solution.py
+++ b/solution.py
@@ -10,6 +10,10 @@
 RIM = 3
 LEAD = 8
 LANES = 128
+UNROLL_E = 5
+UNROLL_S = 1
+TILE_M = 1024
+BLOCK = 1024
 
 
 def split_bf16(values):
@@ -23,27 +27,27 @@
 
 
 def brick_kernel(
-    pieces_count, cx, cy, nt, patches, place,
+    layout, strip, cx, cy, nt, patches,
     where_ref, low_ref, high_ref, band5_ref, band9_ref, faults_ref, *refs,
 ):
-    pieces = refs[:pieces_count]
-    picks_hbm, offsets_hbm, attr_hbm, partial_ref = refs[pieces_count:pieces_count + 4]
-    amp, exy, ett, box, rows_bf, attr, picks, offsets, windows, sems = refs[pieces_count + 4:]
+    pieces = refs[:len(layout)]
+    picks_hbm, offsets_hbm, attr_hbm, partial_ref = refs[len(layout):len(layout) + 4]
+    amp, exy, ett, box, fields, rows_bf, attr, picks, offsets, windows, sems = refs[len(layout) + 4:]
     halves = nt // LANES
-    strip = cy // pieces_count
     brick, slab, bricks, slabs = where_ref[0], where_ref[1], where_ref[2], where_ref[3]
     wide = cy + 8
 
     fetches = []
-    for d in range(pieces_count):
-        column = pl.multiple_of(LEAD + strip * (brick ^ d), 8)
+    for n, (d, part, width) in enumerate(layout):
+        source = brick ^ d
+        column = LEAD + strip * source + width * part_of(source, bricks, part)
         for h in range(halves):
             fetches.append(pltpu.make_async_copy(
-                pieces[d].at[:, :, pl.ds(h * LANES, LANES)],
-                amp.at[:, h, pl.ds(column, strip), :],
-                sems.at[d * halves + h],
+                pieces[n].at[:, :, pl.ds(h * LANES, LANES)],
+                amp.at[:, h, pl.ds(pl.multiple_of(column, 8), width), :],
+                sems.at[n * halves + h],
             ))
-    base = pieces_count * halves
+    base = len(layout) * halves
     fetch_picks = pltpu.make_async_copy(picks_hbm, picks, sems.at[base])
     fetch_offsets = pltpu.make_async_copy(offsets_hbm, offsets, sems.at[base + 1])
     for copy in fetches:
@@ -85,64 +89,65 @@
             ett[e, h] = slope_t * slope_t * mask
         return carry
 
-    lax.fori_loop(0, cx + 4, energy_row, 0)
-
-    def summed(field, slot, radius, rows, band):
-        parts = []
+    lax.fori_loop(0, cx + 4, energy_row, 0, unroll=UNROLL_E)
+
+    def across(slot, h, radius, row):
+        box[slot, h] = row
+        total = box[slot, h, 0:cy, :]
+        for j in range(1, 2 * radius + 1):
+            total = total + box[slot, h, j:j + cy, :]
+        return total
+
+    def inline5(field, r, h):
+        total = field[r, h]
+        for j in range(1, 5):
+            total = total + field[r + j, h]
+        return total
+
+    def keep(index, at, h, values):
+        high, low = split_bf16(values)
+        fields[index, 0, at, h * LANES:(h + 1) * LANES] = high
+        fields[index, 1, at, h * LANES:(h + 1) * LANES] = low
+
+    def sum_row(r, carry):
+        at = pl.ds(pl.multiple_of(r * cy, 16), cy)
+        near = slice(LEAD - 1, LEAD - 1 + wide)
         for h in range(halves):
-            box[slot, h] = rows[h]
-        for h in range(halves):
-            total = box[slot, h, 0:cy, :]
-            for j in range(1, 2 * radius + 1):
-                total = total + box[slot, h, j:j + cy, :]
-            parts.append(total)
-        return parts
-
-    def through_time(parts, band):
-        whole = jnp.concatenate(parts, axis=1)
-        high, low = split_bf16(whole)
-        return dot(high, band) + dot(low, band)
-
-    def attribute_row(r, carry):
-        def inline5(field, h):
-            total = field[r, h]
-            for j in range(1, 5):
-                total = total + field[r + j, h]
-            return total
-
-        tensor_xy = through_time(
-            summed(exy, 0, 2, [inline5(exy, h) for h in range(halves)], None), band5_ref[...])
-        tensor_t = through_time(
-            summed(ett, 1, 2, [inline5(ett, h) for h in range(halves)], None), band5_ref[...])
-        near = slice(LEAD - 1, LEAD - 1 + wide)
-        stack_rows, power_rows = [], []
-        for h in range(halves):
+            keep(0, at, h, across(0, h, 2, inline5(exy, r, h)))
+            keep(1, at, h, across(1, h, 2, inline5(ett, r, h)))
             rows = [amp[r + RIM + j, h, near, :] for j in (-1, 0, 1)]
-            stack_rows.append(rows[0] + rows[1] + rows[2])
-            power_rows.append(rows[0] * rows[0] + rows[1] * rows[1] + rows[2] * rows[2])
-        stack = summed(None, 2, 1, stack_rows, None)
-        power = summed(None, 3, 1, power_rows, None)
-        spread = [9.0 * p - s * s for p, s in zip(power, stack)]
-        scatter = through_time(spread, band9_ref[...]) + 1e-5
-        whole = 9.0 * through_time(power, band9_ref[...]) + 1e-5
-        both = whole * (tensor_xy + tensor_t + 4e-5)
+            stack = across(2, h, 1, rows[0] + rows[1] + rows[2])
+            power = 9.0 * across(3, h, 1, rows[0] * rows[0] + rows[1] * rows[1] + rows[2] * rows[2])
+            keep(2, at, h, power - stack * stack)
+            keep(3, at, h, power)
+        return carry
+
+    lax.fori_loop(0, cx, sum_row, 0, unroll=UNROLL_S)
+
+    band5, band9 = band5_ref[...], band9_ref[...]
+    tile = TILE_M
+
+    def finish_tile(j, carry):
+        at = pl.ds(pl.multiple_of(j * tile, tile), tile)
+        sums = [dot(fields[f, 0, at, :], b) + dot(fields[f, 1, at, :], b)
+                for f, b in enumerate((band5, band5, band9, band9))]
+        both = (sums[3] + 1e-5) * (sums[0] + sums[1] + 4e-5)
         inverse = pl.reciprocal(both, approx=True)
         inverse = inverse * (2.0 - both * inverse)
-        values = scatter * tensor_xy * inverse
-        attr[r] = values
+        values = (sums[2] + 1e-5) * sums[0] * inverse
+        attr[at, :] = values
         high, low = split_bf16(values)
-        at = pl.ds(pl.multiple_of(r * cy, 16), cy)
         rows_bf[at, 0:nt] = high
         rows_bf[at, nt:2 * nt] = low
         return carry
 
-    lax.fori_loop(0, cx, attribute_row, 0)
+    lax.fori_loop(0, cx * cy // tile, finish_tile, 0)
     store = pltpu.make_async_copy(attr, attr_hbm, sems.at[base + 2])
     store.start()
 
     fetch_picks.wait()
     fetch_offsets.wait()
-    block = 512
+    block = BLOCK
     lane_block = lax.broadcasted_iota(jnp.int32, (block, LANES), 1)
 
     def window_block(j, carry):
@@ -168,26 +173,43 @@
     return (jnp.abs(at[:, None] - at[None, :]) <= radius).astype(jnp.bfloat16)
 
 
+def part_of(strip_index, bricks, part):
+    if part is None:
+        return 0
+    upper = (strip_index >= bricks // 2).astype(jnp.int32) if hasattr(strip_index, "astype") else int(
+        strip_index >= bricks // 2)
+    return upper if part == 0 else 1 - upper
+
+
 def exchange_bricks(amp, cx):
     bricks = lax.axis_size("brick")
     mine = lax.axis_index("brick")
+    strip = amp.shape[1]
     padded = jnp.pad(amp, ((RIM, RIM), (0, 0), (0, 0)))
-    pieces = []
-    for d in range(bricks):
-        piece = lax.dynamic_slice_in_dim(padded, (mine ^ d) * cx, cx + 2 * RIM, axis=0)
-        if d > 0:
-            piece = lax.ppermute(piece, "brick", [(s, s ^ d) for s in range(bricks)])
-        pieces.append(piece)
-    return pieces
-
-
-def halo_columns(pieces, strip):
+    rows = cx + 2 * RIM
+    parts, width = ((0, 1), strip // 2) if strip % 16 == 0 else ((None,), strip)
+    pieces, layout = [], []
+    for part in parts:
+        begin = width * part_of(mine, bricks, part)
+        for d in range(1, bricks):
+            piece = lax.dynamic_slice(
+                padded, ((mine ^ d) * cx, begin, 0), (rows, width, amp.shape[2]))
+            pieces.append(lax.ppermute(piece, "brick", [(s, s ^ d) for s in range(bricks)]))
+            layout.append((d, part, width))
+    pieces.append(lax.dynamic_slice_in_dim(padded, mine * cx, rows, axis=0))
+    layout.append((0, None, strip))
+    return pieces, layout
+
+
+def halo_columns(pieces, layout):
     bricks = lax.axis_size("brick")
     slabs = lax.axis_size("bulk")
     mine = lax.axis_index("brick")
-    left = sum(jnp.where((mine ^ d) == 0, p[:, :RIM], 0.0) for d, p in enumerate(pieces))
-    right = sum(
-        jnp.where((mine ^ d) == bricks - 1, p[:, strip - RIM:], 0.0) for d, p in enumerate(pieces))
+    left, right = 0.0, 0.0
+    for piece, (d, part, width) in zip(pieces, layout):
+        if part != 1:
+            left = jnp.where((mine ^ d) == 0, piece[:, :RIM], left)
+            right = jnp.where((mine ^ d) == bricks - 1, piece[:, width - RIM:], right)
     low = lax.ppermute(right, "bulk", [(s, s + 1) for s in range(slabs - 1)])
     high = lax.ppermute(left, "bulk", [(s + 1, s) for s in range(slabs - 1)])
     return low, high
@@ -214,8 +236,8 @@
     patches = patch_fault.shape[0]
     faults = slabs * F_DEV
 
-    pieces = exchange_bricks(amp_traces, cx)
-    low, high = halo_columns(pieces, strip)
+    pieces, layout = exchange_bricks(amp_traces, cx)
+    low, high = halo_columns(pieces, layout)
 
     picks = (patch_trace[:, None] == jnp.arange(cx * cy, dtype=jnp.int32)[None, :]).astype(jnp.bfloat16)
     offsets = jnp.broadcast_to(patch_offset[:, None], (patches, LANES))
@@ -232,27 +254,28 @@
     anywhere = pl.BlockSpec(memory_space=pl.ANY)
 
     def kernel(*refs):
-        brick_kernel(bricks, cx, cy, nt, patches, None, *refs)
+        brick_kernel(layout, strip, cx, cy, nt, patches, *refs)
 
     attribute, partial = pl.pallas_call(
         kernel,
         out_shape=(
-            jax.ShapeDtypeStruct((cx, cy, nt), jnp.float32),
+            jax.ShapeDtypeStruct((cx * cy, nt), jnp.float32),
             jax.ShapeDtypeStruct((faults, PATCH), jnp.float32),
         ),
-        in_specs=[pl.BlockSpec(memory_space=pltpu.SMEM)] + [vmem] * 5 + [anywhere] * (bricks + 2),
+        in_specs=[pl.BlockSpec(memory_space=pltpu.SMEM)] + [vmem] * 5 + [anywhere] * (len(layout) + 2),
         out_specs=(anywhere, vmem),
         scratch_shapes=[
             pltpu.VMEM((cx + 2 * RIM, halves, cy + 2 * LEAD, LANES), jnp.float32),
             pltpu.VMEM((cx + 4, halves, wide, LANES), jnp.float32),
             pltpu.VMEM((cx + 4, halves, wide, LANES), jnp.float32),
             pltpu.VMEM((4, halves, wide, LANES), jnp.float32),
+            pltpu.VMEM((4, 2, cx * cy, nt), jnp.bfloat16),
             pltpu.VMEM((cx * cy, 2 * nt), jnp.bfloat16),
-            pltpu.VMEM((cx, cy, nt), jnp.float32),
+            pltpu.VMEM((cx * cy, nt), jnp.float32),
             pltpu.VMEM((patches, cx * cy), jnp.bfloat16),
             pltpu.VMEM((patches, LANES), jnp.int32),
             pltpu.VMEM((patches, 2 * PATCH), jnp.bfloat16),
-            pltpu.SemaphoreType.DMA((bricks * halves + 3,)),
+            pltpu.SemaphoreType.DMA((len(layout) * halves + 3,)),
         ],
         compiler_params=pltpu.CompilerParams(vmem_limit_bytes=48 * 1024 * 1024),
         cost_estimate=pl.CostEstimate(flops=2_500_000_000, bytes_accessed=10_000_000, transcendentals=0),
@@ -263,7 +286,7 @@
     parts = jnp.concatenate([partial.reshape(slabs, F_DEV, PATCH), tally], axis=1)
     total = reduce_scatter(parts, "bulk")
     profile = total[:F_DEV] / jnp.maximum(total[F_DEV, :F_DEV], 1.0)[:, None]
-    return attribute, profile
+    return attribute.reshape(cx, cy, nt), profile
 
 
 def solution(mesh):

time: 54.6 us -> 47 us (0.86)
  waiting for transfers between devices: 18.2 us -> 8.45 us
  starting transfers between devices: 16.5 us -> 22 us
  Pallas kernels: 12.5 us -> 8.94 us
    ppermute x3 -> x6, waiting for transfers between devices: 13.2 us -> 3.42 us  [exchange_bricks(): lax.ppermute(piece, 'brick', [(s, s ^ d) for s in range(bricks)])]
    ppermute x3 -> x6, starting transfers between devices: 4.46 us -> 9.85 us  [exchange_bricks(): lax.ppermute(piece, 'brick', [(s, s ^ d) for s in range(bricks)])]
    pallas_call x1, Pallas kernels: 12.5 us -> 8.94 us  [local(): pl.pallas_call(kernel, out_shape=(jax.ShapeDtypeStruct((cx * cy, nt), jnp...]
    dynamic_slice x1 -> x2, local copies, waits for them, and re-layouts: 2.17 us -> 2.2 us  [the longest x1 2.16 us: exchange_bricks(): lax.dynamic_slice(padded, ((mine ^ d) * cx, begin, 0), (rows, width, amp....]
  transfers between devices with their start and end apart: 8 -> 11, of which waited for: 7 -> 6; matrix products, arithmetic and copies ran while one was open for 5% -> 7% of each run, Pallas kernels for 0% -> 0%
where the time goes in v2:
time: 47 us; the launch traced here: 46.7 us
  starting transfers between devices  22 us (47%)
  Pallas kernels  8.94 us (19%)
  waiting for transfers between devices  8.45 us (18%)
  other arithmetic  3.67 us (8%)
  local copies, waits for them, and re-layouts  2.7 us (6%)
  between operations  0.92 us (2%)
    ppermute x6, starting transfers between devices, exchange_bricks(): lax.ppermute(piece, 'brick', [(s, s ^ d) for s in range(bricks)])  9.85 us
    pallas_call x1, Pallas kernels, local(): pl.pallas_call(kernel, out_shape=(jax.ShapeDtypeStruct((cx * cy, nt), jnp...  8.94 us
    ppermute x3, starting transfers between devices, reduce_scatter(): lax.ppermute(sent, axis, [(s, s ^ bit) for s in range(count)])  7.87 us
    ppermute x3, waiting for transfers between devices, reduce_scatter(): lax.ppermute(sent, axis, [(s, s ^ bit) for s in range(count)])  4.23 us
    ppermute x6, waiting for transfers between devices, exchange_bricks(): lax.ppermute(piece, 'brick', [(s, s ^ d) for s in range(bricks)])  3.42 us
    ppermute x1, starting transfers between devices, halo_columns(): low = lax.ppermute(right, 'bulk', [(s, s + 1) for s in range(slabs - 1)])  3.04 us
    convert_element_type x1, other arithmetic, local(): (patch_trace[:, None] == jnp.arange(cx * cy, dtype=jnp.int32)[None, :]).a...  2.38 us
    dynamic_slice x1, local copies, waits for them, and re-layouts, exchange_bricks(): lax.dynamic_slice(padded, ((mine ^ d) * cx, begin, 0), (rows, width, amp....  2.16 us
  transfers between devices with their start and end apart: 11, of which 6 were waited for; matrix products, arithmetic and copies ran while one was open for 7% of the time, Pallas kernels for 0%

profile of v2, /device:TPU:0, one launch (start us, length us, event | category | flops | bytes accessed | tf_op | source)
XLA Modules:
  0.0 46.7 jit_solution(2154384720846476301)
XLA Ops:
  0.7 2.2 %pad_dynamic-slice_fusion.2 = (f32[22,8,256]{2,1,0:T(8,128)S(1)}, f32[22,8,256]{2,1,0:T(8,128)}, f32[22,8,256]{2,1,0:T(8,128)}, f32[22,8,256]{2,1,0:T(8,128)S(1)...) fusion(s32[]{:T(128)S(6)} %select_n.122, s32[]{:T(128)S(6)} %select_n.139, f32[64,16,256]{2,1,0:T(8,128)} %param.5, ...), kind=kLoop, calls=%fused_computation.7 | loop fusion | bytes 2129940 | tf_op jit(solution)/shard_map/dynamic_slice | solution.py:195
  2.8 3.9 %collective-permute-start.7 = (f32[22,8,256]{2,1,0:T(8,128)S(1)}, f32[22,8,256]{2,1,0:T(8,128)S(1)}, u32[]{:S(2)}, u32[]{:S(2)}) collective-permute-start(f32[22,8,256]{2,1,0:T(8,128)S(1)} %get-tuple-element.8), channel_id=1, source_target_pairs={{0,24},{8,16},{16,8},{24,0},{1,25},{9,17},{17,9},{25,1},{2,26},{10... | collective-permute-start | bytes 540680 | tf_op jit(solution)/shard_map/ppermute | solution.py:197
  6.7 0.5 %collective-permute-start.1 = (f32[22,8,256]{2,1,0:T(8,128)}, f32[22,8,256]{2,1,0:T(8,128)S(1)}, u32[]{:S(2)}, u32[]{:S(2)}) collective-permute-start(f32[22,8,256]{2,1,0:T(8,128)} %get-tuple-element.9), channel_id=1, source_target_pairs={{0,16},{8,24},{16,0},{24,8},{1,17},{9,25},{17,1},{25,9},{2,18},{10... | collective-permute-start | bytes 540680 | tf_op jit(solution)/shard_map/ppermute | solution.py:197
  7.3 2.0 %collective-permute-start.6 = (f32[22,8,256]{2,1,0:T(8,128)S(1)}, f32[22,8,256]{2,1,0:T(8,128)S(1)}, u32[]{:S(2)}, u32[]{:S(2)}) collective-permute-start(f32[22,8,256]{2,1,0:T(8,128)S(1)} %get-tuple-element.11), channel_id=1, source_target_pairs={{0,16},{8,24},{16,0},{24,8},{1,17},{9,25},{17,1},{25,9},{2,18},{10... | collective-permute-start | bytes 540680 | tf_op jit(solution)/shard_map/ppermute | solution.py:197
  9.3 1.4 %collective-permute-start = (f32[22,8,256]{2,1,0:T(8,128)S(1)}, f32[22,8,256]{2,1,0:T(8,128)S(1)}, u32[]{:S(2)}, u32[]{:S(2)}) collective-permute-start(f32[22,8,256]{2,1,0:T(8,128)S(1)} %get-tuple-element.13), channel_id=1, source_target_pairs={{0,24},{8,16},{16,8},{24,0},{1,25},{9,17},{17,9},{25,1},{2,26},{10... | collective-permute-start | bytes 540680 | tf_op jit(solution)/shard_map/ppermute | solution.py:197
  10.8 0.2 convert_reduce_fusion
  10.9 0.1 fusion.1.refs_5_
  11.1 2.4 %fusion.refs_13_ = bf16[2048,1024]{1,0:T(8,128)(2,1)} fusion(s32[2048]{0:T(1024)S(1)} %copy-done.1), kind=kLoop, calls=%fused_computation.1 | loop fusion | flops 4194304 | bytes 4202496 | tf_op jit(solution)/shard_map/convert_element_type | solution.py:242
  13.7 2.4 %collective-permute-done.1.refs_7_ = f32[22,8,256]{2,1,0:T(8,128)S(1)} collective-permute-done((f32[22,8,256]{2,1,0:T(8,128)}, f32[22,8,256]{2,1,0:T(8,128)S(1)}, u32[]{:S(2)}, u32[]{:S(2)}) %collective-permute-start.1) | collective-permute-done | bytes 180256 | tf_op jit(solution)/shard_map/ppermute | solution.py:197
  16.1 2.0 %collective-permute-start.5 = (f32[22,8,256]{2,1,0:T(8,128)S(1)}, f32[22,8,256]{2,1,0:T(8,128)S(1)}, u32[]{:S(2)}, u32[]{:S(2)}) collective-permute-start(f32[22,8,256]{2,1,0:T(8,128)S(1)} %get-tuple-element.12), channel_id=1, source_target_pairs={{0,8},{8,0},{16,24},{24,16},{1,9},{9,1},{17,25},{25,17},{2,10},{10... | collective-permute-start | bytes 540680 | tf_op jit(solution)/shard_map/ppermute | solution.py:197
  18.1 1.0 %collective-permute-done.refs_8_ = f32[22,8,256]{2,1,0:T(8,128)S(1)} collective-permute-done((f32[22,8,256]{2,1,0:T(8,128)S(1)}, f32[22,8,256]{2,1,0:T(8,128)S(1)}, u32[]{:S(2)}, u32[]{:S(2)}) %collective-permute-start) | collective-permute-done | bytes 180256 | tf_op jit(solution)/shard_map/ppermute | solution.py:197
  19.1 0.1 fusion.7
  19.2 1.3 %collective-permute-start.4 = (f32[22,3,256]{2,1,0:T(4,128)S(1)}, f32[22,3,256]{2,1,0:T(4,128)S(1)}, u32[]{:S(2)}, u32[]{:S(2)}) collective-permute-start(f32[22,3,256]{2,1,0:T(4,128)S(1)} %get-tuple-element.6), channel_id=1, source_target_pairs={{1,0},{2,1},{3,2},{4,3},{5,4},{6,5},{7,6},{9,8},{10,9},{11,10},{12... | collective-permute-start | bytes 202760 | tf_op jit(solution)/shard_map/ppermute | solution.py:214
  20.5 3.0 %collective-permute-start.3 = (f32[22,3,256]{2,1,0:T(4,128)S(1)}, f32[22,3,256]{2,1,0:T(4,128)S(1)}, u32[]{:S(2)}, u32[]{:S(2)}) collective-permute-start(f32[22,3,256]{2,1,0:T(4,128)S(1)} %get-tuple-element.7), channel_id=1, source_target_pairs={{0,1},{1,2},{2,3},{3,4},{4,5},{5,6},{6,7},{8,9},{9,10},{10,11},{11... | collective-permute-start | bytes 202760 | tf_op jit(solution)/shard_map/ppermute | solution.py:213
  23.7 0.8 %collective-permute-done.3.refs_1_ = f32[22,3,256]{2,1,0:T(4,128)S(1)} collective-permute-done((f32[22,3,256]{2,1,0:T(4,128)S(1)}, f32[22,3,256]{2,1,0:T(4,128)S(1)}, u32[]{:S(2)}, u32[]{:S(2)}) %collective-permute-start.3) | collective-permute-done | bytes 67616 | tf_op jit(solution)/shard_map/ppermute | solution.py:213
  24.5 0.3 broadcast_in_dim.8.refs_14_
  24.8 8.9 %brick_attribute.1 = (f32[1024,256]{1,0:T(8,128)}, f32[128,128]{1,0:T(8,128)S(1)}) custom-call(s32[4]{0:T(128)S(1)} %pad_add_fusion.refs_0_, f32[22,3,256]{2,1,0:T(4,128)S(1)} %collective-permute-done.3.refs_1_, f32[22,3,256]{2,1,0:T(4,128)S(1)} %collective-permute-done.4.refs_2_, bf16[256,256]{1,0:T(8,128)(2,1)S(1)} %get-tuple-element.18.refs_3_, ...), custom_call_target="tpu_custom_call" | custom-call | flops 2500000000 | bytes 10000000 | tf_op jit(solution)/shard_map/brick_attribute/pallas_call | solution.py:259
  33.8 2.1 %collective-permute-start.8 = (f32[4,17,128]{2,0,1:T(4,128)S(1)}, f32[4,17,128]{2,0,1:T(4,128)S(1)}, u32[]{:S(2)}, u32[]{:S(2)}) collective-permute-start(f32[4,17,128]{2,0,1:T(4,128)S(1)} %bitcast.25), channel_id=1, source_target_pairs={{0,1},{1,0},{2,3},{3,2},{4,5},{5,4},{6,7},{7,6},{8,9},{9,8},{10,11... | collective-permute-start | bytes 104456 | tf_op jit(solution)/shard_map/ppermute | solution.py:227
  35.9 0.9 %collective-permute-done.8 = f32[4,17,128]{2,0,1:T(4,128)S(1)} collective-permute-done((f32[4,17,128]{2,0,1:T(4,128)S(1)}, f32[4,17,128]{2,0,1:T(4,128)S(1)}, u32[]{:S(2)}, u32[]{:S(2)}) %collective-permute-start.8) | collective-permute-done | bytes 34848 | tf_op jit(solution)/shard_map/ppermute | solution.py:227
  36.8 2.7 %collective-permute-start.9 = (f32[2,17,128]{2,0,1:T(2,128)S(1)}, f32[2,17,128]{2,0,1:T(2,128)S(1)}, u32[]{:S(2)}, u32[]{:S(2)}) collective-permute-start(f32[2,17,128]{2,0,1:T(2,128)S(1)} %bitcast.28), channel_id=1, source_target_pairs={{0,2},{1,3},{2,0},{3,1},{4,6},{5,7},{6,4},{7,5},{8,10},{9,11},{10,... | collective-permute-start | bytes 52232 | tf_op jit(solution)/shard_map/ppermute | solution.py:227
  39.5 1.7 %collective-permute-done.9 = f32[2,17,128]{2,0,1:T(2,128)S(1)} collective-permute-done((f32[2,17,128]{2,0,1:T(2,128)S(1)}, f32[2,17,128]{2,0,1:T(2,128)S(1)}, u32[]{:S(2)}, u32[]{:S(2)}) %collective-permute-start.9) | collective-permute-done | bytes 17440 | tf_op jit(solution)/shard_map/ppermute | solution.py:227
  41.3 3.1 %collective-permute-start.10 = (f32[1,17,128]{2,0,1:T(1,128)S(1)}, f32[1,17,128]{2,0,1:T(1,128)S(1)}, u32[]{:S(2)}, u32[]{:S(2)}) collective-permute-start(f32[1,17,128]{2,0,1:T(1,128)S(1)} %constant_dynamic-slice_fusion), channel_id=1, source_target_pairs={{0,4},{1,5},{2,6},{3,7},{4,0},{5,1},{6,2},{7,3},{8,12},{9,13},{10,... | collective-permute-start | bytes 26120 | tf_op jit(solution)/shard_map/ppermute | solution.py:227
  44.4 1.6 %collective-permute-done.10 = f32[1,17,128]{2,0,1:T(1,128)S(1)} collective-permute-done((f32[1,17,128]{2,0,1:T(1,128)S(1)}, f32[1,17,128]{2,0,1:T(1,128)S(1)}, u32[]{:S(2)}, u32[]{:S(2)}) %collective-permute-start.10) | collective-permute-done | bytes 8736 | tf_op jit(solution)/shard_map/ppermute | solution.py:227
  46.1 0.7 %broadcast_divide_fusion = f32[16,128]{1,0:T(8,128)} fusion(f32[16,128]{1,0:T(8,128)S(1)} %bitcast.27, f32[16]{0:T(128)S(1)} %fusion.14), kind=kLoop, calls=%fused_computation.40 | loop fusion | flops 2048 | bytes 16448 | tf_op jit(solution)/shard_map/div | solution.py:288
  (33 shorter events, 0.5 us)
Async XLA Ops:
  0.6 10.1 %copy-start.4 = (s32[2048,1]{0,1:T(1,128)S(1)}, s32[2048,1]{0,1:T(1,128)}, u32[]{:S(2)}) copy-start(s32[2048,1]{0,1:T(1,128)} %param.6) | copy-start | bytes 24580
  0.6 10.1 %copy-start.3 = (s32[2048]{0:T(1024)S(1)}, s32[2048]{0:T(1024)}, u32[]{:S(2)}) copy-start(s32[2048]{0:T(1024)} %param.7) | copy-start | bytes 24580
  0.7 10.4 %copy-start.1 = (s32[2048]{0:T(1024)S(1)}, s32[2048]{0:T(1024)}, u32[]{:S(2)}) copy-start(s32[2048]{0:T(1024)} %param.8) | copy-start | bytes 24580
  2.8 20.8 %collective-permute-start.7 = (f32[22,8,256]{2,1,0:T(8,128)S(1)}, f32[22,8,256]{2,1,0:T(8,128)S(1)}, u32[]{:S(2)}, u32[]{:S(2)}) collective-permute-start(f32[22,8,256]{2,1,0:T(8,128)S(1)} %get-tuple-element.8), channel_id=1, source_target_pairs={{0,24},{8,16},{16,8},{24,0},{1,25},{9,17},{17,9},{25,1},{2,26},{10... | collective-permute-start | bytes 540680 | tf_op jit(solution)/shard_map/ppermute | solution.py:197
  6.7 9.3 %collective-permute-start.1 = (f32[22,8,256]{2,1,0:T(8,128)}, f32[22,8,256]{2,1,0:T(8,128)S(1)}, u32[]{:S(2)}, u32[]{:S(2)}) collective-permute-start(f32[22,8,256]{2,1,0:T(8,128)} %get-tuple-element.9), channel_id=1, source_target_pairs={{0,16},{8,24},{16,0},{24,8},{1,17},{9,25},{17,1},{25,9},{2,18},{10... | collective-permute-start | bytes 540680 | tf_op jit(solution)/shard_map/ppermute | solution.py:197
  7.2 10.8 %collective-permute-start.2 = (f32[22,8,256]{2,1,0:T(8,128)}, f32[22,8,256]{2,1,0:T(8,128)S(1)}, u32[]{:S(2)}, u32[]{:S(2)}) collective-permute-start(f32[22,8,256]{2,1,0:T(8,128)} %get-tuple-element.10), channel_id=1, source_target_pairs={{0,8},{8,0},{16,24},{24,16},{1,9},{9,1},{17,25},{25,17},{2,10},{10... | collective-permute-start | bytes 540680 | tf_op jit(solution)/shard_map/ppermute | solution.py:197
  7.3 16.4 %collective-permute-start.6 = (f32[22,8,256]{2,1,0:T(8,128)S(1)}, f32[22,8,256]{2,1,0:T(8,128)S(1)}, u32[]{:S(2)}, u32[]{:S(2)}) collective-permute-start(f32[22,8,256]{2,1,0:T(8,128)S(1)} %get-tuple-element.11), channel_id=1, source_target_pairs={{0,16},{8,24},{16,0},{24,8},{1,17},{9,25},{17,1},{25,9},{2,18},{10... | collective-permute-start | bytes 540680 | tf_op jit(solution)/shard_map/ppermute | solution.py:197
  9.3 9.8 %collective-permute-start = (f32[22,8,256]{2,1,0:T(8,128)S(1)}, f32[22,8,256]{2,1,0:T(8,128)S(1)}, u32[]{:S(2)}, u32[]{:S(2)}) collective-permute-start(f32[22,8,256]{2,1,0:T(8,128)S(1)} %get-tuple-element.13), channel_id=1, source_target_pairs={{0,24},{8,16},{16,8},{24,0},{1,25},{9,17},{17,9},{25,1},{2,26},{10... | collective-permute-start | bytes 540680 | tf_op jit(solution)/shard_map/ppermute | solution.py:197
  11.1 2.6 %copy-start = (f32[64,16,256]{2,1,0:T(8,128)S(1)}, f32[64,16,256]{2,1,0:T(8,128)}, u32[]{:S(2)}) copy-start(f32[64,16,256]{2,1,0:T(8,128)} %param.5) | copy-start | bytes 3145732
  13.7 10.8 %copy-start.2 = (s32[2048]{0:T(1024)S(1)}, s32[2048]{0:T(1024)}, u32[]{:S(2)}) copy-start(s32[2048]{0:T(1024)} %param.9) | copy-start | bytes 24580
  16.1 7.6 %collective-permute-start.5 = (f32[22,8,256]{2,1,0:T(8,128)S(1)}, f32[22,8,256]{2,1,0:T(8,128)S(1)}, u32[]{:S(2)}, u32[]{:S(2)}) collective-permute-start(f32[22,8,256]{2,1,0:T(8,128)S(1)} %get-tuple-element.12), channel_id=1, source_target_pairs={{0,8},{8,0},{16,24},{24,16},{1,9},{9,1},{17,25},{25,17},{2,10},{10... | collective-permute-start | bytes 540680 | tf_op jit(solution)/shard_map/ppermute | solution.py:197
  19.2 4.4 %collective-permute-start.4 = (f32[22,3,256]{2,1,0:T(4,128)S(1)}, f32[22,3,256]{2,1,0:T(4,128)S(1)}, u32[]{:S(2)}, u32[]{:S(2)}) collective-permute-start(f32[22,3,256]{2,1,0:T(4,128)S(1)} %get-tuple-element.6), channel_id=1, source_target_pairs={{1,0},{2,1},{3,2},{4,3},{5,4},{6,5},{7,6},{9,8},{10,9},{11,10},{12... | collective-permute-start | bytes 202760 | tf_op jit(solution)/shard_map/ppermute | solution.py:214
  20.5 4.0 %collective-permute-start.3 = (f32[22,3,256]{2,1,0:T(4,128)S(1)}, f32[22,3,256]{2,1,0:T(4,128)S(1)}, u32[]{:S(2)}, u32[]{:S(2)}) collective-permute-start(f32[22,3,256]{2,1,0:T(4,128)S(1)} %get-tuple-element.7), channel_id=1, source_target_pairs={{0,1},{1,2},{2,3},{3,4},{4,5},{5,6},{6,7},{8,9},{9,10},{10,11},{11... | collective-permute-start | bytes 202760 | tf_op jit(solution)/shard_map/ppermute | solution.py:213
  33.8 3.0 %collective-permute-start.8 = (f32[4,17,128]{2,0,1:T(4,128)S(1)}, f32[4,17,128]{2,0,1:T(4,128)S(1)}, u32[]{:S(2)}, u32[]{:S(2)}) collective-permute-start(f32[4,17,128]{2,0,1:T(4,128)S(1)} %bitcast.25), channel_id=1, source_target_pairs={{0,1},{1,0},{2,3},{3,2},{4,5},{5,4},{6,7},{7,6},{8,9},{9,8},{10,11... | collective-permute-start | bytes 104456 | tf_op jit(solution)/shard_map/ppermute | solution.py:227
  36.8 4.4 %collective-permute-start.9 = (f32[2,17,128]{2,0,1:T(2,128)S(1)}, f32[2,17,128]{2,0,1:T(2,128)S(1)}, u32[]{:S(2)}, u32[]{:S(2)}) collective-permute-start(f32[2,17,128]{2,0,1:T(2,128)S(1)} %bitcast.28), channel_id=1, source_target_pairs={{0,2},{1,3},{2,0},{3,1},{4,6},{5,7},{6,4},{7,5},{8,10},{9,11},{10,... | collective-permute-start | bytes 52232 | tf_op jit(solution)/shard_map/ppermute | solution.py:227
  41.3 4.7 %collective-permute-start.10 = (f32[1,17,128]{2,0,1:T(1,128)S(1)}, f32[1,17,128]{2,0,1:T(1,128)S(1)}, u32[]{:S(2)}, u32[]{:S(2)}) collective-permute-start(f32[1,17,128]{2,0,1:T(1,128)S(1)} %constant_dynamic-slice_fusion), channel_id=1, source_target_pairs={{0,4},{1,5},{2,6},{3,7},{4,0},{5,1},{6,2},{7,3},{8,12},{9,13},{10,... | collective-permute-start | bytes 26120 | tf_op jit(solution)/shard_map/ppermute | solution.py:227

commit v3 on v2

--- a/solution.py
+++ b/solution.py
@@ -10,10 +10,8 @@
 RIM = 3
 LEAD = 8
 LANES = 128
-UNROLL_E = 5
-UNROLL_S = 1
 TILE_M = 1024
-BLOCK = 1024
+BLOCK = 256
 
 
 def split_bf16(values):
@@ -37,14 +35,17 @@
     brick, slab, bricks, slabs = where_ref[0], where_ref[1], where_ref[2], where_ref[3]
     wide = cy + 8
 
+    rows = cx + 2 * RIM
+    top = jnp.where(brick == 0, 2 * RIM, jnp.where(brick == bricks - 1, 0, RIM))
     fetches = []
     for n, (d, part, width) in enumerate(layout):
         source = brick ^ d
         column = LEAD + strip * source + width * part_of(source, bricks, part)
+        piece = pieces[n] if d else pieces[n].at[pl.ds(brick * cx + top - 2 * RIM, rows)]
         for h in range(halves):
             fetches.append(pltpu.make_async_copy(
-                pieces[n].at[:, :, pl.ds(h * LANES, LANES)],
-                amp.at[:, h, pl.ds(pl.multiple_of(column, 8), width), :],
+                piece.at[:, :, pl.ds(h * LANES, LANES)],
+                amp.at[h, pl.ds(top, rows), pl.ds(pl.multiple_of(column, 8), width), :],
                 sems.at[n * halves + h],
             ))
     base = len(layout) * halves
@@ -54,12 +55,22 @@
         copy.start()
     fetch_picks.start()
     fetch_offsets.start()
+    even = lax.rem(slab, 2) == 0
     for h in range(halves):
         lanes = pl.ds(h * LANES, LANES)
-        amp[:, h, LEAD - RIM:LEAD, :] = low_ref[:, :, lanes]
-        amp[:, h, LEAD + cy:LEAD + cy + RIM, :] = high_ref[:, :, lanes]
+        near, far = low_ref[:, :, lanes], high_ref[:, :, lanes]
+        amp[h, pl.ds(top, rows), LEAD - RIM:LEAD, :] = jnp.where(even, far, near)
+        amp[h, pl.ds(top, rows), LEAD + cy:LEAD + cy + RIM, :] = jnp.where(even, near, far)
     for copy in fetches:
         copy.wait()
+
+    @pl.when(brick == 0)
+    def _():
+        amp[:, RIM:2 * RIM] = jnp.zeros((halves, RIM) + amp.shape[2:], jnp.float32)
+
+    @pl.when(brick == bricks - 1)
+    def _():
+        amp[:, cx + 2 * RIM:cx + 3 * RIM] = jnp.zeros((halves, RIM) + amp.shape[2:], jnp.float32)
 
     lane = lax.broadcasted_iota(jnp.int32, (wide, LANES), 1)
     first, last = lane == 0, lane == LANES - 1
@@ -74,14 +85,14 @@
         position = brick * cx + e - 2
         valid = jnp.logical_and(position >= 0, position < bricks * cx).astype(jnp.float32)
         mask = inside * valid
-        centre = [amp[e + 1, h, origin + 1:origin + 1 + wide, :] for h in range(halves)]
+        centre = [amp[h, e + 1 + RIM, origin + 1:origin + 1 + wide, :] for h in range(halves)]
         back = [pltpu.roll(c, 1, 1) for c in centre]
         ahead = [pltpu.roll(c, LANES - 1, 1) for c in centre]
         for h in range(halves):
-            slope_x = (amp[e + 2, h, origin + 1:origin + 1 + wide, :]
-                       - amp[e, h, origin + 1:origin + 1 + wide, :])
-            slope_y = (amp[e + 1, h, origin + 2:origin + 2 + wide, :]
-                       - amp[e + 1, h, origin:origin + wide, :])
+            slope_x = (amp[h, e + 2 + RIM, origin + 1:origin + 1 + wide, :]
+                       - amp[h, e + RIM, origin + 1:origin + 1 + wide, :])
+            slope_y = (amp[h, e + 1 + RIM, origin + 2:origin + 2 + wide, :]
+                       - amp[h, e + 1 + RIM, origin:origin + wide, :])
             before = jnp.where(first, back[h - 1] if h > 0 else 0.0, back[h])
             after = jnp.where(last, ahead[h + 1] if h < halves - 1 else 0.0, ahead[h])
             slope_t = after - before
@@ -89,7 +100,7 @@
             ett[e, h] = slope_t * slope_t * mask
         return carry
 
-    lax.fori_loop(0, cx + 4, energy_row, 0, unroll=UNROLL_E)
+    lax.fori_loop(0, cx + 4, energy_row, 0, unroll=True)
 
     def across(slot, h, radius, row):
         box[slot, h] = row
@@ -99,30 +110,39 @@
         return total
 
     def inline5(field, r, h):
-        total = field[r, h]
-        for j in range(1, 5):
-            total = total + field[r + j, h]
-        return total
+        e = [field[r + j, h] for j in range(8)]
+        low, middle, high = e[1] + e[2], e[3] + e[4], e[5] + e[6]
+        left, right = low + middle, middle + high
+        return left + e[0], left + e[5], right + e[2], right + e[7]
+
+    def inline3(e):
+        low, high = e[1] + e[2], e[3] + e[4]
+        return low + e[0], low + e[3], high + e[2], high + e[5]
 
     def keep(index, at, h, values):
         high, low = split_bf16(values)
         fields[index, 0, at, h * LANES:(h + 1) * LANES] = high
         fields[index, 1, at, h * LANES:(h + 1) * LANES] = low
 
-    def sum_row(r, carry):
-        at = pl.ds(pl.multiple_of(r * cy, 16), cy)
+    def sum_rows(q, carry):
+        r = 4 * q
         near = slice(LEAD - 1, LEAD - 1 + wide)
         for h in range(halves):
-            keep(0, at, h, across(0, h, 2, inline5(exy, r, h)))
-            keep(1, at, h, across(1, h, 2, inline5(ett, r, h)))
-            rows = [amp[r + RIM + j, h, near, :] for j in (-1, 0, 1)]
-            stack = across(2, h, 1, rows[0] + rows[1] + rows[2])
-            power = 9.0 * across(3, h, 1, rows[0] * rows[0] + rows[1] * rows[1] + rows[2] * rows[2])
-            keep(2, at, h, power - stack * stack)
-            keep(3, at, h, power)
+            rows = [amp[h, r + 2 * RIM - 1 + j, near, :] for j in range(6)]
+            stacks = inline3(rows)
+            powers = inline3([row * row for row in rows])
+            xys, ts = inline5(exy, r, h), inline5(ett, r, h)
+            for j in range(4):
+                at = pl.ds(pl.multiple_of((r + j) * cy, 16), cy)
+                keep(0, at, h, across(4 * j + 0, h, 2, xys[j]))
+                keep(1, at, h, across(4 * j + 1, h, 2, ts[j]))
+                stack = across(4 * j + 2, h, 1, stacks[j])
+                power = 9.0 * across(4 * j + 3, h, 1, powers[j])
+                keep(2, at, h, power - stack * stack)
+                keep(3, at, h, power)
         return carry
 
-    lax.fori_loop(0, cx, sum_row, 0, unroll=UNROLL_S)
+    lax.fori_loop(0, cx // 4, sum_rows, 0, unroll=True)
 
     band5, band9 = band5_ref[...], band9_ref[...]
     tile = TILE_M
@@ -162,7 +182,7 @@
         windows[at, PATCH:2 * PATCH] = low
         return carry
 
-    lax.fori_loop(0, patches // block, window_block, 0)
+    lax.fori_loop(0, patches // block, window_block, 0, unroll=True)
     sums = dot(faults_ref[...], windows[...])
     partial_ref[...] = sums[:, 0:PATCH] + sums[:, PATCH:2 * PATCH]
     store.wait()
@@ -184,35 +204,57 @@
 def exchange_bricks(amp, cx):
     bricks = lax.axis_size("brick")
     mine = lax.axis_index("brick")
-    strip = amp.shape[1]
-    padded = jnp.pad(amp, ((RIM, RIM), (0, 0), (0, 0)))
+    nx, strip, nt = amp.shape
     rows = cx + 2 * RIM
     parts, width = ((0, 1), strip // 2) if strip % 16 == 0 else ((None,), strip)
+    order = (bricks - 1, *range(1, bricks - 1))
     pieces, layout = [], []
+
+    def cut(source, d, begin, columns):
+        first = jnp.clip((mine ^ d) * cx - RIM, 0, nx - rows)
+        return lax.dynamic_slice(source, (first, begin, 0), (rows, columns, nt))
+
+    def send(piece, d):
+        return lax.ppermute(piece, "brick", [(s, s ^ d) for s in range(bricks)])
+
+    source = amp
     for part in parts:
         begin = width * part_of(mine, bricks, part)
-        for d in range(1, bricks):
-            piece = lax.dynamic_slice(
-                padded, ((mine ^ d) * cx, begin, 0), (rows, width, amp.shape[2]))
-            pieces.append(lax.ppermute(piece, "brick", [(s, s ^ d) for s in range(bricks)]))
+        for n, d in enumerate(order):
+            piece = cut(source, d, begin, width)
+            if part == 1:
+                piece, _ = lax.optimization_barrier((piece, pieces[n]))
+            elif n == 0:
+                source, piece = lax.optimization_barrier((amp, piece))
+            pieces.append(send(piece, d))
             layout.append((d, part, width))
-    pieces.append(lax.dynamic_slice_in_dim(padded, mine * cx, rows, axis=0))
+    pieces.append(amp)
     layout.append((0, None, strip))
     return pieces, layout
 
 
-def halo_columns(pieces, layout):
+def halo_columns(pieces, layout, cx, prepared):
     bricks = lax.axis_size("brick")
     slabs = lax.axis_size("bulk")
     mine = lax.axis_index("brick")
+    rows = cx + 2 * RIM
     left, right = 0.0, 0.0
     for piece, (d, part, width) in zip(pieces, layout):
+        if d == 0:
+            first = jnp.clip(mine * cx - RIM, 0, piece.shape[0] - rows)
+            piece = lax.dynamic_slice_in_dim(piece, first, rows, axis=0)
         if part != 1:
             left = jnp.where((mine ^ d) == 0, piece[:, :RIM], left)
             right = jnp.where((mine ^ d) == bricks - 1, piece[:, width - RIM:], right)
-    low = lax.ppermute(right, "bulk", [(s, s + 1) for s in range(slabs - 1)])
-    high = lax.ppermute(left, "bulk", [(s + 1, s) for s in range(slabs - 1)])
-    return low, high
+    left, right, *prepared = lax.optimization_barrier((left, right, *prepared))
+    even = lax.axis_index("bulk") % 2 == 0
+    inner = [p for s in range(0, slabs - 1, 2) for p in ((s, s + 1), (s + 1, s))]
+    outer = [p for s in range(1, slabs - 1, 2) for p in ((s, s + 1), (s + 1, s))]
+    near, far = jnp.where(even, right, left), jnp.where(even, left, right)
+    far = lax.ppermute(far, "bulk", outer)
+    near = lax.ppermute(near, "bulk", inner)
+    low, high = near, far
+    return low, high, prepared
 
 
 def reduce_scatter(parts, axis):
@@ -237,10 +279,10 @@
     faults = slabs * F_DEV
 
     pieces, layout = exchange_bricks(amp_traces, cx)
-    low, high = halo_columns(pieces, layout)
+    offsets = jnp.broadcast_to(patch_offset[:, None], (patches, LANES))
+    low, high, (offsets,) = halo_columns(pieces, layout, cx, (offsets,))
 
     picks = (patch_trace[:, None] == jnp.arange(cx * cy, dtype=jnp.int32)[None, :]).astype(jnp.bfloat16)
-    offsets = jnp.broadcast_to(patch_offset[:, None], (patches, LANES))
     fault = patch_owner[:, 0] * F_DEV + patch_fault
     members = fault[None, :] == jnp.arange(faults, dtype=jnp.int32)[:, None]
     counts = jnp.sum(members.astype(jnp.float32), axis=1)
@@ -265,10 +307,10 @@
         in_specs=[pl.BlockSpec(memory_space=pltpu.SMEM)] + [vmem] * 5 + [anywhere] * (len(layout) + 2),
         out_specs=(anywhere, vmem),
         scratch_shapes=[
-            pltpu.VMEM((cx + 2 * RIM, halves, cy + 2 * LEAD, LANES), jnp.float32),
+            pltpu.VMEM((halves, cx + 4 * RIM, cy + 2 * LEAD, LANES), jnp.float32),
             pltpu.VMEM((cx + 4, halves, wide, LANES), jnp.float32),
             pltpu.VMEM((cx + 4, halves, wide, LANES), jnp.float32),
-            pltpu.VMEM((4, halves, wide, LANES), jnp.float32),
+            pltpu.VMEM((16, halves, wide, LANES), jnp.float32),
             pltpu.VMEM((4, 2, cx * cy, nt), jnp.bfloat16),
             pltpu.VMEM((cx * cy, 2 * nt), jnp.bfloat16),
             pltpu.VMEM((cx * cy, nt), jnp.float32),

time: 47 us -> 41.9 us (0.89)
  starting transfers between devices: 22 us -> 16.7 us
  other arithmetic: 3.67 us -> 5.77 us
  Pallas kernels: 8.94 us -> 7.59 us
  waiting for transfers between devices: 8.45 us -> 7.83 us
    ppermute x3, starting transfers between devices: 7.87 us -> 4.37 us  [reduce_scatter(): lax.ppermute(sent, axis, [(s, s ^ bit) for s in range(count)])]
    ppermute x8, starting transfers between devices: 14.2 us -> 12.3 us  [the longest x6 8.31 us: send(): return lax.ppermute(piece, 'brick', [(s, s ^ d) for s in range(bricks)])]
    ppermute x8, waiting for transfers between devices: 4.23 us -> 2.53 us  [the longest x6 1.68 us: send(): return lax.ppermute(piece, 'brick', [(s, s ^ d) for s in range(bricks)])]
    pallas_call x1, Pallas kernels: 8.94 us -> 7.59 us  [local(): pl.pallas_call(kernel, out_shape=(jax.ShapeDtypeStruct((cx * cy, nt), jnp...]
    ppermute x3, waiting for transfers between devices: 4.23 us -> 5.29 us  [reduce_scatter(): lax.ppermute(sent, axis, [(s, s ^ bit) for s in range(count)])]
    mul x1, other arithmetic: 0.01 us -> 0.7 us  [local(): fault = patch_owner[:, 0] * F_DEV + patch_fault]
    add x1, other arithmetic: 0.01 us -> 0.7 us  [local(): fault = patch_owner[:, 0] * F_DEV + patch_fault]
    convert_element_type x1, other arithmetic: 2.38 us -> 3.07 us  [local(): (patch_trace[:, None] == jnp.arange(cx * cy, dtype=jnp.int32)[None, :]).a...]
  transfers between devices with their start and end apart: 11 -> 11, of which waited for: 6 -> 5; matrix products, arithmetic and copies ran while one was open for 7% -> 16% of each run, Pallas kernels for 0% -> 0%
where the time goes in v3:
time: 41.9 us; the launch traced here: 41.6 us
  starting transfers between devices  16.7 us (40%)
  waiting for transfers between devices  7.83 us (19%)
  Pallas kernels  7.59 us (18%)
  other arithmetic  5.77 us (14%)
  local copies, waits for them, and re-layouts  2.82 us (7%)
  between operations  0.92 us (2%)
    ppermute x6, starting transfers between devices, send(): return lax.ppermute(piece, 'brick', [(s, s ^ d) for s in range(bricks)])  8.31 us
    pallas_call x1, Pallas kernels, local(): pl.pallas_call(kernel, out_shape=(jax.ShapeDtypeStruct((cx * cy, nt), jnp...  7.59 us
    ppermute x3, waiting for transfers between devices, reduce_scatter(): lax.ppermute(sent, axis, [(s, s ^ bit) for s in range(count)])  5.29 us
    ppermute x3, starting transfers between devices, reduce_scatter(): lax.ppermute(sent, axis, [(s, s ^ bit) for s in range(count)])  4.37 us
    ppermute x1, starting transfers between devices, halo_columns(): near = lax.ppermute(near, 'bulk', inner)  3.31 us
    convert_element_type x1, other arithmetic, local(): (patch_trace[:, None] == jnp.arange(cx * cy, dtype=jnp.int32)[None, :]).a...  3.07 us
    dynamic_slice x2, local copies, waits for them, and re-layouts, cut(): return lax.dynamic_slice(source, (first, begin, 0), (rows, columns, nt))  2.33 us
    ppermute x6, waiting for transfers between devices, send(): return lax.ppermute(piece, 'brick', [(s, s ^ d) for s in range(bricks)])  1.68 us
  transfers between devices with their start and end apart: 11, of which 5 were waited for; matrix products, arithmetic and copies ran while one was open for 16% of the time, Pallas kernels for 0%

profile of v3, /device:TPU:0, one launch (start us, length us, event | category | flops | bytes accessed | tf_op | source)
XLA Modules:
  0.0 41.6 jit_solution(16797110069414449140)
XLA Ops:
  0.7 1.0 %constant_dynamic-slice_fusion.8 = f32[22,8,256]{2,1,0:T(8,128)S(1)} fusion(f32[64,16,256]{2,1,0:T(8,128)} %refs_12_.1, s32[]{:T(128)S(6)} %min.17, s32[]{:T(128)S(6)} %mul.32), kind=kLoop, calls=%fused_computation.40 | loop fusion | bytes 360456 | tf_op jit(solution)/shard_map/dynamic_slice | solution.py:215
  1.7 4.0 %collective-permute-start.2 = (f32[22,8,256]{2,1,0:T(8,128)S(1)}, f32[22,8,256]{2,1,0:T(8,128)S(1)}, u32[]{:S(2)}, u32[]{:S(2)}) collective-permute-start(f32[22,8,256]{2,1,0:T(8,128)S(1)} %constant_dynamic-slice_fusion.8), channel_id=1, source_target_pairs={{0,24},{8,16},{16,8},{24,0},{1,25},{9,17},{17,9},{25,1},{2,26},{10... | collective-permute-start | bytes 540680 | tf_op jit(solution)/shard_map/ppermute | solution.py:218
  5.7 1.3 %constant_dynamic-slice_fusion.3 = (f32[22,8,256]{2,1,0:T(8,128)S(1)}, f32[22,8,256]{2,1,0:T(8,128)S(1)}, f32[22,8,256]{2,1,0:T(8,128)S(1)}, f32[22,8,256]{2,1,0:T(8,128)S(1)}, f32[22,8,256]{2,1,0:T(8,128)S(1)}) fusion(f32[64,16,256]{2,1,0:T(8,128)} %refs_12_.1, s32[]{:T(128)S(6)} %min.18, s32[]{:T(128)S(6)} %select_n.143, s32[]{:T(128)S(6)} %min.19, ...), kind=kLoop, calls=%fused_computation.35 | loop fusion | bytes 1802260 | tf_op jit(solution)/shard_map/dynamic_slice | solution.py:215
  7.0 0.6 %collective-permute-start.1 = (f32[22,8,256]{2,1,0:T(8,128)S(1)}, f32[22,8,256]{2,1,0:T(8,128)S(1)}, u32[]{:S(2)}, u32[]{:S(2)}) collective-permute-start(f32[22,8,256]{2,1,0:T(8,128)S(1)} %get-tuple-element.27), channel_id=1, source_target_pairs={{0,8},{8,0},{16,24},{24,16},{1,9},{9,1},{17,25},{25,17},{2,10},{10... | collective-permute-start | bytes 540680 | tf_op jit(solution)/shard_map/ppermute | solution.py:218
  7.7 0.7 %broadcast_multiply_fusion = s32[2048,1]{0,1:T(1,128)S(1)} fusion(s32[2048,1]{0,1:T(1,128)} %param.6), kind=kLoop, calls=%fused_computation.31 | loop fusion | flops 2048 | bytes 16384 | tf_op jit(solution)/shard_map/mul | solution.py:286
  8.4 0.7 %add.72 = s32[2048]{0:T(1024)S(1)} add(s32[2048]{0:T(1024)S(1)} %bitcast.26, s32[2048]{0:T(1024)} %param.7) | non-fusion elementwise | flops 2048 | bytes 24576 | tf_op jit(solution)/shard_map/add | solution.py:286
  9.2 3.1 %fusion.refs_13_ = bf16[2048,1024]{1,0:T(8,128)(2,1)} fusion(s32[2048]{0:T(1024)} %param.8), kind=kLoop, calls=%fused_computation.1 | loop fusion | flops 4194304 | bytes 4202496 | tf_op jit(solution)/shard_map/convert_element_type | solution.py:285
  12.2 0.2 convert_reduce_fusion
  12.6 2.9 %collective-permute-start.5 = (f32[22,8,256]{2,1,0:T(8,128)S(1)}, f32[22,8,256]{2,1,0:T(8,128)S(1)}, u32[]{:S(2)}, u32[]{:S(2)}) collective-permute-start(f32[22,8,256]{2,1,0:T(8,128)S(1)} %get-tuple-element.16), channel_id=1, source_target_pairs={{0,24},{8,16},{16,8},{24,0},{1,25},{9,17},{17,9},{25,1},{2,26},{10... | collective-permute-start | bytes 540680 | tf_op jit(solution)/shard_map/ppermute | solution.py:218
  15.6 0.5 %collective-permute-start.6 = (f32[22,8,256]{2,1,0:T(8,128)S(1)}, f32[22,8,256]{2,1,0:T(8,128)S(1)}, u32[]{:S(2)}, u32[]{:S(2)}) collective-permute-start(f32[22,8,256]{2,1,0:T(8,128)S(1)} %get-tuple-element.17), channel_id=1, source_target_pairs={{0,8},{8,0},{16,24},{24,16},{1,9},{9,1},{17,25},{25,17},{2,10},{10... | collective-permute-start | bytes 540680 | tf_op jit(solution)/shard_map/ppermute | solution.py:218
  16.1 0.2 collective-permute-start.7
  16.3 0.1 fusion.8
  16.4 0.3 broadcast_in_dim.8.refs_14_
  16.8 0.7 %collective-permute-start.4 = (f32[22,3,256]{2,1,0:T(4,128)S(1)}, f32[22,3,256]{2,1,0:T(4,128)S(1)}, u32[]{:S(2)}, u32[]{:S(2)}) collective-permute-start(f32[22,3,256]{2,1,0:T(4,128)S(1)} %get-tuple-element.29), channel_id=1, source_target_pairs={{1,2},{2,1},{3,4},{4,3},{5,6},{6,5},{9,10},{10,9},{11,12},{12,11},... | collective-permute-start | bytes 202760 | tf_op jit(solution)/shard_map/ppermute | solution.py:254
  17.5 3.3 %collective-permute-start.3 = (f32[22,3,256]{2,1,0:T(4,128)S(1)}, f32[22,3,256]{2,1,0:T(4,128)S(1)}, u32[]{:S(2)}, u32[]{:S(2)}) collective-permute-start(f32[22,3,256]{2,1,0:T(4,128)S(1)} %get-tuple-element.30), channel_id=1, source_target_pairs={{0,1},{1,0},{2,3},{3,2},{4,5},{5,4},{6,7},{7,6},{8,9},{9,8},{10,11... | collective-permute-start | bytes 202760 | tf_op jit(solution)/shard_map/ppermute | solution.py:255
  20.9 0.9 %collective-permute-done.3.refs_1_ = f32[22,3,256]{2,1,0:T(4,128)S(1)} collective-permute-done((f32[22,3,256]{2,1,0:T(4,128)S(1)}, f32[22,3,256]{2,1,0:T(4,128)S(1)}, u32[]{:S(2)}, u32[]{:S(2)}) %collective-permute-start.3) | collective-permute-done | bytes 67616 | tf_op jit(solution)/shard_map/ppermute | solution.py:255
  21.7 1.7 %collective-permute-done.6.refs_10_ = f32[22,8,256]{2,1,0:T(8,128)S(1)} collective-permute-done((f32[22,8,256]{2,1,0:T(8,128)S(1)}, f32[22,8,256]{2,1,0:T(8,128)S(1)}, u32[]{:S(2)}, u32[]{:S(2)}) %collective-permute-start.6) | collective-permute-done | bytes 180256 | tf_op jit(solution)/shard_map/ppermute | solution.py:218
  23.4 7.6 %brick_attribute.1 = (f32[1024,256]{1,0:T(8,128)}, f32[128,128]{1,0:T(8,128)S(1)}) custom-call(s32[4]{0:T(128)S(1)} %pad_add_fusion.refs_0_, f32[22,3,256]{2,1,0:T(4,128)S(1)} %collective-permute-done.3.refs_1_, f32[22,3,256]{2,1,0:T(4,128)S(1)} %collective-permute-done.4.refs_2_, bf16[256,256]{1,0:T(8,128)(2,1)S(1)} %get-tuple-element.35.refs_3_, ...), custom_call_target="tpu_custom_call" | custom-call | flops 2500000000 | bytes 10000000 | tf_op jit(solution)/shard_map/brick_attribute/pallas_call | solution.py:301
  31.2 1.2 %collective-permute-done.8 = f32[4,17,128]{2,0,1:T(4,128)S(1)} collective-permute-done((f32[4,17,128]{2,0,1:T(4,128)S(1)}, f32[4,17,128]{2,0,1:T(4,128)S(1)}, u32[]{:S(2)}, u32[]{:S(2)}) %collective-permute-start.8) | collective-permute-done | bytes 34848 | tf_op jit(solution)/shard_map/ppermute | solution.py:269
  32.4 1.6 %collective-permute-start.9 = (f32[2,17,128]{2,0,1:T(2,128)S(1)}, f32[2,17,128]{2,0,1:T(2,128)S(1)}, u32[]{:S(2)}, u32[]{:S(2)}) collective-permute-start(f32[2,17,128]{2,0,1:T(2,128)S(1)} %bitcast.28), channel_id=1, source_target_pairs={{0,2},{1,3},{2,0},{3,1},{4,6},{5,7},{6,4},{7,5},{8,10},{9,11},{10,... | collective-permute-start | bytes 52232 | tf_op jit(solution)/shard_map/ppermute | solution.py:269
  34.0 2.2 %collective-permute-done.9 = f32[2,17,128]{2,0,1:T(2,128)S(1)} collective-permute-done((f32[2,17,128]{2,0,1:T(2,128)S(1)}, f32[2,17,128]{2,0,1:T(2,128)S(1)}, u32[]{:S(2)}, u32[]{:S(2)}) %collective-permute-start.9) | collective-permute-done | bytes 17440 | tf_op jit(solution)/shard_map/ppermute | solution.py:269
  36.2 2.7 %collective-permute-start.10 = (f32[1,17,128]{2,0,1:T(1,128)S(1)}, f32[1,17,128]{2,0,1:T(1,128)S(1)}, u32[]{:S(2)}, u32[]{:S(2)}) collective-permute-start(f32[1,17,128]{2,0,1:T(1,128)S(1)} %constant_dynamic-slice_fusion), channel_id=1, source_target_pairs={{0,4},{1,5},{2,6},{3,7},{4,0},{5,1},{6,2},{7,3},{8,12},{9,13},{10,... | collective-permute-start | bytes 26120 | tf_op jit(solution)/shard_map/ppermute | solution.py:269
  38.9 2.0 %collective-permute-done.10 = f32[1,17,128]{2,0,1:T(1,128)S(1)} collective-permute-done((f32[1,17,128]{2,0,1:T(1,128)S(1)}, f32[1,17,128]{2,0,1:T(1,128)S(1)}, u32[]{:S(2)}, u32[]{:S(2)}) %collective-permute-start.10) | collective-permute-done | bytes 8736 | tf_op jit(solution)/shard_map/ppermute | solution.py:269
  40.9 0.7 %broadcast_divide_fusion = f32[16,128]{1,0:T(8,128)} fusion(f32[16,128]{1,0:T(8,128)S(1)} %bitcast.27, f32[16]{0:T(128)S(1)} %fusion.14), kind=kLoop, calls=%fused_computation.30 | loop fusion | flops 2048 | bytes 16448 | tf_op jit(solution)/shard_map/div | solution.py:330
  (28 shorter events, 0.7 us)
Async XLA Ops:
  0.6 15.7 %copy-start = (f32[64,16,256]{2,1,0:T(8,128)S(1)}, f32[64,16,256]{2,1,0:T(8,128)}, u32[]{:S(2)}) copy-start(f32[64,16,256]{2,1,0:T(8,128)} %refs_12_.1) | copy-start | bytes 3145732
  0.6 15.8 %copy-start.1 = (s32[2048]{0:T(1024)S(1)}, s32[2048]{0:T(1024)}, u32[]{:S(2)}) copy-start(s32[2048]{0:T(1024)} %param.9) | copy-start | bytes 24580
  1.7 10.9 %collective-permute-start.2 = (f32[22,8,256]{2,1,0:T(8,128)S(1)}, f32[22,8,256]{2,1,0:T(8,128)S(1)}, u32[]{:S(2)}, u32[]{:S(2)}) collective-permute-start(f32[22,8,256]{2,1,0:T(8,128)S(1)} %constant_dynamic-slice_fusion.8), channel_id=1, source_target_pairs={{0,24},{8,16},{16,8},{24,0},{1,25},{9,17},{17,9},{25,1},{2,26},{10... | collective-permute-start | bytes 540680 | tf_op jit(solution)/shard_map/ppermute | solution.py:218
  7.0 8.6 %collective-permute-start.1 = (f32[22,8,256]{2,1,0:T(8,128)S(1)}, f32[22,8,256]{2,1,0:T(8,128)S(1)}, u32[]{:S(2)}, u32[]{:S(2)}) collective-permute-start(f32[22,8,256]{2,1,0:T(8,128)S(1)} %get-tuple-element.27), channel_id=1, source_target_pairs={{0,8},{8,0},{16,24},{24,16},{1,9},{9,1},{17,25},{25,17},{2,10},{10... | collective-permute-start | bytes 540680 | tf_op jit(solution)/shard_map/ppermute | solution.py:218
  7.6 8.5 %collective-permute-start = (f32[22,8,256]{2,1,0:T(8,128)S(1)}, f32[22,8,256]{2,1,0:T(8,128)S(1)}, u32[]{:S(2)}, u32[]{:S(2)}) collective-permute-start(f32[22,8,256]{2,1,0:T(8,128)S(1)} %get-tuple-element.28), channel_id=1, source_target_pairs={{0,16},{8,24},{16,0},{24,8},{1,17},{9,25},{17,1},{25,9},{2,18},{10... | collective-permute-start | bytes 540680 | tf_op jit(solution)/shard_map/ppermute | solution.py:218
  12.6 9.1 %collective-permute-start.5 = (f32[22,8,256]{2,1,0:T(8,128)S(1)}, f32[22,8,256]{2,1,0:T(8,128)S(1)}, u32[]{:S(2)}, u32[]{:S(2)}) collective-permute-start(f32[22,8,256]{2,1,0:T(8,128)S(1)} %get-tuple-element.16), channel_id=1, source_target_pairs={{0,24},{8,16},{16,8},{24,0},{1,25},{9,17},{17,9},{25,1},{2,26},{10... | collective-permute-start | bytes 540680 | tf_op jit(solution)/shard_map/ppermute | solution.py:218
  15.6 7.8 %collective-permute-start.6 = (f32[22,8,256]{2,1,0:T(8,128)S(1)}, f32[22,8,256]{2,1,0:T(8,128)S(1)}, u32[]{:S(2)}, u32[]{:S(2)}) collective-permute-start(f32[22,8,256]{2,1,0:T(8,128)S(1)} %get-tuple-element.17), channel_id=1, source_target_pairs={{0,8},{8,0},{16,24},{24,16},{1,9},{9,1},{17,25},{25,17},{2,10},{10... | collective-permute-start | bytes 540680 | tf_op jit(solution)/shard_map/ppermute | solution.py:218
  16.1 7.3 %collective-permute-start.7 = (f32[22,8,256]{2,1,0:T(8,128)S(1)}, f32[22,8,256]{2,1,0:T(8,128)S(1)}, u32[]{:S(2)}, u32[]{:S(2)}) collective-permute-start(f32[22,8,256]{2,1,0:T(8,128)S(1)} %get-tuple-element.18), channel_id=1, source_target_pairs={{0,16},{8,24},{16,0},{24,8},{1,17},{9,25},{17,1},{25,9},{2,18},{10... | collective-permute-start | bytes 540680 | tf_op jit(solution)/shard_map/ppermute | solution.py:218
  16.8 4.1 %collective-permute-start.4 = (f32[22,3,256]{2,1,0:T(4,128)S(1)}, f32[22,3,256]{2,1,0:T(4,128)S(1)}, u32[]{:S(2)}, u32[]{:S(2)}) collective-permute-start(f32[22,3,256]{2,1,0:T(4,128)S(1)} %get-tuple-element.29), channel_id=1, source_target_pairs={{1,2},{2,1},{3,4},{4,3},{5,6},{6,5},{9,10},{10,9},{11,12},{12,11},... | collective-permute-start | bytes 202760 | tf_op jit(solution)/shard_map/ppermute | solution.py:254
  17.5 4.2 %collective-permute-start.3 = (f32[22,3,256]{2,1,0:T(4,128)S(1)}, f32[22,3,256]{2,1,0:T(4,128)S(1)}, u32[]{:S(2)}, u32[]{:S(2)}) collective-permute-start(f32[22,3,256]{2,1,0:T(4,128)S(1)} %get-tuple-element.30), channel_id=1, source_target_pairs={{0,1},{1,0},{2,3},{3,2},{4,5},{5,4},{6,7},{7,6},{8,9},{9,8},{10,11... | collective-permute-start | bytes 202760 | tf_op jit(solution)/shard_map/ppermute | solution.py:255
  31.0 1.3 %collective-permute-start.8 = (f32[4,17,128]{2,0,1:T(4,128)S(1)}, f32[4,17,128]{2,0,1:T(4,128)S(1)}, u32[]{:S(2)}, u32[]{:S(2)}) collective-permute-start(f32[4,17,128]{2,0,1:T(4,128)S(1)} %bitcast.25), channel_id=1, source_target_pairs={{0,1},{1,0},{2,3},{3,2},{4,5},{5,4},{6,7},{7,6},{8,9},{9,8},{10,11... | collective-permute-start | bytes 104456 | tf_op jit(solution)/shard_map/ppermute | solution.py:269
  32.4 3.8 %collective-permute-start.9 = (f32[2,17,128]{2,0,1:T(2,128)S(1)}, f32[2,17,128]{2,0,1:T(2,128)S(1)}, u32[]{:S(2)}, u32[]{:S(2)}) collective-permute-start(f32[2,17,128]{2,0,1:T(2,128)S(1)} %bitcast.28), channel_id=1, source_target_pairs={{0,2},{1,3},{2,0},{3,1},{4,6},{5,7},{6,4},{7,5},{8,10},{9,11},{10,... | collective-permute-start | bytes 52232 | tf_op jit(solution)/shard_map/ppermute | solution.py:269
  36.2 4.6 %collective-permute-start.10 = (f32[1,17,128]{2,0,1:T(1,128)S(1)}, f32[1,17,128]{2,0,1:T(1,128)S(1)}, u32[]{:S(2)}, u32[]{:S(2)}) collective-permute-start(f32[1,17,128]{2,0,1:T(1,128)S(1)} %constant_dynamic-slice_fusion), channel_id=1, source_target_pairs={{0,4},{1,5},{2,6},{3,7},{4,0},{5,1},{6,2},{7,3},{8,12},{9,13},{10,... | collective-permute-start | bytes 26120 | tf_op jit(solution)/shard_map/ppermute | solution.py:269

commit v4 on v3

--- a/solution.py
+++ b/solution.py
@@ -10,6 +10,8 @@
 RIM = 3
 LEAD = 8
 LANES = 128
+TIES = (0, 0, 0)
+WHICH = 2
 TILE_M = 1024
 BLOCK = 256
 
@@ -29,8 +31,8 @@
     where_ref, low_ref, high_ref, band5_ref, band9_ref, faults_ref, *refs,
 ):
     pieces = refs[:len(layout)]
-    picks_hbm, offsets_hbm, attr_hbm, partial_ref = refs[len(layout):len(layout) + 4]
-    amp, exy, ett, box, fields, rows_bf, attr, picks, offsets, windows, sems = refs[len(layout) + 4:]
+    places_hbm, attr_hbm, partial_ref = refs[len(layout):len(layout) + 3]
+    amp, exy, ett, box, fields, rows_bf, attr, places, windows, sems = refs[len(layout) + 3:]
     halves = nt // LANES
     brick, slab, bricks, slabs = where_ref[0], where_ref[1], where_ref[2], where_ref[3]
     wide = cy + 8
@@ -49,12 +51,10 @@
                 sems.at[n * halves + h],
             ))
     base = len(layout) * halves
-    fetch_picks = pltpu.make_async_copy(picks_hbm, picks, sems.at[base])
-    fetch_offsets = pltpu.make_async_copy(offsets_hbm, offsets, sems.at[base + 1])
+    fetch_places = pltpu.make_async_copy(places_hbm, places, sems.at[base])
     for copy in fetches:
         copy.start()
-    fetch_picks.start()
-    fetch_offsets.start()
+    fetch_places.start()
     even = lax.rem(slab, 2) == 0
     for h in range(halves):
         lanes = pl.ds(h * LANES, LANES)
@@ -162,19 +162,22 @@
         return carry
 
     lax.fori_loop(0, cx * cy // tile, finish_tile, 0)
-    store = pltpu.make_async_copy(attr, attr_hbm, sems.at[base + 2])
+    store = pltpu.make_async_copy(attr, attr_hbm, sems.at[base + 1])
     store.start()
 
-    fetch_picks.wait()
-    fetch_offsets.wait()
+    fetch_places.wait()
     block = BLOCK
     lane_block = lax.broadcasted_iota(jnp.int32, (block, LANES), 1)
 
     def window_block(j, carry):
         at = pl.ds(pl.multiple_of(j * block, block), block)
-        chosen = dot(picks[at, :], rows_bf[...])
+        place = places[at, :]
+        trace = lax.shift_right_logical(place, nt.bit_length() - 1)
+        chosen = dot(jnp.concatenate([
+            (lane_block + k == trace).astype(jnp.float32).astype(jnp.bfloat16)
+            for k in range(0, cx * cy, LANES)], axis=1), rows_bf[...])
         rows = chosen[:, 0:nt] + chosen[:, nt:2 * nt]
-        shift = offsets[at, :]
+        shift = place - trace * nt
         mixed = jnp.where(lane_block < shift, rows[:, LANES:nt], rows[:, 0:LANES])
         window = jnp.take_along_axis(mixed, (lane_block + shift) & (LANES - 1), axis=1)
         high, low = split_bf16(window)
@@ -201,7 +204,7 @@
     return upper if part == 0 else 1 - upper
 
 
-def exchange_bricks(amp, cx):
+def exchange_bricks(amp, cx, prepared):
     bricks = lax.axis_size("brick")
     mine = lax.axis_index("brick")
     nx, strip, nt = amp.shape
@@ -223,14 +226,17 @@
         for n, d in enumerate(order):
             piece = cut(source, d, begin, width)
             if part == 1:
-                piece, _ = lax.optimization_barrier((piece, pieces[n]))
+                if n == WHICH:
+                    piece, _, prepared = lax.optimization_barrier((piece, pieces[TIES[n]], prepared))
+                else:
+                    piece, _ = lax.optimization_barrier((piece, pieces[TIES[n]]))
             elif n == 0:
                 source, piece = lax.optimization_barrier((amp, piece))
             pieces.append(send(piece, d))
             layout.append((d, part, width))
     pieces.append(amp)
     layout.append((0, None, strip))
-    return pieces, layout
+    return pieces, layout, prepared
 
 
 def halo_columns(pieces, layout, cx, prepared):
@@ -278,11 +284,10 @@
     patches = patch_fault.shape[0]
     faults = slabs * F_DEV
 
-    pieces, layout = exchange_bricks(amp_traces, cx)
-    offsets = jnp.broadcast_to(patch_offset[:, None], (patches, LANES))
-    low, high, (offsets,) = halo_columns(pieces, layout, cx, (offsets,))
-
-    picks = (patch_trace[:, None] == jnp.arange(cx * cy, dtype=jnp.int32)[None, :]).astype(jnp.bfloat16)
+    places = jnp.broadcast_to((patch_trace * nt + patch_offset)[:, None], (patches, LANES))
+    pieces, layout, places = exchange_bricks(amp_traces, cx, places)
+    low, high, _ = halo_columns(pieces, layout, cx, ())
+
     fault = patch_owner[:, 0] * F_DEV + patch_fault
     members = fault[None, :] == jnp.arange(faults, dtype=jnp.int32)[:, None]
     counts = jnp.sum(members.astype(jnp.float32), axis=1)
@@ -304,7 +309,7 @@
             jax.ShapeDtypeStruct((cx * cy, nt), jnp.float32),
             jax.ShapeDtypeStruct((faults, PATCH), jnp.float32),
         ),
-        in_specs=[pl.BlockSpec(memory_space=pltpu.SMEM)] + [vmem] * 5 + [anywhere] * (len(layout) + 2),
+        in_specs=[pl.BlockSpec(memory_space=pltpu.SMEM)] + [vmem] * 5 + [anywhere] * (len(layout) + 1),
         out_specs=(anywhere, vmem),
         scratch_shapes=[
             pltpu.VMEM((halves, cx + 4 * RIM, cy + 2 * LEAD, LANES), jnp.float32),
@@ -314,15 +319,14 @@
             pltpu.VMEM((4, 2, cx * cy, nt), jnp.bfloat16),
             pltpu.VMEM((cx * cy, 2 * nt), jnp.bfloat16),
             pltpu.VMEM((cx * cy, nt), jnp.float32),
-            pltpu.VMEM((patches, cx * cy), jnp.bfloat16),
             pltpu.VMEM((patches, LANES), jnp.int32),
             pltpu.VMEM((patches, 2 * PATCH), jnp.bfloat16),
-            pltpu.SemaphoreType.DMA((len(layout) * halves + 3,)),
+            pltpu.SemaphoreType.DMA((len(layout) * halves + 2,)),
         ],
         compiler_params=pltpu.CompilerParams(vmem_limit_bytes=48 * 1024 * 1024),
         cost_estimate=pl.CostEstimate(flops=2_500_000_000, bytes_accessed=10_000_000, transcendentals=0),
         name="brick_attribute",
-    )(where, low, high, band(nt, 2), band(nt, 4), members, *pieces, picks, offsets)
+    )(where, low, high, band(nt, 2), band(nt, 4), members, *pieces, places)
 
     tally = jnp.pad(counts.reshape(slabs, 1, F_DEV), ((0, 0), (0, 0), (0, PATCH - F_DEV)))
     parts = jnp.concatenate([partial.reshape(slabs, F_DEV, PATCH), tally], axis=1)

time: 41.9 us -> 41.6 us (level)
  other arithmetic: 5.77 us -> 1.32 us
  starting transfers between devices: 16.7 us -> 19.2 us
  local copies, waits for them, and re-layouts: 2.82 us -> 4.75 us
  waiting for transfers between devices: 7.83 us -> 7.34 us
    convert_element_type x1 -> x0, other arithmetic: 3.07 us -> none  [local(): (patch_trace[:, None] == jnp.arange(cx * cy, dtype=jnp.int32)[None, :]).a...]
    unnamed x5 -> x11, local copies, waits for them, and re-layouts: 0.01 us -> 1.95 us
    ppermute x3, starting transfers between devices: 4.37 us -> 5.87 us  [reduce_scatter(): lax.ppermute(sent, axis, [(s, s ^ bit) for s in range(count)])]
    ppermute x6, starting transfers between devices: 8.31 us -> 9.65 us  [send(): return lax.ppermute(piece, 'brick', [(s, s ^ d) for s in range(bricks)])]
    ppermute x3, waiting for transfers between devices: 5.29 us -> 4.28 us  [reduce_scatter(): lax.ppermute(sent, axis, [(s, s ^ bit) for s in range(count)])]
    mul x1, other arithmetic: 0.7 us -> 0.01 us  [local(): fault = patch_owner[:, 0] * F_DEV + patch_fault]
    add x1, other arithmetic: 0.7 us -> 0.01 us  [local(): fault = patch_owner[:, 0] * F_DEV + patch_fault]
    ppermute x6, waiting for transfers between devices: 1.68 us -> 2.2 us  [send(): return lax.ppermute(piece, 'brick', [(s, s ^ d) for s in range(bricks)])]
  transfers between devices with their start and end apart: 11 -> 11, of which waited for: 5 -> 8; matrix products, arithmetic and copies ran while one was open for 16% -> 6% of each run, Pallas kernels for 0% -> 0%
where the time goes in v4:
time: 41.6 us; the launch traced here: 41.2 us
  starting transfers between devices  19.2 us (46%)
  Pallas kernels  7.84 us (19%)
  waiting for transfers between devices  7.34 us (18%)
  local copies, waits for them, and re-layouts  4.75 us (11%)
  other arithmetic  1.32 us (3%)
  between operations  0.82 us (2%)
    ppermute x6, starting transfers between devices, send(): return lax.ppermute(piece, 'brick', [(s, s ^ d) for s in range(bricks)])  9.65 us
    pallas_call x1, Pallas kernels, local(): pl.pallas_call(kernel, out_shape=(jax.ShapeDtypeStruct((cx * cy, nt), jnp...  7.84 us
    ppermute x3, starting transfers between devices, reduce_scatter(): lax.ppermute(sent, axis, [(s, s ^ bit) for s in range(count)])  5.87 us
    ppermute x3, waiting for transfers between devices, reduce_scatter(): lax.ppermute(sent, axis, [(s, s ^ bit) for s in range(count)])  4.28 us
    ppermute x1, starting transfers between devices, halo_columns(): near = lax.ppermute(near, 'bulk', inner)  3 us
    dynamic_slice x2, local copies, waits for them, and re-layouts, cut(): return lax.dynamic_slice(source, (first, begin, 0), (rows, columns, nt))  2.33 us
    ppermute x6, waiting for transfers between devices, send(): return lax.ppermute(piece, 'brick', [(s, s ^ d) for s in range(bricks)])  2.2 us
    unnamed x11, local copies, waits for them, and re-layouts  1.95 us
  transfers between devices with their start and end apart: 11, of which 8 were waited for; matrix products, arithmetic and copies ran while one was open for 6% of the time, Pallas kernels for 0%

profile of v4, /device:TPU:0, one launch (start us, length us, event | category | flops | bytes accessed | tf_op | source)
XLA Modules:
  0.0 41.2 jit_solution(12893015900649498698)
XLA Ops:
  0.6 0.9 %constant_dynamic-slice_fusion.8 = f32[22,8,256]{2,1,0:T(8,128)S(1)} fusion(f32[64,16,256]{2,1,0:T(8,128)} %refs_12_.1, s32[]{:T(128)S(6)} %min.17, s32[]{:T(128)S(6)} %mul.38), kind=kLoop, calls=%fused_computation.39 | loop fusion | bytes 360456 | tf_op jit(solution)/shard_map/dynamic_slice | solution.py:218
  1.6 4.0 %collective-permute-start.2 = (f32[22,8,256]{2,1,0:T(8,128)S(1)}, f32[22,8,256]{2,1,0:T(8,128)S(1)}, u32[]{:S(2)}, u32[]{:S(2)}) collective-permute-start(f32[22,8,256]{2,1,0:T(8,128)S(1)} %constant_dynamic-slice_fusion.8), channel_id=1, source_target_pairs={{0,24},{8,16},{16,8},{24,0},{1,25},{9,17},{17,9},{25,1},{2,26},{10... | collective-permute-start | bytes 540680 | tf_op jit(solution)/shard_map/ppermute | solution.py:221
  5.6 1.4 %constant_dynamic-slice_fusion.3 = (f32[22,8,256]{2,1,0:T(8,128)S(1)}, f32[22,8,256]{2,1,0:T(8,128)S(1)}, f32[22,8,256]{2,1,0:T(8,128)S(1)}, f32[22,8,256]{2,1,0:T(8,128)S(1)}, f32[22,8,256]{2,1,0:T(8,128)S(1)}) fusion(f32[64,16,256]{2,1,0:T(8,128)} %refs_12_.1, s32[]{:T(128)S(6)} %min.18, s32[]{:T(128)S(6)} %select_n.143, s32[]{:T(128)S(6)} %min.19, ...), kind=kLoop, calls=%fused_computation.34 | loop fusion | bytes 1802260 | tf_op jit(solution)/shard_map/dynamic_slice | solution.py:218
  7.0 0.6 %collective-permute-start.1 = (f32[22,8,256]{2,1,0:T(8,128)S(1)}, f32[22,8,256]{2,1,0:T(8,128)S(1)}, u32[]{:S(2)}, u32[]{:S(2)}) collective-permute-start(f32[22,8,256]{2,1,0:T(8,128)S(1)} %get-tuple-element.27), channel_id=1, source_target_pairs={{0,8},{8,0},{16,24},{24,16},{1,9},{9,1},{17,25},{25,17},{2,10},{10... | collective-permute-start | bytes 540680 | tf_op jit(solution)/shard_map/ppermute | solution.py:221
  7.7 0.6 %copy-done.4 = s32[2048,1]{0,1:T(1,128)S(1)} copy-done((s32[2048,1]{0,1:T(1,128)S(1)}, s32[2048,1]{0,1:T(1,128)}, u32[]{:S(2)}) %copy-start.4) | copy-done | bytes 8216
  8.3 0.7 %copy-done.1 = s32[2048]{0:T(1024)S(1)} copy-done((s32[2048]{0:T(1024)S(1)}, s32[2048]{0:T(1024)}, u32[]{:S(2)}) %copy-start.1) | copy-done | bytes 8216
  9.5 0.6 %copy-done.2 = s32[2048]{0:T(1024)S(1)} copy-done((s32[2048]{0:T(1024)S(1)}, s32[2048]{0:T(1024)}, u32[]{:S(2)}) %copy-start.2) | copy-done | bytes 8216
  10.1 0.9 %collective-permute-done.2.refs_6_ = f32[22,8,256]{2,1,0:T(8,128)S(1)} collective-permute-done((f32[22,8,256]{2,1,0:T(8,128)S(1)}, f32[22,8,256]{2,1,0:T(8,128)S(1)}, u32[]{:S(2)}, u32[]{:S(2)}) %collective-permute-start.2) | collective-permute-done | bytes 180256 | tf_op jit(solution)/shard_map/ppermute | solution.py:221
  10.9 3.0 %collective-permute-start.5 = (f32[22,8,256]{2,1,0:T(8,128)S(1)}, f32[22,8,256]{2,1,0:T(8,128)S(1)}, u32[]{:S(2)}, u32[]{:S(2)}) collective-permute-start(f32[22,8,256]{2,1,0:T(8,128)S(1)} %get-tuple-element.16), channel_id=1, source_target_pairs={{0,24},{8,16},{16,8},{24,0},{1,25},{9,17},{17,9},{25,1},{2,26},{10... | collective-permute-start | bytes 540680 | tf_op jit(solution)/shard_map/ppermute | solution.py:221
  13.9 0.5 %collective-permute-start.6 = (f32[22,8,256]{2,1,0:T(8,128)S(1)}, f32[22,8,256]{2,1,0:T(8,128)S(1)}, u32[]{:S(2)}, u32[]{:S(2)}) collective-permute-start(f32[22,8,256]{2,1,0:T(8,128)S(1)} %get-tuple-element.17), channel_id=1, source_target_pairs={{0,8},{8,0},{16,24},{24,16},{1,9},{9,1},{17,25},{25,17},{2,10},{10... | collective-permute-start | bytes 540680 | tf_op jit(solution)/shard_map/ppermute | solution.py:221
  14.4 0.8 %collective-permute-done.1.refs_7_ = f32[22,8,256]{2,1,0:T(8,128)S(1)} collective-permute-done((f32[22,8,256]{2,1,0:T(8,128)S(1)}, f32[22,8,256]{2,1,0:T(8,128)S(1)}, u32[]{:S(2)}, u32[]{:S(2)}) %collective-permute-start.1) | collective-permute-done | bytes 180256 | tf_op jit(solution)/shard_map/ppermute | solution.py:221
  15.7 1.5 %collective-permute-start.7 = (f32[22,8,256]{2,1,0:T(8,128)S(1)}, f32[22,8,256]{2,1,0:T(8,128)S(1)}, u32[]{:S(2)}, u32[]{:S(2)}) collective-permute-start(f32[22,8,256]{2,1,0:T(8,128)S(1)} %get-tuple-element.18), channel_id=1, source_target_pairs={{0,16},{8,24},{16,0},{24,8},{1,17},{9,25},{17,1},{25,9},{2,18},{10... | collective-permute-start | bytes 540680 | tf_op jit(solution)/shard_map/ppermute | solution.py:221
  17.3 0.7 %collective-permute-start.4 = (f32[22,3,256]{2,1,0:T(4,128)S(1)}, f32[22,3,256]{2,1,0:T(4,128)S(1)}, u32[]{:S(2)}, u32[]{:S(2)}) collective-permute-start(f32[22,3,256]{2,1,0:T(4,128)S(1)} %get-tuple-element.29), channel_id=1, source_target_pairs={{1,2},{2,1},{3,4},{4,3},{5,6},{6,5},{9,10},{10,9},{11,12},{12,11},... | collective-permute-start | bytes 202760 | tf_op jit(solution)/shard_map/ppermute | solution.py:260
  17.9 3.0 %collective-permute-start.3 = (f32[22,3,256]{2,1,0:T(4,128)S(1)}, f32[22,3,256]{2,1,0:T(4,128)S(1)}, u32[]{:S(2)}, u32[]{:S(2)}) collective-permute-start(f32[22,3,256]{2,1,0:T(4,128)S(1)} %get-tuple-element.30), channel_id=1, source_target_pairs={{0,1},{1,0},{2,3},{3,2},{4,5},{5,4},{6,7},{7,6},{8,9},{9,8},{10,11... | collective-permute-start | bytes 202760 | tf_op jit(solution)/shard_map/ppermute | solution.py:261
  21.0 0.9 %collective-permute-done.3.refs_1_ = f32[22,3,256]{2,1,0:T(4,128)S(1)} collective-permute-done((f32[22,3,256]{2,1,0:T(4,128)S(1)}, f32[22,3,256]{2,1,0:T(4,128)S(1)}, u32[]{:S(2)}, u32[]{:S(2)}) %collective-permute-start.3) | collective-permute-done | bytes 67616 | tf_op jit(solution)/shard_map/ppermute | solution.py:261
  21.9 0.4 %collective-permute-done.7.refs_11_ = f32[22,8,256]{2,1,0:T(8,128)S(1)} collective-permute-done((f32[22,8,256]{2,1,0:T(8,128)S(1)}, f32[22,8,256]{2,1,0:T(8,128)S(1)}, u32[]{:S(2)}, u32[]{:S(2)}) %collective-permute-start.7) | collective-permute-done | bytes 180256 | tf_op jit(solution)/shard_map/ppermute | solution.py:221
  22.4 7.8 %brick_attribute.1 = (f32[1024,256]{1,0:T(8,128)}, f32[128,128]{1,0:T(8,128)S(1)}) custom-call(s32[4]{0:T(128)S(1)} %pad_add_fusion.refs_0_, f32[22,3,256]{2,1,0:T(4,128)S(1)} %collective-permute-done.3.refs_1_, f32[22,3,256]{2,1,0:T(4,128)S(1)} %collective-permute-done.4.refs_2_, bf16[256,256]{1,0:T(8,128)(2,1)S(1)} %get-tuple-element.35.refs_3_, ...), custom_call_target="tpu_custom_call" | custom-call | flops 2500000000 | bytes 10000000 | tf_op jit(solution)/shard_map/brick_attribute/pallas_call | solution.py:306
  30.3 0.8 %collective-permute-start.8 = (f32[4,17,128]{2,0,1:T(4,128)S(1)}, f32[4,17,128]{2,0,1:T(4,128)S(1)}, u32[]{:S(2)}, u32[]{:S(2)}) collective-permute-start(f32[4,17,128]{2,0,1:T(4,128)S(1)} %bitcast.25), channel_id=1, source_target_pairs={{0,1},{1,0},{2,3},{3,2},{4,5},{5,4},{6,7},{7,6},{8,9},{9,8},{10,11... | collective-permute-start | bytes 104456 | tf_op jit(solution)/shard_map/ppermute | solution.py:275
  31.1 0.9 %collective-permute-done.8 = f32[4,17,128]{2,0,1:T(4,128)S(1)} collective-permute-done((f32[4,17,128]{2,0,1:T(4,128)S(1)}, f32[4,17,128]{2,0,1:T(4,128)S(1)}, u32[]{:S(2)}, u32[]{:S(2)}) %collective-permute-start.8) | collective-permute-done | bytes 34848 | tf_op jit(solution)/shard_map/ppermute | solution.py:275
  32.0 2.0 %collective-permute-start.9 = (f32[2,17,128]{2,0,1:T(2,128)S(1)}, f32[2,17,128]{2,0,1:T(2,128)S(1)}, u32[]{:S(2)}, u32[]{:S(2)}) collective-permute-start(f32[2,17,128]{2,0,1:T(2,128)S(1)} %bitcast.28), channel_id=1, source_target_pairs={{0,2},{1,3},{2,0},{3,1},{4,6},{5,7},{6,4},{7,5},{8,10},{9,11},{10,... | collective-permute-start | bytes 52232 | tf_op jit(solution)/shard_map/ppermute | solution.py:275
  34.0 1.8 %collective-permute-done.9 = f32[2,17,128]{2,0,1:T(2,128)S(1)} collective-permute-done((f32[2,17,128]{2,0,1:T(2,128)S(1)}, f32[2,17,128]{2,0,1:T(2,128)S(1)}, u32[]{:S(2)}, u32[]{:S(2)}) %collective-permute-start.9) | collective-permute-done | bytes 17440 | tf_op jit(solution)/shard_map/ppermute | solution.py:275
  35.8 3.0 %collective-permute-start.10 = (f32[1,17,128]{2,0,1:T(1,128)S(1)}, f32[1,17,128]{2,0,1:T(1,128)S(1)}, u32[]{:S(2)}, u32[]{:S(2)}) collective-permute-start(f32[1,17,128]{2,0,1:T(1,128)S(1)} %constant_dynamic-slice_fusion), channel_id=1, source_target_pairs={{0,4},{1,5},{2,6},{3,7},{4,0},{5,1},{6,2},{7,3},{8,12},{9,13},{10,... | collective-permute-start | bytes 26120 | tf_op jit(solution)/shard_map/ppermute | solution.py:275
  38.9 1.6 %collective-permute-done.10 = f32[1,17,128]{2,0,1:T(1,128)S(1)} collective-permute-done((f32[1,17,128]{2,0,1:T(1,128)S(1)}, f32[1,17,128]{2,0,1:T(1,128)S(1)}, u32[]{:S(2)}, u32[]{:S(2)}) %collective-permute-start.10) | collective-permute-done | bytes 8736 | tf_op jit(solution)/shard_map/ppermute | solution.py:275
  40.6 0.7 %broadcast_divide_fusion = f32[16,128]{1,0:T(8,128)} fusion(f32[16,128]{1,0:T(8,128)S(1)} %bitcast.27, f32[16]{0:T(128)S(1)} %fusion.13), kind=kLoop, calls=%fused_computation.29 | loop fusion | flops 2048 | bytes 16448 | tf_op jit(solution)/shard_map/div | solution.py:334
  (34 shorter events, 1.3 us)
Async XLA Ops:
  1.6 9.3 %collective-permute-start.2 = (f32[22,8,256]{2,1,0:T(8,128)S(1)}, f32[22,8,256]{2,1,0:T(8,128)S(1)}, u32[]{:S(2)}, u32[]{:S(2)}) collective-permute-start(f32[22,8,256]{2,1,0:T(8,128)S(1)} %constant_dynamic-slice_fusion.8), channel_id=1, source_target_pairs={{0,24},{8,16},{16,8},{24,0},{1,25},{9,17},{17,9},{25,1},{2,26},{10... | collective-permute-start | bytes 540680 | tf_op jit(solution)/shard_map/ppermute | solution.py:221
  5.6 9.7 %copy-start = (f32[64,16,256]{2,1,0:T(8,128)S(1)}, f32[64,16,256]{2,1,0:T(8,128)}, u32[]{:S(2)}) copy-start(f32[64,16,256]{2,1,0:T(8,128)} %refs_12_.1) | copy-start | bytes 3145732
  7.0 8.3 %collective-permute-start.1 = (f32[22,8,256]{2,1,0:T(8,128)S(1)}, f32[22,8,256]{2,1,0:T(8,128)S(1)}, u32[]{:S(2)}, u32[]{:S(2)}) collective-permute-start(f32[22,8,256]{2,1,0:T(8,128)S(1)} %get-tuple-element.27), channel_id=1, source_target_pairs={{0,8},{8,0},{16,24},{24,16},{1,9},{9,1},{17,25},{25,17},{2,10},{10... | collective-permute-start | bytes 540680 | tf_op jit(solution)/shard_map/ppermute | solution.py:221
  7.6 7.7 %collective-permute-start = (f32[22,8,256]{2,1,0:T(8,128)S(1)}, f32[22,8,256]{2,1,0:T(8,128)S(1)}, u32[]{:S(2)}, u32[]{:S(2)}) collective-permute-start(f32[22,8,256]{2,1,0:T(8,128)S(1)} %get-tuple-element.28), channel_id=1, source_target_pairs={{0,16},{8,24},{16,0},{24,8},{1,17},{9,25},{17,1},{25,9},{2,18},{10... | collective-permute-start | bytes 540680 | tf_op jit(solution)/shard_map/ppermute | solution.py:221
  7.6 0.7 %copy-start.4 = (s32[2048,1]{0,1:T(1,128)S(1)}, s32[2048,1]{0,1:T(1,128)}, u32[]{:S(2)}) copy-start(s32[2048,1]{0,1:T(1,128)} %param.6) | copy-start | bytes 24580
  8.3 0.7 %copy-start.1 = (s32[2048]{0:T(1024)S(1)}, s32[2048]{0:T(1024)}, u32[]{:S(2)}) copy-start(s32[2048]{0:T(1024)} %param.7) | copy-start | bytes 24580
  9.4 0.7 %copy-start.2 = (s32[2048]{0:T(1024)S(1)}, s32[2048]{0:T(1024)}, u32[]{:S(2)}) copy-start(s32[2048]{0:T(1024)} %param.9) | copy-start | bytes 24580
  9.4 0.7 %copy-start.3 = (s32[2048]{0:T(1024)S(1)}, s32[2048]{0:T(1024)}, u32[]{:S(2)}) copy-start(s32[2048]{0:T(1024)} %param.8) | copy-start | bytes 24580
  10.9 10.9 %collective-permute-start.5 = (f32[22,8,256]{2,1,0:T(8,128)S(1)}, f32[22,8,256]{2,1,0:T(8,128)S(1)}, u32[]{:S(2)}, u32[]{:S(2)}) collective-permute-start(f32[22,8,256]{2,1,0:T(8,128)S(1)} %get-tuple-element.16), channel_id=1, source_target_pairs={{0,24},{8,16},{16,8},{24,0},{1,25},{9,17},{17,9},{25,1},{2,26},{10... | collective-permute-start | bytes 540680 | tf_op jit(solution)/shard_map/ppermute | solution.py:221
  13.9 8.0 %collective-permute-start.6 = (f32[22,8,256]{2,1,0:T(8,128)S(1)}, f32[22,8,256]{2,1,0:T(8,128)S(1)}, u32[]{:S(2)}, u32[]{:S(2)}) collective-permute-start(f32[22,8,256]{2,1,0:T(8,128)S(1)} %get-tuple-element.17), channel_id=1, source_target_pairs={{0,8},{8,0},{16,24},{24,16},{1,9},{9,1},{17,25},{25,17},{2,10},{10... | collective-permute-start | bytes 540680 | tf_op jit(solution)/shard_map/ppermute | solution.py:221
  15.7 6.7 %collective-permute-start.7 = (f32[22,8,256]{2,1,0:T(8,128)S(1)}, f32[22,8,256]{2,1,0:T(8,128)S(1)}, u32[]{:S(2)}, u32[]{:S(2)}) collective-permute-start(f32[22,8,256]{2,1,0:T(8,128)S(1)} %get-tuple-element.18), channel_id=1, source_target_pairs={{0,16},{8,24},{16,0},{24,8},{1,17},{9,25},{17,1},{25,9},{2,18},{10... | collective-permute-start | bytes 540680 | tf_op jit(solution)/shard_map/ppermute | solution.py:221
  17.3 3.8 %collective-permute-start.4 = (f32[22,3,256]{2,1,0:T(4,128)S(1)}, f32[22,3,256]{2,1,0:T(4,128)S(1)}, u32[]{:S(2)}, u32[]{:S(2)}) collective-permute-start(f32[22,3,256]{2,1,0:T(4,128)S(1)} %get-tuple-element.29), channel_id=1, source_target_pairs={{1,2},{2,1},{3,4},{4,3},{5,6},{6,5},{9,10},{10,9},{11,12},{12,11},... | collective-permute-start | bytes 202760 | tf_op jit(solution)/shard_map/ppermute | solution.py:260
  17.9 3.9 %collective-permute-start.3 = (f32[22,3,256]{2,1,0:T(4,128)S(1)}, f32[22,3,256]{2,1,0:T(4,128)S(1)}, u32[]{:S(2)}, u32[]{:S(2)}) collective-permute-start(f32[22,3,256]{2,1,0:T(4,128)S(1)} %get-tuple-element.30), channel_id=1, source_target_pairs={{0,1},{1,0},{2,3},{3,2},{4,5},{5,4},{6,7},{7,6},{8,9},{9,8},{10,11... | collective-permute-start | bytes 202760 | tf_op jit(solution)/shard_map/ppermute | solution.py:261
  30.3 1.7 %collective-permute-start.8 = (f32[4,17,128]{2,0,1:T(4,128)S(1)}, f32[4,17,128]{2,0,1:T(4,128)S(1)}, u32[]{:S(2)}, u32[]{:S(2)}) collective-permute-start(f32[4,17,128]{2,0,1:T(4,128)S(1)} %bitcast.25), channel_id=1, source_target_pairs={{0,1},{1,0},{2,3},{3,2},{4,5},{5,4},{6,7},{7,6},{8,9},{9,8},{10,11... | collective-permute-start | bytes 104456 | tf_op jit(solution)/shard_map/ppermute | solution.py:275
  32.0 3.8 %collective-permute-start.9 = (f32[2,17,128]{2,0,1:T(2,128)S(1)}, f32[2,17,128]{2,0,1:T(2,128)S(1)}, u32[]{:S(2)}, u32[]{:S(2)}) collective-permute-start(f32[2,17,128]{2,0,1:T(2,128)S(1)} %bitcast.28), channel_id=1, source_target_pairs={{0,2},{1,3},{2,0},{3,1},{4,6},{5,7},{6,4},{7,5},{8,10},{9,11},{10,... | collective-permute-start | bytes 52232 | tf_op jit(solution)/shard_map/ppermute | solution.py:275
  35.8 4.7 %collective-permute-start.10 = (f32[1,17,128]{2,0,1:T(1,128)S(1)}, f32[1,17,128]{2,0,1:T(1,128)S(1)}, u32[]{:S(2)}, u32[]{:S(2)}) collective-permute-start(f32[1,17,128]{2,0,1:T(1,128)S(1)} %constant_dynamic-slice_fusion), channel_id=1, source_target_pairs={{0,4},{1,5},{2,6},{3,7},{4,0},{5,1},{6,2},{7,3},{8,12},{9,13},{10,... | collective-permute-start | bytes 26120 | tf_op jit(solution)/shard_map/ppermute | solution.py:275

commit v5 on v4

--- a/solution.py
+++ b/solution.py
@@ -10,9 +10,8 @@
 RIM = 3
 LEAD = 8
 LANES = 128
-TIES = (0, 0, 0)
+TIES = (0, 0, 2)
 WHICH = 2
-TILE_M = 1024
 BLOCK = 256
 
 
@@ -32,7 +31,7 @@
 ):
     pieces = refs[:len(layout)]
     places_hbm, attr_hbm, partial_ref = refs[len(layout):len(layout) + 3]
-    amp, exy, ett, box, fields, rows_bf, attr, places, windows, sems = refs[len(layout) + 3:]
+    amp, exy, ett, box, fields, rows_bf, attr, places, windows, early, sems = refs[len(layout) + 3:]
     halves = nt // LANES
     brick, slab, bricks, slabs = where_ref[0], where_ref[1], where_ref[2], where_ref[3]
     wide = cy + 8
@@ -100,7 +99,8 @@
             ett[e, h] = slope_t * slope_t * mask
         return carry
 
-    lax.fori_loop(0, cx + 4, energy_row, 0, unroll=True)
+    for e in range(cx // 2 + 4):
+        energy_row(e, 0)
 
     def across(slot, h, radius, row):
         box[slot, h] = row
@@ -133,7 +133,7 @@
             powers = inline3([row * row for row in rows])
             xys, ts = inline5(exy, r, h), inline5(ett, r, h)
             for j in range(4):
-                at = pl.ds(pl.multiple_of((r + j) * cy, 16), cy)
+                at = pl.ds((r + j) * cy, cy)
                 keep(0, at, h, across(4 * j + 0, h, 2, xys[j]))
                 keep(1, at, h, across(4 * j + 1, h, 2, ts[j]))
                 stack = across(4 * j + 2, h, 1, stacks[j])
@@ -142,13 +142,12 @@
                 keep(3, at, h, power)
         return carry
 
-    lax.fori_loop(0, cx // 4, sum_rows, 0, unroll=True)
-
     band5, band9 = band5_ref[...], band9_ref[...]
-    tile = TILE_M
-
-    def finish_tile(j, carry):
-        at = pl.ds(pl.multiple_of(j * tile, tile), tile)
+    half = cx * cy // 2
+    lane_block = lax.broadcasted_iota(jnp.int32, (BLOCK, LANES), 1)
+
+    def finish_half(j):
+        at = pl.ds(j * half, half)
         sums = [dot(fields[f, 0, at, :], b) + dot(fields[f, 1, at, :], b)
                 for f, b in enumerate((band5, band5, band9, band9))]
         both = (sums[3] + 1e-5) * (sums[0] + sums[1] + 4e-5)
@@ -159,33 +158,39 @@
         high, low = split_bf16(values)
         rows_bf[at, 0:nt] = high
         rows_bf[at, nt:2 * nt] = low
-        return carry
-
-    lax.fori_loop(0, cx * cy // tile, finish_tile, 0)
-    store = pltpu.make_async_copy(attr, attr_hbm, sems.at[base + 1])
-    store.start()
-
-    fetch_places.wait()
-    block = BLOCK
-    lane_block = lax.broadcasted_iota(jnp.int32, (block, LANES), 1)
-
-    def window_block(j, carry):
-        at = pl.ds(pl.multiple_of(j * block, block), block)
+
+    def picked(n, j):
+        at = pl.ds(n * BLOCK, BLOCK)
         place = places[at, :]
         trace = lax.shift_right_logical(place, nt.bit_length() - 1)
         chosen = dot(jnp.concatenate([
             (lane_block + k == trace).astype(jnp.float32).astype(jnp.bfloat16)
-            for k in range(0, cx * cy, LANES)], axis=1), rows_bf[...])
-        rows = chosen[:, 0:nt] + chosen[:, nt:2 * nt]
-        shift = place - trace * nt
+            for k in range(j * half, (j + 1) * half, LANES)], axis=1), rows_bf[pl.ds(j * half, half), :])
+        return at, place - trace * nt, chosen[:, 0:nt] + chosen[:, nt:2 * nt]
+
+    blocks, quads = patches // BLOCK, cx // 4
+    for q in range(quads // 2):
+        sum_rows(q, 0)
+    finish_half(0)
+    for e in range(cx // 2 + 4, cx + 4):
+        energy_row(e, 0)
+    fetch_places.wait()
+    for q in range(quads // 2, quads):
+        sum_rows(q, 0)
+        for n in range(blocks * (q - quads // 2) * 2 // quads, blocks * (q - quads // 2 + 1) * 2 // quads):
+            at, _, rows = picked(n, 0)
+            early[at, :] = rows
+    finish_half(1)
+    store = pltpu.make_async_copy(attr, attr_hbm, sems.at[base + 1])
+    store.start()
+    for n in range(blocks):
+        at, shift, rows = picked(n, 1)
+        rows = rows + early[at, :]
         mixed = jnp.where(lane_block < shift, rows[:, LANES:nt], rows[:, 0:LANES])
         window = jnp.take_along_axis(mixed, (lane_block + shift) & (LANES - 1), axis=1)
         high, low = split_bf16(window)
         windows[at, 0:PATCH] = high
         windows[at, PATCH:2 * PATCH] = low
-        return carry
-
-    lax.fori_loop(0, patches // block, window_block, 0, unroll=True)
     sums = dot(faults_ref[...], windows[...])
     partial_ref[...] = sums[:, 0:PATCH] + sums[:, PATCH:2 * PATCH]
     store.wait()
@@ -321,6 +326,7 @@
             pltpu.VMEM((cx * cy, nt), jnp.float32),
             pltpu.VMEM((patches, LANES), jnp.int32),
             pltpu.VMEM((patches, 2 * PATCH), jnp.bfloat16),
+            pltpu.VMEM((patches, nt), jnp.float32),
             pltpu.SemaphoreType.DMA((len(layout) * halves + 2,)),
         ],
         compiler_params=pltpu.CompilerParams(vmem_limit_bytes=48 * 1024 * 1024),

time: 41.6 us -> 41.4 us (level)
  no operation moved by 1% of the time
where the time goes in v5:
time: 41.4 us; the launch traced here: 41 us
  starting transfers between devices  19.2 us (46%)
  Pallas kernels  7.63 us (18%)
  waiting for transfers between devices  7.35 us (18%)
  local copies, waits for them, and re-layouts  4.75 us (11%)
  other arithmetic  1.32 us (3%)
  between operations  0.82 us (2%)
    ppermute x6, starting transfers between devices, send(): return lax.ppermute(piece, 'brick', [(s, s ^ d) for s in range(bricks)])  9.65 us
    pallas_call x1, Pallas kernels, local(): pl.pallas_call(kernel, out_shape=(jax.ShapeDtypeStruct((cx * cy, nt), jnp...  7.63 us
    ppermute x3, starting transfers between devices, reduce_scatter(): lax.ppermute(sent, axis, [(s, s ^ bit) for s in range(count)])  5.85 us
    ppermute x3, waiting for transfers between devices, reduce_scatter(): lax.ppermute(sent, axis, [(s, s ^ bit) for s in range(count)])  4.29 us
    ppermute x1, starting transfers between devices, halo_columns(): near = lax.ppermute(near, 'bulk', inner)  3 us
    dynamic_slice x2, local copies, waits for them, and re-layouts, cut(): return lax.dynamic_slice(source, (first, begin, 0), (rows, columns, nt))  2.33 us
    ppermute x6, waiting for transfers between devices, send(): return lax.ppermute(piece, 'brick', [(s, s ^ d) for s in range(bricks)])  2.2 us
    unnamed x11, local copies, waits for them, and re-layouts  1.95 us
  transfers between devices with their start and end apart: 11, of which 8 were waited for; matrix products, arithmetic and copies ran while one was open for 6% of the time, Pallas kernels for 0%

profile of v5, /device:TPU:0, one launch (start us, length us, event | category | flops | bytes accessed | tf_op | source)
XLA Modules:
  0.0 41.0 jit_solution(9052820965157523074)
XLA Ops:
  0.6 0.9 %constant_dynamic-slice_fusion.8 = f32[22,8,256]{2,1,0:T(8,128)S(1)} fusion(f32[64,16,256]{2,1,0:T(8,128)} %refs_12_.1, s32[]{:T(128)S(6)} %min.17, s32[]{:T(128)S(6)} %mul.38), kind=kLoop, calls=%fused_computation.39 | loop fusion | bytes 360456 | tf_op jit(solution)/shard_map/dynamic_slice | solution.py:223
  1.6 4.0 %collective-permute-start.2 = (f32[22,8,256]{2,1,0:T(8,128)S(1)}, f32[22,8,256]{2,1,0:T(8,128)S(1)}, u32[]{:S(2)}, u32[]{:S(2)}) collective-permute-start(f32[22,8,256]{2,1,0:T(8,128)S(1)} %constant_dynamic-slice_fusion.8), channel_id=1, source_target_pairs={{0,24},{8,16},{16,8},{24,0},{1,25},{9,17},{17,9},{25,1},{2,26},{10... | collective-permute-start | bytes 540680 | tf_op jit(solution)/shard_map/ppermute | solution.py:226
  5.6 1.4 %constant_dynamic-slice_fusion.3 = (f32[22,8,256]{2,1,0:T(8,128)S(1)}, f32[22,8,256]{2,1,0:T(8,128)S(1)}, f32[22,8,256]{2,1,0:T(8,128)S(1)}, f32[22,8,256]{2,1,0:T(8,128)S(1)}, f32[22,8,256]{2,1,0:T(8,128)S(1)}) fusion(f32[64,16,256]{2,1,0:T(8,128)} %refs_12_.1, s32[]{:T(128)S(6)} %min.18, s32[]{:T(128)S(6)} %select_n.143, s32[]{:T(128)S(6)} %min.19, ...), kind=kLoop, calls=%fused_computation.34 | loop fusion | bytes 1802260 | tf_op jit(solution)/shard_map/dynamic_slice | solution.py:223
  7.0 0.6 %collective-permute-start.1 = (f32[22,8,256]{2,1,0:T(8,128)S(1)}, f32[22,8,256]{2,1,0:T(8,128)S(1)}, u32[]{:S(2)}, u32[]{:S(2)}) collective-permute-start(f32[22,8,256]{2,1,0:T(8,128)S(1)} %get-tuple-element.27), channel_id=1, source_target_pairs={{0,8},{8,0},{16,24},{24,16},{1,9},{9,1},{17,25},{25,17},{2,10},{10... | collective-permute-start | bytes 540680 | tf_op jit(solution)/shard_map/ppermute | solution.py:226
  7.7 0.6 %copy-done.4 = s32[2048,1]{0,1:T(1,128)S(1)} copy-done((s32[2048,1]{0,1:T(1,128)S(1)}, s32[2048,1]{0,1:T(1,128)}, u32[]{:S(2)}) %copy-start.4) | copy-done | bytes 8216
  8.3 0.7 %copy-done.1 = s32[2048]{0:T(1024)S(1)} copy-done((s32[2048]{0:T(1024)S(1)}, s32[2048]{0:T(1024)}, u32[]{:S(2)}) %copy-start.1) | copy-done | bytes 8216
  9.5 0.6 %copy-done.2 = s32[2048]{0:T(1024)S(1)} copy-done((s32[2048]{0:T(1024)S(1)}, s32[2048]{0:T(1024)}, u32[]{:S(2)}) %copy-start.2) | copy-done | bytes 8216
  10.1 0.9 %collective-permute-done.2.refs_6_ = f32[22,8,256]{2,1,0:T(8,128)S(1)} collective-permute-done((f32[22,8,256]{2,1,0:T(8,128)S(1)}, f32[22,8,256]{2,1,0:T(8,128)S(1)}, u32[]{:S(2)}, u32[]{:S(2)}) %collective-permute-start.2) | collective-permute-done | bytes 180256 | tf_op jit(solution)/shard_map/ppermute | solution.py:226
  10.9 3.0 %collective-permute-start.5 = (f32[22,8,256]{2,1,0:T(8,128)S(1)}, f32[22,8,256]{2,1,0:T(8,128)S(1)}, u32[]{:S(2)}, u32[]{:S(2)}) collective-permute-start(f32[22,8,256]{2,1,0:T(8,128)S(1)} %get-tuple-element.16), channel_id=1, source_target_pairs={{0,24},{8,16},{16,8},{24,0},{1,25},{9,17},{17,9},{25,1},{2,26},{10... | collective-permute-start | bytes 540680 | tf_op jit(solution)/shard_map/ppermute | solution.py:226
  13.9 0.5 %collective-permute-start.6 = (f32[22,8,256]{2,1,0:T(8,128)S(1)}, f32[22,8,256]{2,1,0:T(8,128)S(1)}, u32[]{:S(2)}, u32[]{:S(2)}) collective-permute-start(f32[22,8,256]{2,1,0:T(8,128)S(1)} %get-tuple-element.17), channel_id=1, source_target_pairs={{0,8},{8,0},{16,24},{24,16},{1,9},{9,1},{17,25},{25,17},{2,10},{10... | collective-permute-start | bytes 540680 | tf_op jit(solution)/shard_map/ppermute | solution.py:226
  14.4 0.8 %collective-permute-done.1.refs_7_ = f32[22,8,256]{2,1,0:T(8,128)S(1)} collective-permute-done((f32[22,8,256]{2,1,0:T(8,128)S(1)}, f32[22,8,256]{2,1,0:T(8,128)S(1)}, u32[]{:S(2)}, u32[]{:S(2)}) %collective-permute-start.1) | collective-permute-done | bytes 180256 | tf_op jit(solution)/shard_map/ppermute | solution.py:226
  15.7 1.5 %collective-permute-start.7 = (f32[22,8,256]{2,1,0:T(8,128)S(1)}, f32[22,8,256]{2,1,0:T(8,128)S(1)}, u32[]{:S(2)}, u32[]{:S(2)}) collective-permute-start(f32[22,8,256]{2,1,0:T(8,128)S(1)} %get-tuple-element.18), channel_id=1, source_target_pairs={{0,16},{8,24},{16,0},{24,8},{1,17},{9,25},{17,1},{25,9},{2,18},{10... | collective-permute-start | bytes 540680 | tf_op jit(solution)/shard_map/ppermute | solution.py:226
  17.3 0.7 %collective-permute-start.4 = (f32[22,3,256]{2,1,0:T(4,128)S(1)}, f32[22,3,256]{2,1,0:T(4,128)S(1)}, u32[]{:S(2)}, u32[]{:S(2)}) collective-permute-start(f32[22,3,256]{2,1,0:T(4,128)S(1)} %get-tuple-element.29), channel_id=1, source_target_pairs={{1,2},{2,1},{3,4},{4,3},{5,6},{6,5},{9,10},{10,9},{11,12},{12,11},... | collective-permute-start | bytes 202760 | tf_op jit(solution)/shard_map/ppermute | solution.py:265
  17.9 3.0 %collective-permute-start.3 = (f32[22,3,256]{2,1,0:T(4,128)S(1)}, f32[22,3,256]{2,1,0:T(4,128)S(1)}, u32[]{:S(2)}, u32[]{:S(2)}) collective-permute-start(f32[22,3,256]{2,1,0:T(4,128)S(1)} %get-tuple-element.30), channel_id=1, source_target_pairs={{0,1},{1,0},{2,3},{3,2},{4,5},{5,4},{6,7},{7,6},{8,9},{9,8},{10,11... | collective-permute-start | bytes 202760 | tf_op jit(solution)/shard_map/ppermute | solution.py:266
  21.0 0.9 %collective-permute-done.3.refs_1_ = f32[22,3,256]{2,1,0:T(4,128)S(1)} collective-permute-done((f32[22,3,256]{2,1,0:T(4,128)S(1)}, f32[22,3,256]{2,1,0:T(4,128)S(1)}, u32[]{:S(2)}, u32[]{:S(2)}) %collective-permute-start.3) | collective-permute-done | bytes 67616 | tf_op jit(solution)/shard_map/ppermute | solution.py:266
  21.9 0.4 %collective-permute-done.7.refs_11_ = f32[22,8,256]{2,1,0:T(8,128)S(1)} collective-permute-done((f32[22,8,256]{2,1,0:T(8,128)S(1)}, f32[22,8,256]{2,1,0:T(8,128)S(1)}, u32[]{:S(2)}, u32[]{:S(2)}) %collective-permute-start.7) | collective-permute-done | bytes 180256 | tf_op jit(solution)/shard_map/ppermute | solution.py:226
  22.4 7.6 %brick_attribute.1 = (f32[1024,256]{1,0:T(8,128)}, f32[128,128]{1,0:T(8,128)S(1)}) custom-call(s32[4]{0:T(128)S(1)} %pad_add_fusion.refs_0_, f32[22,3,256]{2,1,0:T(4,128)S(1)} %collective-permute-done.3.refs_1_, f32[22,3,256]{2,1,0:T(4,128)S(1)} %collective-permute-done.4.refs_2_, bf16[256,256]{1,0:T(8,128)(2,1)S(1)} %get-tuple-element.35.refs_3_, ...), custom_call_target="tpu_custom_call" | custom-call | flops 2500000000 | bytes 10000000 | tf_op jit(solution)/shard_map/brick_attribute/pallas_call | solution.py:311
  30.1 0.8 %collective-permute-start.8 = (f32[4,17,128]{2,0,1:T(4,128)S(1)}, f32[4,17,128]{2,0,1:T(4,128)S(1)}, u32[]{:S(2)}, u32[]{:S(2)}) collective-permute-start(f32[4,17,128]{2,0,1:T(4,128)S(1)} %bitcast.25), channel_id=1, source_target_pairs={{0,1},{1,0},{2,3},{3,2},{4,5},{5,4},{6,7},{7,6},{8,9},{9,8},{10,11... | collective-permute-start | bytes 104456 | tf_op jit(solution)/shard_map/ppermute | solution.py:280
  30.9 0.9 %collective-permute-done.8 = f32[4,17,128]{2,0,1:T(4,128)S(1)} collective-permute-done((f32[4,17,128]{2,0,1:T(4,128)S(1)}, f32[4,17,128]{2,0,1:T(4,128)S(1)}, u32[]{:S(2)}, u32[]{:S(2)}) %collective-permute-start.8) | collective-permute-done | bytes 34848 | tf_op jit(solution)/shard_map/ppermute | solution.py:280
  31.8 2.0 %collective-permute-start.9 = (f32[2,17,128]{2,0,1:T(2,128)S(1)}, f32[2,17,128]{2,0,1:T(2,128)S(1)}, u32[]{:S(2)}, u32[]{:S(2)}) collective-permute-start(f32[2,17,128]{2,0,1:T(2,128)S(1)} %bitcast.28), channel_id=1, source_target_pairs={{0,2},{1,3},{2,0},{3,1},{4,6},{5,7},{6,4},{7,5},{8,10},{9,11},{10,... | collective-permute-start | bytes 52232 | tf_op jit(solution)/shard_map/ppermute | solution.py:280
  33.8 1.8 %collective-permute-done.9 = f32[2,17,128]{2,0,1:T(2,128)S(1)} collective-permute-done((f32[2,17,128]{2,0,1:T(2,128)S(1)}, f32[2,17,128]{2,0,1:T(2,128)S(1)}, u32[]{:S(2)}, u32[]{:S(2)}) %collective-permute-start.9) | collective-permute-done | bytes 17440 | tf_op jit(solution)/shard_map/ppermute | solution.py:280
  35.6 3.0 %collective-permute-start.10 = (f32[1,17,128]{2,0,1:T(1,128)S(1)}, f32[1,17,128]{2,0,1:T(1,128)S(1)}, u32[]{:S(2)}, u32[]{:S(2)}) collective-permute-start(f32[1,17,128]{2,0,1:T(1,128)S(1)} %constant_dynamic-slice_fusion), channel_id=1, source_target_pairs={{0,4},{1,5},{2,6},{3,7},{4,0},{5,1},{6,2},{7,3},{8,12},{9,13},{10,... | collective-permute-start | bytes 26120 | tf_op jit(solution)/shard_map/ppermute | solution.py:280
  38.7 1.6 %collective-permute-done.10 = f32[1,17,128]{2,0,1:T(1,128)S(1)} collective-permute-done((f32[1,17,128]{2,0,1:T(1,128)S(1)}, f32[1,17,128]{2,0,1:T(1,128)S(1)}, u32[]{:S(2)}, u32[]{:S(2)}) %collective-permute-start.10) | collective-permute-done | bytes 8736 | tf_op jit(solution)/shard_map/ppermute | solution.py:280
  40.4 0.7 %broadcast_divide_fusion = f32[16,128]{1,0:T(8,128)} fusion(f32[16,128]{1,0:T(8,128)S(1)} %bitcast.27, f32[16]{0:T(128)S(1)} %fusion.13), kind=kLoop, calls=%fused_computation.29 | loop fusion | flops 2048 | bytes 16448 | tf_op jit(solution)/shard_map/div | solution.py:340
  (34 shorter events, 1.3 us)
Async XLA Ops:
  1.6 9.3 %collective-permute-start.2 = (f32[22,8,256]{2,1,0:T(8,128)S(1)}, f32[22,8,256]{2,1,0:T(8,128)S(1)}, u32[]{:S(2)}, u32[]{:S(2)}) collective-permute-start(f32[22,8,256]{2,1,0:T(8,128)S(1)} %constant_dynamic-slice_fusion.8), channel_id=1, source_target_pairs={{0,24},{8,16},{16,8},{24,0},{1,25},{9,17},{17,9},{25,1},{2,26},{10... | collective-permute-start | bytes 540680 | tf_op jit(solution)/shard_map/ppermute | solution.py:226
  5.6 9.7 %copy-start = (f32[64,16,256]{2,1,0:T(8,128)S(1)}, f32[64,16,256]{2,1,0:T(8,128)}, u32[]{:S(2)}) copy-start(f32[64,16,256]{2,1,0:T(8,128)} %refs_12_.1) | copy-start | bytes 3145732
  7.0 8.3 %collective-permute-start.1 = (f32[22,8,256]{2,1,0:T(8,128)S(1)}, f32[22,8,256]{2,1,0:T(8,128)S(1)}, u32[]{:S(2)}, u32[]{:S(2)}) collective-permute-start(f32[22,8,256]{2,1,0:T(8,128)S(1)} %get-tuple-element.27), channel_id=1, source_target_pairs={{0,8},{8,0},{16,24},{24,16},{1,9},{9,1},{17,25},{25,17},{2,10},{10... | collective-permute-start | bytes 540680 | tf_op jit(solution)/shard_map/ppermute | solution.py:226
  7.6 7.7 %collective-permute-start = (f32[22,8,256]{2,1,0:T(8,128)S(1)}, f32[22,8,256]{2,1,0:T(8,128)S(1)}, u32[]{:S(2)}, u32[]{:S(2)}) collective-permute-start(f32[22,8,256]{2,1,0:T(8,128)S(1)} %get-tuple-element.28), channel_id=1, source_target_pairs={{0,16},{8,24},{16,0},{24,8},{1,17},{9,25},{17,1},{25,9},{2,18},{10... | collective-permute-start | bytes 540680 | tf_op jit(solution)/shard_map/ppermute | solution.py:226
  7.6 0.7 %copy-start.4 = (s32[2048,1]{0,1:T(1,128)S(1)}, s32[2048,1]{0,1:T(1,128)}, u32[]{:S(2)}) copy-start(s32[2048,1]{0,1:T(1,128)} %param.6) | copy-start | bytes 24580
  8.3 0.7 %copy-start.1 = (s32[2048]{0:T(1024)S(1)}, s32[2048]{0:T(1024)}, u32[]{:S(2)}) copy-start(s32[2048]{0:T(1024)} %param.7) | copy-start | bytes 24580
  9.4 0.7 %copy-start.2 = (s32[2048]{0:T(1024)S(1)}, s32[2048]{0:T(1024)}, u32[]{:S(2)}) copy-start(s32[2048]{0:T(1024)} %param.9) | copy-start | bytes 24580
  9.4 0.7 %copy-start.3 = (s32[2048]{0:T(1024)S(1)}, s32[2048]{0:T(1024)}, u32[]{:S(2)}) copy-start(s32[2048]{0:T(1024)} %param.8) | copy-start | bytes 24580
  10.9 10.9 %collective-permute-start.5 = (f32[22,8,256]{2,1,0:T(8,128)S(1)}, f32[22,8,256]{2,1,0:T(8,128)S(1)}, u32[]{:S(2)}, u32[]{:S(2)}) collective-permute-start(f32[22,8,256]{2,1,0:T(8,128)S(1)} %get-tuple-element.16), channel_id=1, source_target_pairs={{0,24},{8,16},{16,8},{24,0},{1,25},{9,17},{17,9},{25,1},{2,26},{10... | collective-permute-start | bytes 540680 | tf_op jit(solution)/shard_map/ppermute | solution.py:226
  13.9 8.0 %collective-permute-start.6 = (f32[22,8,256]{2,1,0:T(8,128)S(1)}, f32[22,8,256]{2,1,0:T(8,128)S(1)}, u32[]{:S(2)}, u32[]{:S(2)}) collective-permute-start(f32[22,8,256]{2,1,0:T(8,128)S(1)} %get-tuple-element.17), channel_id=1, source_target_pairs={{0,8},{8,0},{16,24},{24,16},{1,9},{9,1},{17,25},{25,17},{2,10},{10... | collective-permute-start | bytes 540680 | tf_op jit(solution)/shard_map/ppermute | solution.py:226
  15.7 6.7 %collective-permute-start.7 = (f32[22,8,256]{2,1,0:T(8,128)S(1)}, f32[22,8,256]{2,1,0:T(8,128)S(1)}, u32[]{:S(2)}, u32[]{:S(2)}) collective-permute-start(f32[22,8,256]{2,1,0:T(8,128)S(1)} %get-tuple-element.18), channel_id=1, source_target_pairs={{0,16},{8,24},{16,0},{24,8},{1,17},{9,25},{17,1},{25,9},{2,18},{10... | collective-permute-start | bytes 540680 | tf_op jit(solution)/shard_map/ppermute | solution.py:226
  17.3 3.8 %collective-permute-start.4 = (f32[22,3,256]{2,1,0:T(4,128)S(1)}, f32[22,3,256]{2,1,0:T(4,128)S(1)}, u32[]{:S(2)}, u32[]{:S(2)}) collective-permute-start(f32[22,3,256]{2,1,0:T(4,128)S(1)} %get-tuple-element.29), channel_id=1, source_target_pairs={{1,2},{2,1},{3,4},{4,3},{5,6},{6,5},{9,10},{10,9},{11,12},{12,11},... | collective-permute-start | bytes 202760 | tf_op jit(solution)/shard_map/ppermute | solution.py:265
  17.9 3.9 %collective-permute-start.3 = (f32[22,3,256]{2,1,0:T(4,128)S(1)}, f32[22,3,256]{2,1,0:T(4,128)S(1)}, u32[]{:S(2)}, u32[]{:S(2)}) collective-permute-start(f32[22,3,256]{2,1,0:T(4,128)S(1)} %get-tuple-element.30), channel_id=1, source_target_pairs={{0,1},{1,0},{2,3},{3,2},{4,5},{5,4},{6,7},{7,6},{8,9},{9,8},{10,11... | collective-permute-start | bytes 202760 | tf_op jit(solution)/shard_map/ppermute | solution.py:266
  30.1 1.7 %collective-permute-start.8 = (f32[4,17,128]{2,0,1:T(4,128)S(1)}, f32[4,17,128]{2,0,1:T(4,128)S(1)}, u32[]{:S(2)}, u32[]{:S(2)}) collective-permute-start(f32[4,17,128]{2,0,1:T(4,128)S(1)} %bitcast.25), channel_id=1, source_target_pairs={{0,1},{1,0},{2,3},{3,2},{4,5},{5,4},{6,7},{7,6},{8,9},{9,8},{10,11... | collective-permute-start | bytes 104456 | tf_op jit(solution)/shard_map/ppermute | solution.py:280
  31.8 3.8 %collective-permute-start.9 = (f32[2,17,128]{2,0,1:T(2,128)S(1)}, f32[2,17,128]{2,0,1:T(2,128)S(1)}, u32[]{:S(2)}, u32[]{:S(2)}) collective-permute-start(f32[2,17,128]{2,0,1:T(2,128)S(1)} %bitcast.28), channel_id=1, source_target_pairs={{0,2},{1,3},{2,0},{3,1},{4,6},{5,7},{6,4},{7,5},{8,10},{9,11},{10,... | collective-permute-start | bytes 52232 | tf_op jit(solution)/shard_map/ppermute | solution.py:280
  35.6 4.7 %collective-permute-start.10 = (f32[1,17,128]{2,0,1:T(1,128)S(1)}, f32[1,17,128]{2,0,1:T(1,128)S(1)}, u32[]{:S(2)}, u32[]{:S(2)}) collective-permute-start(f32[1,17,128]{2,0,1:T(1,128)S(1)} %constant_dynamic-slice_fusion), channel_id=1, source_target_pairs={{0,4},{1,5},{2,6},{3,7},{4,0},{5,1},{6,2},{7,3},{8,12},{9,13},{10,... | collective-permute-start | bytes 26120 | tf_op jit(solution)/shard_map/ppermute | solution.py:280

commit v6 on v5

--- a/solution.py
+++ b/solution.py
@@ -95,8 +95,13 @@
             before = jnp.where(first, back[h - 1] if h > 0 else 0.0, back[h])
             after = jnp.where(last, ahead[h + 1] if h < halves - 1 else 0.0, ahead[h])
             slope_t = after - before
-            exy[e, h] = (slope_x * slope_x + slope_y * slope_y) * mask
-            ett[e, h] = slope_t * slope_t * mask
+            across_xy = slope_x * slope_x + slope_y * slope_y
+            along_t = slope_t * slope_t
+            for field, values in ((exy, across_xy), (ett, along_t)):
+                inner = values[8:cy]
+                field[e, h, 0:8, :] = values[0:8] * mask[0:8]
+                field[e, h, 8:cy, :] = inner if 2 <= e < cx + 2 else inner * mask[8:cy]
+                field[e, h, cy:wide, :] = values[cy:wide] * mask[cy:wide]
         return carry
 
     for e in range(cx // 2 + 4):
@@ -329,7 +334,7 @@
             pltpu.VMEM((patches, nt), jnp.float32),
             pltpu.SemaphoreType.DMA((len(layout) * halves + 2,)),
         ],
-        compiler_params=pltpu.CompilerParams(vmem_limit_bytes=48 * 1024 * 1024),
+        compiler_params=pltpu.CompilerParams(vmem_limit_bytes=32 * 1024 * 1024),
         cost_estimate=pl.CostEstimate(flops=2_500_000_000, bytes_accessed=10_000_000, transcendentals=0),
         name="brick_attribute",
     )(where, low, high, band(nt, 2), band(nt, 4), members, *pieces, places)

time: 41.4 us -> 41.4 us (level)
  no operation moved by 1% of the time
where the time goes in v6:
time: 41.4 us; the launch traced here: 41 us
  starting transfers between devices  19.2 us (46%)
  Pallas kernels  7.59 us (18%)
  waiting for transfers between devices  7.34 us (18%)
  local copies, waits for them, and re-layouts  4.75 us (11%)
  other arithmetic  1.32 us (3%)
  between operations  0.82 us (2%)
    ppermute x6, starting transfers between devices, send(): return lax.ppermute(piece, 'brick', [(s, s ^ d) for s in range(bricks)])  9.65 us
    pallas_call x1, Pallas kernels, local(): pl.pallas_call(kernel, out_shape=(jax.ShapeDtypeStruct((cx * cy, nt), jnp...  7.59 us
    ppermute x3, starting transfers between devices, reduce_scatter(): lax.ppermute(sent, axis, [(s, s ^ bit) for s in range(count)])  5.86 us
    ppermute x3, waiting for transfers between devices, reduce_scatter(): lax.ppermute(sent, axis, [(s, s ^ bit) for s in range(count)])  4.29 us
    ppermute x1, starting transfers between devices, halo_columns(): near = lax.ppermute(near, 'bulk', inner)  3 us
    dynamic_slice x2, local copies, waits for them, and re-layouts, cut(): return lax.dynamic_slice(source, (first, begin, 0), (rows, columns, nt))  2.33 us
    ppermute x6, waiting for transfers between devices, send(): return lax.ppermute(piece, 'brick', [(s, s ^ d) for s in range(bricks)])  2.2 us
    unnamed x11, local copies, waits for them, and re-layouts  1.95 us
  transfers between devices with their start and end apart: 11, of which 8 were waited for; matrix products, arithmetic and copies ran while one was open for 6% of the time, Pallas kernels for 0%

profile of v6, /device:TPU:0, one launch (start us, length us, event | category | flops | bytes accessed | tf_op | source)
XLA Modules:
  0.0 41.0 jit_solution(7660835423273301429)
XLA Ops:
  0.6 0.9 %constant_dynamic-slice_fusion.8 = f32[22,8,256]{2,1,0:T(8,128)S(1)} fusion(f32[64,16,256]{2,1,0:T(8,128)} %refs_12_.1, s32[]{:T(128)S(6)} %min.17, s32[]{:T(128)S(6)} %mul.38), kind=kLoop, calls=%fused_computation.39 | loop fusion | bytes 360456 | tf_op jit(solution)/shard_map/dynamic_slice | solution.py:228
  1.6 4.0 %collective-permute-start.2 = (f32[22,8,256]{2,1,0:T(8,128)S(1)}, f32[22,8,256]{2,1,0:T(8,128)S(1)}, u32[]{:S(2)}, u32[]{:S(2)}) collective-permute-start(f32[22,8,256]{2,1,0:T(8,128)S(1)} %constant_dynamic-slice_fusion.8), channel_id=1, source_target_pairs={{0,24},{8,16},{16,8},{24,0},{1,25},{9,17},{17,9},{25,1},{2,26},{10... | collective-permute-start | bytes 540680 | tf_op jit(solution)/shard_map/ppermute | solution.py:231
  5.6 1.4 %constant_dynamic-slice_fusion.3 = (f32[22,8,256]{2,1,0:T(8,128)S(1)}, f32[22,8,256]{2,1,0:T(8,128)S(1)}, f32[22,8,256]{2,1,0:T(8,128)S(1)}, f32[22,8,256]{2,1,0:T(8,128)S(1)}, f32[22,8,256]{2,1,0:T(8,128)S(1)}) fusion(f32[64,16,256]{2,1,0:T(8,128)} %refs_12_.1, s32[]{:T(128)S(6)} %min.18, s32[]{:T(128)S(6)} %select_n.143, s32[]{:T(128)S(6)} %min.19, ...), kind=kLoop, calls=%fused_computation.34 | loop fusion | bytes 1802260 | tf_op jit(solution)/shard_map/dynamic_slice | solution.py:228
  7.0 0.6 %collective-permute-start.1 = (f32[22,8,256]{2,1,0:T(8,128)S(1)}, f32[22,8,256]{2,1,0:T(8,128)S(1)}, u32[]{:S(2)}, u32[]{:S(2)}) collective-permute-start(f32[22,8,256]{2,1,0:T(8,128)S(1)} %get-tuple-element.27), channel_id=1, source_target_pairs={{0,8},{8,0},{16,24},{24,16},{1,9},{9,1},{17,25},{25,17},{2,10},{10... | collective-permute-start | bytes 540680 | tf_op jit(solution)/shard_map/ppermute | solution.py:231
  7.7 0.6 %copy-done.4 = s32[2048,1]{0,1:T(1,128)S(1)} copy-done((s32[2048,1]{0,1:T(1,128)S(1)}, s32[2048,1]{0,1:T(1,128)}, u32[]{:S(2)}) %copy-start.4) | copy-done | bytes 8216
  8.3 0.7 %copy-done.1 = s32[2048]{0:T(1024)S(1)} copy-done((s32[2048]{0:T(1024)S(1)}, s32[2048]{0:T(1024)}, u32[]{:S(2)}) %copy-start.1) | copy-done | bytes 8216
  9.5 0.6 %copy-done.2 = s32[2048]{0:T(1024)S(1)} copy-done((s32[2048]{0:T(1024)S(1)}, s32[2048]{0:T(1024)}, u32[]{:S(2)}) %copy-start.2) | copy-done | bytes 8216
  10.1 0.9 %collective-permute-done.2.refs_6_ = f32[22,8,256]{2,1,0:T(8,128)S(1)} collective-permute-done((f32[22,8,256]{2,1,0:T(8,128)S(1)}, f32[22,8,256]{2,1,0:T(8,128)S(1)}, u32[]{:S(2)}, u32[]{:S(2)}) %collective-permute-start.2) | collective-permute-done | bytes 180256 | tf_op jit(solution)/shard_map/ppermute | solution.py:231
  10.9 3.0 %collective-permute-start.5 = (f32[22,8,256]{2,1,0:T(8,128)S(1)}, f32[22,8,256]{2,1,0:T(8,128)S(1)}, u32[]{:S(2)}, u32[]{:S(2)}) collective-permute-start(f32[22,8,256]{2,1,0:T(8,128)S(1)} %get-tuple-element.16), channel_id=1, source_target_pairs={{0,24},{8,16},{16,8},{24,0},{1,25},{9,17},{17,9},{25,1},{2,26},{10... | collective-permute-start | bytes 540680 | tf_op jit(solution)/shard_map/ppermute | solution.py:231
  13.9 0.5 %collective-permute-start.6 = (f32[22,8,256]{2,1,0:T(8,128)S(1)}, f32[22,8,256]{2,1,0:T(8,128)S(1)}, u32[]{:S(2)}, u32[]{:S(2)}) collective-permute-start(f32[22,8,256]{2,1,0:T(8,128)S(1)} %get-tuple-element.17), channel_id=1, source_target_pairs={{0,8},{8,0},{16,24},{24,16},{1,9},{9,1},{17,25},{25,17},{2,10},{10... | collective-permute-start | bytes 540680 | tf_op jit(solution)/shard_map/ppermute | solution.py:231
  14.4 0.8 %collective-permute-done.1.refs_7_ = f32[22,8,256]{2,1,0:T(8,128)S(1)} collective-permute-done((f32[22,8,256]{2,1,0:T(8,128)S(1)}, f32[22,8,256]{2,1,0:T(8,128)S(1)}, u32[]{:S(2)}, u32[]{:S(2)}) %collective-permute-start.1) | collective-permute-done | bytes 180256 | tf_op jit(solution)/shard_map/ppermute | solution.py:231
  15.7 1.5 %collective-permute-start.7 = (f32[22,8,256]{2,1,0:T(8,128)S(1)}, f32[22,8,256]{2,1,0:T(8,128)S(1)}, u32[]{:S(2)}, u32[]{:S(2)}) collective-permute-start(f32[22,8,256]{2,1,0:T(8,128)S(1)} %get-tuple-element.18), channel_id=1, source_target_pairs={{0,16},{8,24},{16,0},{24,8},{1,17},{9,25},{17,1},{25,9},{2,18},{10... | collective-permute-start | bytes 540680 | tf_op jit(solution)/shard_map/ppermute | solution.py:231
  17.3 0.7 %collective-permute-start.4 = (f32[22,3,256]{2,1,0:T(4,128)S(1)}, f32[22,3,256]{2,1,0:T(4,128)S(1)}, u32[]{:S(2)}, u32[]{:S(2)}) collective-permute-start(f32[22,3,256]{2,1,0:T(4,128)S(1)} %get-tuple-element.29), channel_id=1, source_target_pairs={{1,2},{2,1},{3,4},{4,3},{5,6},{6,5},{9,10},{10,9},{11,12},{12,11},... | collective-permute-start | bytes 202760 | tf_op jit(solution)/shard_map/ppermute | solution.py:270
  17.9 3.0 %collective-permute-start.3 = (f32[22,3,256]{2,1,0:T(4,128)S(1)}, f32[22,3,256]{2,1,0:T(4,128)S(1)}, u32[]{:S(2)}, u32[]{:S(2)}) collective-permute-start(f32[22,3,256]{2,1,0:T(4,128)S(1)} %get-tuple-element.30), channel_id=1, source_target_pairs={{0,1},{1,0},{2,3},{3,2},{4,5},{5,4},{6,7},{7,6},{8,9},{9,8},{10,11... | collective-permute-start | bytes 202760 | tf_op jit(solution)/shard_map/ppermute | solution.py:271
  21.0 0.9 %collective-permute-done.3.refs_1_ = f32[22,3,256]{2,1,0:T(4,128)S(1)} collective-permute-done((f32[22,3,256]{2,1,0:T(4,128)S(1)}, f32[22,3,256]{2,1,0:T(4,128)S(1)}, u32[]{:S(2)}, u32[]{:S(2)}) %collective-permute-start.3) | collective-permute-done | bytes 67616 | tf_op jit(solution)/shard_map/ppermute | solution.py:271
  21.9 0.4 %collective-permute-done.7.refs_11_ = f32[22,8,256]{2,1,0:T(8,128)S(1)} collective-permute-done((f32[22,8,256]{2,1,0:T(8,128)S(1)}, f32[22,8,256]{2,1,0:T(8,128)S(1)}, u32[]{:S(2)}, u32[]{:S(2)}) %collective-permute-start.7) | collective-permute-done | bytes 180256 | tf_op jit(solution)/shard_map/ppermute | solution.py:231
  22.4 7.6 %brick_attribute.1 = (f32[1024,256]{1,0:T(8,128)}, f32[128,128]{1,0:T(8,128)S(1)}) custom-call(s32[4]{0:T(128)S(1)} %pad_add_fusion.refs_0_, f32[22,3,256]{2,1,0:T(4,128)S(1)} %collective-permute-done.3.refs_1_, f32[22,3,256]{2,1,0:T(4,128)S(1)} %collective-permute-done.4.refs_2_, bf16[256,256]{1,0:T(8,128)(2,1)S(1)} %get-tuple-element.35.refs_3_, ...), custom_call_target="tpu_custom_call" | custom-call | flops 2500000000 | bytes 10000000 | tf_op jit(solution)/shard_map/brick_attribute/pallas_call | solution.py:316
  30.0 0.8 %collective-permute-start.8 = (f32[4,17,128]{2,0,1:T(4,128)S(1)}, f32[4,17,128]{2,0,1:T(4,128)S(1)}, u32[]{:S(2)}, u32[]{:S(2)}) collective-permute-start(f32[4,17,128]{2,0,1:T(4,128)S(1)} %bitcast.25), channel_id=1, source_target_pairs={{0,1},{1,0},{2,3},{3,2},{4,5},{5,4},{6,7},{7,6},{8,9},{9,8},{10,11... | collective-permute-start | bytes 104456 | tf_op jit(solution)/shard_map/ppermute | solution.py:285
  30.8 0.9 %collective-permute-done.8 = f32[4,17,128]{2,0,1:T(4,128)S(1)} collective-permute-done((f32[4,17,128]{2,0,1:T(4,128)S(1)}, f32[4,17,128]{2,0,1:T(4,128)S(1)}, u32[]{:S(2)}, u32[]{:S(2)}) %collective-permute-start.8) | collective-permute-done | bytes 34848 | tf_op jit(solution)/shard_map/ppermute | solution.py:285
  31.7 2.0 %collective-permute-start.9 = (f32[2,17,128]{2,0,1:T(2,128)S(1)}, f32[2,17,128]{2,0,1:T(2,128)S(1)}, u32[]{:S(2)}, u32[]{:S(2)}) collective-permute-start(f32[2,17,128]{2,0,1:T(2,128)S(1)} %bitcast.28), channel_id=1, source_target_pairs={{0,2},{1,3},{2,0},{3,1},{4,6},{5,7},{6,4},{7,5},{8,10},{9,11},{10,... | collective-permute-start | bytes 52232 | tf_op jit(solution)/shard_map/ppermute | solution.py:285
  33.8 1.8 %collective-permute-done.9 = f32[2,17,128]{2,0,1:T(2,128)S(1)} collective-permute-done((f32[2,17,128]{2,0,1:T(2,128)S(1)}, f32[2,17,128]{2,0,1:T(2,128)S(1)}, u32[]{:S(2)}, u32[]{:S(2)}) %collective-permute-start.9) | collective-permute-done | bytes 17440 | tf_op jit(solution)/shard_map/ppermute | solution.py:285
  35.6 3.0 %collective-permute-start.10 = (f32[1,17,128]{2,0,1:T(1,128)S(1)}, f32[1,17,128]{2,0,1:T(1,128)S(1)}, u32[]{:S(2)}, u32[]{:S(2)}) collective-permute-start(f32[1,17,128]{2,0,1:T(1,128)S(1)} %constant_dynamic-slice_fusion), channel_id=1, source_target_pairs={{0,4},{1,5},{2,6},{3,7},{4,0},{5,1},{6,2},{7,3},{8,12},{9,13},{10,... | collective-permute-start | bytes 26120 | tf_op jit(solution)/shard_map/ppermute | solution.py:285
  38.6 1.6 %collective-permute-done.10 = f32[1,17,128]{2,0,1:T(1,128)S(1)} collective-permute-done((f32[1,17,128]{2,0,1:T(1,128)S(1)}, f32[1,17,128]{2,0,1:T(1,128)S(1)}, u32[]{:S(2)}, u32[]{:S(2)}) %collective-permute-start.10) | collective-permute-done | bytes 8736 | tf_op jit(solution)/shard_map/ppermute | solution.py:285
  40.3 0.7 %broadcast_divide_fusion = f32[16,128]{1,0:T(8,128)} fusion(f32[16,128]{1,0:T(8,128)S(1)} %bitcast.27, f32[16]{0:T(128)S(1)} %fusion.13), kind=kLoop, calls=%fused_computation.29 | loop fusion | flops 2048 | bytes 16448 | tf_op jit(solution)/shard_map/div | solution.py:345
  (34 shorter events, 1.3 us)
Async XLA Ops:
  1.6 9.3 %collective-permute-start.2 = (f32[22,8,256]{2,1,0:T(8,128)S(1)}, f32[22,8,256]{2,1,0:T(8,128)S(1)}, u32[]{:S(2)}, u32[]{:S(2)}) collective-permute-start(f32[22,8,256]{2,1,0:T(8,128)S(1)} %constant_dynamic-slice_fusion.8), channel_id=1, source_target_pairs={{0,24},{8,16},{16,8},{24,0},{1,25},{9,17},{17,9},{25,1},{2,26},{10... | collective-permute-start | bytes 540680 | tf_op jit(solution)/shard_map/ppermute | solution.py:231
  5.6 9.7 %copy-start = (f32[64,16,256]{2,1,0:T(8,128)S(1)}, f32[64,16,256]{2,1,0:T(8,128)}, u32[]{:S(2)}) copy-start(f32[64,16,256]{2,1,0:T(8,128)} %refs_12_.1) | copy-start | bytes 3145732
  7.0 8.3 %collective-permute-start.1 = (f32[22,8,256]{2,1,0:T(8,128)S(1)}, f32[22,8,256]{2,1,0:T(8,128)S(1)}, u32[]{:S(2)}, u32[]{:S(2)}) collective-permute-start(f32[22,8,256]{2,1,0:T(8,128)S(1)} %get-tuple-element.27), channel_id=1, source_target_pairs={{0,8},{8,0},{16,24},{24,16},{1,9},{9,1},{17,25},{25,17},{2,10},{10... | collective-permute-start | bytes 540680 | tf_op jit(solution)/shard_map/ppermute | solution.py:231
  7.6 7.7 %collective-permute-start = (f32[22,8,256]{2,1,0:T(8,128)S(1)}, f32[22,8,256]{2,1,0:T(8,128)S(1)}, u32[]{:S(2)}, u32[]{:S(2)}) collective-permute-start(f32[22,8,256]{2,1,0:T(8,128)S(1)} %get-tuple-element.28), channel_id=1, source_target_pairs={{0,16},{8,24},{16,0},{24,8},{1,17},{9,25},{17,1},{25,9},{2,18},{10... | collective-permute-start | bytes 540680 | tf_op jit(solution)/shard_map/ppermute | solution.py:231
  7.6 0.7 %copy-start.4 = (s32[2048,1]{0,1:T(1,128)S(1)}, s32[2048,1]{0,1:T(1,128)}, u32[]{:S(2)}) copy-start(s32[2048,1]{0,1:T(1,128)} %param.6) | copy-start | bytes 24580
  8.3 0.7 %copy-start.1 = (s32[2048]{0:T(1024)S(1)}, s32[2048]{0:T(1024)}, u32[]{:S(2)}) copy-start(s32[2048]{0:T(1024)} %param.7) | copy-start | bytes 24580
  9.4 0.7 %copy-start.2 = (s32[2048]{0:T(1024)S(1)}, s32[2048]{0:T(1024)}, u32[]{:S(2)}) copy-start(s32[2048]{0:T(1024)} %param.9) | copy-start | bytes 24580
  9.4 0.7 %copy-start.3 = (s32[2048]{0:T(1024)S(1)}, s32[2048]{0:T(1024)}, u32[]{:S(2)}) copy-start(s32[2048]{0:T(1024)} %param.8) | copy-start | bytes 24580
  10.9 10.9 %collective-permute-start.5 = (f32[22,8,256]{2,1,0:T(8,128)S(1)}, f32[22,8,256]{2,1,0:T(8,128)S(1)}, u32[]{:S(2)}, u32[]{:S(2)}) collective-permute-start(f32[22,8,256]{2,1,0:T(8,128)S(1)} %get-tuple-element.16), channel_id=1, source_target_pairs={{0,24},{8,16},{16,8},{24,0},{1,25},{9,17},{17,9},{25,1},{2,26},{10... | collective-permute-start | bytes 540680 | tf_op jit(solution)/shard_map/ppermute | solution.py:231
  13.9 8.0 %collective-permute-start.6 = (f32[22,8,256]{2,1,0:T(8,128)S(1)}, f32[22,8,256]{2,1,0:T(8,128)S(1)}, u32[]{:S(2)}, u32[]{:S(2)}) collective-permute-start(f32[22,8,256]{2,1,0:T(8,128)S(1)} %get-tuple-element.17), channel_id=1, source_target_pairs={{0,8},{8,0},{16,24},{24,16},{1,9},{9,1},{17,25},{25,17},{2,10},{10... | collective-permute-start | bytes 540680 | tf_op jit(solution)/shard_map/ppermute | solution.py:231
  15.7 6.7 %collective-permute-start.7 = (f32[22,8,256]{2,1,0:T(8,128)S(1)}, f32[22,8,256]{2,1,0:T(8,128)S(1)}, u32[]{:S(2)}, u32[]{:S(2)}) collective-permute-start(f32[22,8,256]{2,1,0:T(8,128)S(1)} %get-tuple-element.18), channel_id=1, source_target_pairs={{0,16},{8,24},{16,0},{24,8},{1,17},{9,25},{17,1},{25,9},{2,18},{10... | collective-permute-start | bytes 540680 | tf_op jit(solution)/shard_map/ppermute | solution.py:231
  17.3 3.8 %collective-permute-start.4 = (f32[22,3,256]{2,1,0:T(4,128)S(1)}, f32[22,3,256]{2,1,0:T(4,128)S(1)}, u32[]{:S(2)}, u32[]{:S(2)}) collective-permute-start(f32[22,3,256]{2,1,0:T(4,128)S(1)} %get-tuple-element.29), channel_id=1, source_target_pairs={{1,2},{2,1},{3,4},{4,3},{5,6},{6,5},{9,10},{10,9},{11,12},{12,11},... | collective-permute-start | bytes 202760 | tf_op jit(solution)/shard_map/ppermute | solution.py:270
  17.9 3.9 %collective-permute-start.3 = (f32[22,3,256]{2,1,0:T(4,128)S(1)}, f32[22,3,256]{2,1,0:T(4,128)S(1)}, u32[]{:S(2)}, u32[]{:S(2)}) collective-permute-start(f32[22,3,256]{2,1,0:T(4,128)S(1)} %get-tuple-element.30), channel_id=1, source_target_pairs={{0,1},{1,0},{2,3},{3,2},{4,5},{5,4},{6,7},{7,6},{8,9},{9,8},{10,11... | collective-permute-start | bytes 202760 | tf_op jit(solution)/shard_map/ppermute | solution.py:271
  30.0 1.7 %collective-permute-start.8 = (f32[4,17,128]{2,0,1:T(4,128)S(1)}, f32[4,17,128]{2,0,1:T(4,128)S(1)}, u32[]{:S(2)}, u32[]{:S(2)}) collective-permute-start(f32[4,17,128]{2,0,1:T(4,128)S(1)} %bitcast.25), channel_id=1, source_target_pairs={{0,1},{1,0},{2,3},{3,2},{4,5},{5,4},{6,7},{7,6},{8,9},{9,8},{10,11... | collective-permute-start | bytes 104456 | tf_op jit(solution)/shard_map/ppermute | solution.py:285
  31.7 3.8 %collective-permute-start.9 = (f32[2,17,128]{2,0,1:T(2,128)S(1)}, f32[2,17,128]{2,0,1:T(2,128)S(1)}, u32[]{:S(2)}, u32[]{:S(2)}) collective-permute-start(f32[2,17,128]{2,0,1:T(2,128)S(1)} %bitcast.28), channel_id=1, source_target_pairs={{0,2},{1,3},{2,0},{3,1},{4,6},{5,7},{6,4},{7,5},{8,10},{9,11},{10,... | collective-permute-start | bytes 52232 | tf_op jit(solution)/shard_map/ppermute | solution.py:285
  35.6 4.7 %collective-permute-start.10 = (f32[1,17,128]{2,0,1:T(1,128)S(1)}, f32[1,17,128]{2,0,1:T(1,128)S(1)}, u32[]{:S(2)}, u32[]{:S(2)}) collective-permute-start(f32[1,17,128]{2,0,1:T(1,128)S(1)} %constant_dynamic-slice_fusion), channel_id=1, source_target_pairs={{0,4},{1,5},{2,6},{3,7},{4,0},{5,1},{6,2},{7,3},{8,12},{9,13},{10,... | collective-permute-start | bytes 26120 | tf_op jit(solution)/shard_map/ppermute | solution.py:285
